TPU v7x, 32 devices: a whole 2x2x4 slice. The times are simulated.
32 devices in a mesh: depth: 2 (over core), tile: 16 (over z, y, x).
Axes of the slice: x: 2, y: 2, z: 4, core: 2. Of those that a mesh axis runs over, the one named last changes fastest.
Arguments:
- transmission: float32 [2, 4, 1024, 2048], P(None, 'depth', 'tile'), may hold values from -1 to 1, as said below
- probe: float32 [2, 128, 128], replicated, may hold values from -4 to 4
- scan_rows: int32 [128], P('tile'), may hold values from 0 to 896, as said below
- scan_cols: int32 [128], P('tile'), may hold values from 0 to 1920
- tile_counts: int32 [16], replicated, may hold values from 1 to 8, as said below
- diffraction: float32 [128, 128, 128], P('tile'), may hold values from 0 to 2
Outputs:
- object_grad: float32 [2, 4, 1024, 2048], P(None, 'depth', 'tile')
- probe_grad: float32 [2, 128, 128], P(None, 'depth')
Inputs may be any that keep to these rules, and one draw needn't show every extreme that they name: `scan_rows`: slot i's row lies within [t * 64 - 128/2, t * 64 + 64 - 128/2) for t = i // 8, clipped to the specimen; both ends of the specimen are reached. `tile_counts`: some strip has all 8 slots filled and some strip only one. `transmission`: every entry has magnitude between 0.8 and 1.
All inputs are finite; a program needn't handle non-finite values.
Results may differ from a plain program's by a relative error of at most 0.0003.
Values sent between devices are 32-bit elements; how exact they have to be, the bound alone decides.
A program may use at most 320 MiB of HBM per device.

v0:
```python
import math

import jax
import jax.numpy as jnp
from jax import lax
from jax.sharding import PartitionSpec as P

FRESNEL = 0.5
HIGH = lax.Precision.HIGHEST


def with_halo(value, sides, width):
    for axis, dim in sides:
        size, length = (lax.axis_size(axis), value.shape[dim])
        up = [(i, (i + 1) % size) for i in range(size - 1)]
        down = [(j, i) for i, j in up]
        last = lax.slice_in_dim(value, length - width, length, axis=dim)
        first = lax.slice_in_dim(value, 0, width, axis=dim)
        before = lax.ppermute(last, axis, up)
        after = lax.ppermute(first, axis, down)
        value = jnp.concatenate([before, value, after], axis=dim)
    return value


def shifted(value, axis, by):
    size = lax.axis_size(axis)
    pairs = [(i, i + by) for i in range(size) if 0 <= i + by < size]
    return lax.ppermute(value, axis, pairs)


def dft_tables(size):
    index = jnp.arange(size, dtype=jnp.int32)
    product = index[:, None] * index[None, :] % size
    angle = 2.0 * math.pi / size * product.astype(jnp.float32)
    scale = 1.0 / math.sqrt(size)
    cosine = jnp.cos(angle) * scale
    sine = jnp.sin(angle) * scale
    freq = ((index + size // 2) % size - size // 2).astype(jnp.float32)
    phase = FRESNEL * math.pi / size * (freq[:, None] ** 2 + freq[None, :] ** 2)
    return (cosine, sine, jnp.cos(phase), jnp.sin(phase))


def left_mul(real_m, imag_m, wave):
    wave_re = wave[..., 0, :, :]
    wave_im = wave[..., 1, :, :]

    def prod(m, x):
        return jnp.einsum("ij,...jk->...ik", m, x, precision=HIGH)

    return jnp.stack(
        [
            prod(real_m, wave_re) - prod(imag_m, wave_im),
            prod(real_m, wave_im) + prod(imag_m, wave_re),
        ],
        axis=-3,
    )


def right_mul(wave, real_m, imag_m):
    wave_re = wave[..., 0, :, :]
    wave_im = wave[..., 1, :, :]

    def prod(x, m):
        return jnp.einsum("...ij,jk->...ik", x, m, precision=HIGH)

    return jnp.stack(
        [
            prod(wave_re, real_m) - prod(wave_im, imag_m),
            prod(wave_re, imag_m) + prod(wave_im, real_m),
        ],
        axis=-3,
    )


def transform(wave, cosine, sine, sign):
    imag_m = sign * sine
    return right_mul(left_mul(cosine, imag_m, wave), cosine, imag_m)


def times(first, second):
    a_re, a_im = (first[..., 0, :, :], first[..., 1, :, :])
    b_re, b_im = (second[..., 0, :, :], second[..., 1, :, :])
    return jnp.stack([a_re * b_re - a_im * b_im, a_re * b_im + a_im * b_re], axis=-3)


def conj_times(first, second):
    a_re, a_im = (first[..., 0, :, :], first[..., 1, :, :])
    b_re, b_im = (second[..., 0, :, :], second[..., 1, :, :])
    return jnp.stack([a_re * b_re + a_im * b_im, a_re * b_im - a_im * b_re], axis=-3)


def propagate(wave, tables, adjoint):
    cosine, sine, kern_cos, kern_sin = tables
    spectrum = transform(wave, cosine, sine, -1.0)
    kernel = jnp.stack([kern_cos, kern_sin if adjoint else -kern_sin])
    return transform(times(kernel, spectrum), cosine, sine, 1.0)


def shards(transmission, probe, scan_rows, scan_cols, tile_counts, diffraction):
    size = probe.shape[-1]
    half = size // 2
    group = transmission.shape[1]
    strip = transmission.shape[2]
    slots = scan_rows.shape[0]
    tables = dft_tables(size)
    cosine, sine = (tables[0], tables[1])
    n_depth = lax.axis_size("depth")
    depth_pos = lax.axis_index("depth")
    tile_pos = lax.axis_index("tile")
    first = depth_pos == 0
    last = depth_pos == n_depth - 1
    filled = tile_counts[tile_pos]
    extended = with_halo(transmission, (("tile", 2),), half)
    local_rows = scan_rows - (tile_pos * strip - half)
    batch = 1
    offsets = jnp.arange(batch, dtype=jnp.int32)
    zero_index = jnp.int32(0)

    def cut(row, col):
        return lax.dynamic_slice(
            extended, (zero_index, zero_index, row, col), (2, group, size, size)
        )

    own_bank = jax.vmap(cut)(local_rows, scan_cols)

    def walk(wave, patches, finish):
        inputs = []
        for slice_pos in range(group):
            inputs.append(wave)
            if finish or slice_pos + 1 < group:
                wave = propagate(times(patches[:, :, slice_pos], wave), tables, False)
        return (wave, jnp.stack(inputs, axis=1))

    def seed_of(out_wave, measured):
        far = transform(out_wave, cosine, sine, -1.0)
        intensity = far[:, 0] ** 2 + far[:, 1] ** 2
        return transform((intensity - measured)[:, None] * far, cosine, sine, 1.0)

    grads_start = jnp.zeros(extended.shape, jnp.float32)
    order = jnp.arange(slots, dtype=jnp.int32)
    n_blocks = slots // batch
    count = order.shape[0]
    blocks = count // batch
    segments = n_blocks + n_depth - 1
    wave_shape = (batch, 2, size, size)

    def slot_state(block):
        positions = block * batch + offsets
        valid = (block >= 0) & (block < n_blocks) & (positions < filled)
        start = jnp.clip(block, 0, blocks - 1) * batch
        ids = order[start + offsets]
        return (valid, start, ids)

    saved_start = jnp.zeros((count, 2, size, size), jnp.float32)
    seeds_start = jnp.zeros((count, 2, size, size), jnp.float32)

    def forward_segment(step, state):
        incoming, saved, seeds = state
        valid, start, ids = slot_state(step - depth_pos)
        mask = valid.astype(jnp.float32)[:, None, None, None]
        wave = jnp.where(first, probe[None], incoming) * mask

        def forward_work(args):
            saved_in, seeds_in = args
            out_wave, inputs = walk(wave, jnp.take(own_bank, ids, axis=0), True)
            kept = inputs[:, 0]
            saved_out = lax.dynamic_update_slice_in_dim(saved_in, kept, start, 0)

            def write_seed(buffer):
                measured = jnp.take(diffraction, ids, axis=0)
                return lax.dynamic_update_slice_in_dim(
                    buffer, seed_of(out_wave, measured), start, 0
                )

            def leave_seed(buffer):
                return buffer

            seeds_out = lax.cond(last, write_seed, leave_seed, seeds_in)
            return (out_wave, saved_out, seeds_out)

        def forward_rest(args):
            return (jnp.zeros(wave_shape, jnp.float32), args[0], args[1])

        out_wave, saved, seeds = lax.cond(
            jnp.any(valid), forward_work, forward_rest, (saved, seeds)
        )
        incoming = shifted(out_wave, "depth", 1)
        return (incoming, saved, seeds)

    incoming0 = jnp.zeros(wave_shape, jnp.float32)
    _, saved, seeds = lax.fori_loop(
        0, segments, forward_segment, (incoming0, saved_start, seeds_start)
    )

    def backward_segment(step, state):
        incoming, windows, probe_acc = state
        valid, start, ids = slot_state(step - (n_depth - 1 - depth_pos))
        mask = valid.astype(jnp.float32)[:, None, None, None]
        arriving = (
            jnp.where(last, lax.dynamic_slice_in_dim(seeds, start, batch, 0), incoming) * mask
        )

        def backward_work(args):
            windows_in, probe_in = args
            patches = jnp.take(own_bank, ids, axis=0)
            _, inputs = walk(lax.dynamic_slice_in_dim(saved, start, batch, 0), patches, False)
            flow = arriving
            pieces = [None] * group
            for slice_pos in reversed(range(group)):
                along = propagate(flow, tables, True)
                pieces[slice_pos] = conj_times(inputs[:, slice_pos], along)
                flow = conj_times(patches[:, :, slice_pos], along)
            update = (
                jnp.stack(pieces, axis=2) * valid.astype(jnp.float32)[:, None, None, None, None]
            )
            windows_out = lax.dynamic_update_slice_in_dim(windows_in, update, start, 0)
            probe_out = probe_in + jnp.where(first, jnp.sum(flow * mask, axis=0), 0.0)
            return (flow, windows_out, probe_out)

        def backward_rest(args):
            return (jnp.zeros(wave_shape, jnp.float32), args[0], args[1])

        out_wave, windows, probe_acc = lax.cond(
            jnp.any(valid), backward_work, backward_rest, (windows, probe_acc)
        )
        incoming = shifted(out_wave, "depth", -1)
        return (incoming, windows, probe_acc)

    windows_start = jnp.zeros((count, 2, group, size, size), jnp.float32)
    probe_start = jnp.zeros(probe.shape, jnp.float32)
    _, windows, probe_acc = lax.fori_loop(
        0, segments, backward_segment, (incoming0, windows_start, probe_start)
    )
    windows, probe_acc = (windows, probe_acc)
    weights = jnp.ones((slots,), jnp.float32)

    def place_one(item, total):
        slot_id = order[item]
        place = (zero_index, zero_index, local_rows[slot_id], scan_cols[slot_id])
        current = lax.dynamic_slice(total, place, (2, group, size, size))
        return lax.dynamic_update_slice(total, current + windows[item] * weights[item], place)

    grads = lax.fori_loop(0, order.shape[0], place_one, grads_start)
    rims = jnp.concatenate([grads[:, :, :half], grads[:, :, half + strip :]], axis=2)
    arrived = with_halo(rims, (("tile", 2),), half)
    own = grads[:, :, half : half + strip]
    own = own.at[:, :, :half].add(arrived[:, :, :half])
    own = own.at[:, :, strip - half :].add(arrived[:, :, 3 * half :])
    probe_rows = lax.psum_scatter(probe_acc, "depth", scatter_dimension=1, tiled=True)
    probe_grad = lax.psum(probe_rows, "tile")
    return (own, probe_grad)


def solution(mesh):
    placed = (P(None, "depth", "tile", None), P(), P("tile"), P("tile"), P(), P("tile", None, None))
    return jax.shard_map(
        shards,
        mesh=mesh,
        in_specs=placed,
        out_specs=(P(None, "depth", "tile", None), P(None, "depth", None)),
        check_vma=False,
    )
```

profile of v0, /device:TPU:0, one launch (start us, length us, event | category | flops | bytes accessed | tf_op | source)
XLA Modules:
  0.0 847.0 jit_solution(9796558993692898980)
XLA Ops:
  7.2 5.0 collective-permute-start.2
  12.2 1.3 collective-permute-start.3
  16.1 86.1 %collective-permute-done.2 = f32[2,2,64,2048]{3,2,1,0:T(8,128)S(1)} collective-permute-done((f32[2,2,64,2048]{3,2,1,0:T(8,128)}, f32[2,2,64,2048]{3,2,1,0:T(8,128)S(1)}, u32[]{:S(2)}, u32[]{:S(2)}) %collective-permute-start.2) | collective-permute-done | bytes 2097184 | tf_op jit(solution)/shard_map/ppermute | solution.py:19
  102.2 1.9 collective-permute-done.3
  104.1 5.7 pad_maximum_fusion.2
  110.1 24.2 %while.68 = (s32[]{:T(128)}, f32[2,2,192,2048]{3,2,1,0:T(8,128)}, s32[8,4]{0,1:T(4,128)S(1)}, f32[8,2,2,128,128]{4,3,1,2,0:T(8,128)S(1)}, s32[]{:T(128)}) while((s32[]{:T(128)}, f32[2,2,192,2048]{3,2,1,0:T(8,128)}, s32[8,4]{0,1:T(4,128)S(1)}, f32[8,2,2,128,128]{4,3,1,2,0:T(8,128)S(1)}, s32[]{:T(128)}) %tuple.373), condition=%wide.while_cond.6, body=%wide.while_body.6.sunk | while | flops 2 | bytes 525937 | solution.py:120
  110.7 2.4 copy_dynamic-update-slice_fusion.2
  113.8 2.4 copy_dynamic-update-slice_fusion.2
  116.8 2.4 copy_dynamic-update-slice_fusion.2
  119.8 2.4 copy_dynamic-update-slice_fusion.2
  122.8 2.4 copy_dynamic-update-slice_fusion.2
  125.9 2.4 copy_dynamic-update-slice_fusion.2
  128.9 2.4 copy_dynamic-update-slice_fusion.2
  131.9 2.4 copy_dynamic-update-slice_fusion.2
  136.5 91.4 %while.69 = (s32[]{:T(128)}, f32[1,2,128,128]{3,2,1,0:T(8,128)S(1)}, f32[8,2,128,128]{3,2,1,0:T(8,128)}, f32[8,2,128,128]{3,2,1,0:T(8,128)}, s32[]{:T(128)}, /*i...) while((s32[]{:T(128)}, ...), condition=%wide.region_5.7_spmd.clone.clone.clone, body=%wide.region_0.6_spmd.clone.clone.clone.sunk | while | flops 1209614336 | bytes 16059241 | solution.py:191
  137.2 13.6 %conditional.12 = (f32[1,2,128,128]{3,2,1,0:T(8,128)S(1)}, f32[8,2,128,128]{3,2,1,0:T(8,128)}, f32[8,2,128,128]{3,2,1,0:T(8,128)}) conditional(s32[]{:T(128)} %bitcast.558, (f32[8,2,128,128]{3,2,1,0:T(8,128)}, f32[8,2,128,128]{3,2,1,0:T(8,128)}) %tuple.363, (s32[]{:T(128)}, s32[8]{0:T(128)S(1)}, f32[8,2,2,128,128]{4,3,1,2,0:T(8,128)S(1)}, ...), branch_computations={%region_1.1_spmd, %region_2.5_spmd.clone} | conditional | flops 1209352192 | bytes 15337401 | solution.py:184
  150.8 1.3 collective-permute-start
  153.7 13.6 %conditional.12 = (f32[1,2,128,128]{3,2,1,0:T(8,128)S(1)}, f32[8,2,128,128]{3,2,1,0:T(8,128)}, f32[8,2,128,128]{3,2,1,0:T(8,128)}) conditional(s32[]{:T(128)} %bitcast.558, (f32[8,2,128,128]{3,2,1,0:T(8,128)}, f32[8,2,128,128]{3,2,1,0:T(8,128)}) %tuple.363, (s32[]{:T(128)}, s32[8]{0:T(128)S(1)}, f32[8,2,2,128,128]{4,3,1,2,0:T(8,128)S(1)}, ...), branch_computations={%region_1.1_spmd, %region_2.5_spmd.clone} | conditional | flops 1209352192 | bytes 15337401 | solution.py:184
  167.3 10.3 %collective-permute-start = (f32[1,2,128,128]{3,2,1,0:T(8,128)S(1)}, f32[1,2,128,128]{3,2,1,0:T(8,128)S(1)}, u32[]{:S(2)}, u32[]{:S(2)}) collective-permute-start(f32[1,2,128,128]{3,2,1,0:T(8,128)S(1)} %get-tuple-element.2643), channel_id=1, source_target_pairs={{0,16},{1,17},{2,18},{3,19},{4,20},{5,21},{6,22},{7,23},{8,24},{9,... | collective-permute-start | bytes 393224 | tf_op jit(solution)/shard_map/while/body/eval_jaxpr/ppermute | solution.py:28
  179.3 23.9 %collective-permute-start = (f32[1,2,128,128]{3,2,1,0:T(8,128)S(1)}, f32[1,2,128,128]{3,2,1,0:T(8,128)S(1)}, u32[]{:S(2)}, u32[]{:S(2)}) collective-permute-start(f32[1,2,128,128]{3,2,1,0:T(8,128)S(1)} %get-tuple-element.2643), channel_id=1, source_target_pairs={{0,16},{1,17},{2,18},{3,19},{4,20},{5,21},{6,22},{7,23},{8,24},{9,... | collective-permute-start | bytes 393224 | tf_op jit(solution)/shard_map/while/body/eval_jaxpr/ppermute | solution.py:28
  204.8 2.3 collective-permute-start
  208.8 2.3 collective-permute-start
  212.8 2.3 collective-permute-start
  216.7 2.3 collective-permute-start
  220.7 2.3 collective-permute-start
  224.6 2.3 collective-permute-start
  227.9 1.6 broadcast_in_dim.97
  229.5 94.9 %while.70 = (s32[]{:T(128)}, f32[1,2,128,128]{3,2,1,0:T(8,128)S(1)}, f32[8,2,2,128,128]{4,3,1,2,0:T(8,128)}, f32[2,128,128]{2,1,0:T(8,128)S(1)}, s32[]{:T(128)},...) while((s32[]{:T(128)}, ...), condition=%wide.region_9.11_spmd.clone.clone.clone, body=%wide.region_6.10_spmd.clone.clone.clone.sunk | while | flops 1210138624 | bytes 17565816 | solution.py:231
  230.4 1.3 collective-permute-start.1
  231.7 21.1 %collective-permute-done.1 = f32[1,2,128,128]{3,2,1,0:T(8,128)S(1)} collective-permute-done((f32[1,2,128,128]{3,2,1,0:T(8,128)S(1)}, f32[1,2,128,128]{3,2,1,0:T(8,128)S(1)}, u32[]{:S(2)}, u32[]{:S(2)}) %collective-permute-start.1) | collective-permute-done | bytes 131104 | tf_op jit(solution)/shard_map/while/body/eval_jaxpr/ppermute | solution.py:28
  253.5 20.0 %conditional.13 = (f32[1,2,128,128]{3,2,1,0:T(8,128)S(1)}, f32[8,2,2,128,128]{4,3,1,2,0:T(8,128)}, f32[2,128,128]{2,1,0:T(8,128)S(1)}) conditional(s32[]{:T(128)} %bitcast.561, (f32[8,2,2,128,128]{4,3,1,2,0:T(8,128)}, f32[2,128,128]{2,1,0:T(8,128)S(1)}) %tuple.367, (s32[]{:T(128)}, s32[8]{0:T(128)S(1)}, f32[8,2,2,128,128]{4,3,1,2,0:T(8,128)S(1)}, ...), branch_computations={%region_7.8_spmd, %region_8.9_spmd.clone} | conditional | flops 1209876480 | bytes 16843968 | solution.py:223
  273.4 1.3 collective-permute-start.1
  274.7 1.9 collective-permute-done.1
  277.4 20.0 %conditional.13 = (f32[1,2,128,128]{3,2,1,0:T(8,128)S(1)}, f32[8,2,2,128,128]{4,3,1,2,0:T(8,128)}, f32[2,128,128]{2,1,0:T(8,128)S(1)}) conditional(s32[]{:T(128)} %bitcast.561, (f32[8,2,2,128,128]{4,3,1,2,0:T(8,128)}, f32[2,128,128]{2,1,0:T(8,128)S(1)}) %tuple.367, (s32[]{:T(128)}, s32[8]{0:T(128)S(1)}, f32[8,2,2,128,128]{4,3,1,2,0:T(8,128)S(1)}, ...), branch_computations={%region_7.8_spmd, %region_8.9_spmd.clone} | conditional | flops 1209876480 | bytes 16843968 | solution.py:223
  297.3 1.3 collective-permute-start.1
  298.6 1.9 collective-permute-done.1
  301.3 1.3 collective-permute-start.1
  302.6 1.9 collective-permute-done.1
  305.3 1.3 collective-permute-start.1
  306.6 1.9 collective-permute-done.1
  309.2 1.3 collective-permute-start.1
  310.5 1.9 collective-permute-done.1
  313.2 1.3 collective-permute-start.1
  314.5 1.9 collective-permute-done.1
  317.1 1.3 collective-permute-start.1
  318.4 1.9 collective-permute-done.1
  322.4 1.9 collective-permute-done.1
  324.3 3.4 broadcast_in_dim.96
  327.8 96.8 %while.67 = (s32[]{:T(128)}, f32[2,2,192,2048]{3,2,1,0:T(8,128)}, s32[8]{0:T(128)S(1)}, s32[8]{0:T(128)S(1)}, s32[8]{0:T(128)S(1)}, /*index=5*/f32[8,2,2,128,128...) while((s32[]{:T(128)}, f32[2,2,192,2048]{3,2,1,0:T(8,128)}, ...), condition=%wide.region_11.13_spmd, body=%wide.region_10.12_spmd.sunk | while | flops 65547 | bytes 1311491 | solution.py:243
  336.6 3.3 dynamic_update_slice.29
  348.7 3.2 dynamic_update_slice.29
  360.9 3.2 dynamic_update_slice.29
  372.9 3.2 dynamic_update_slice.29
  385.0 3.2 dynamic_update_slice.29
  397.1 3.3 dynamic_update_slice.29
  409.2 3.3 dynamic_update_slice.29
  421.3 3.2 dynamic_update_slice.29
  424.6 4.8 fusion.137
  429.4 93.6 %collective-permute-start.4 = (f32[2,2,64,2048]{3,2,1,0:T(8,128)}, f32[2,2,64,2048]{3,2,1,0:T(8,128)S(1)}, u32[]{:S(2)}, u32[]{:S(2)}) collective-permute-start(f32[2,2,64,2048]{3,2,1,0:T(8,128)} %get-tuple-element.2429), channel_id=1, source_target_pairs={{0,1},{1,2},{2,3},{3,4},{4,5},{5,6},{6,7},{7,8},{8,9},{9,10},{10,1... | collective-permute-start | bytes 6291464 | tf_op jit(solution)/shard_map/ppermute | solution.py:19
  522.9 1.3 collective-permute-start.5
  524.3 173.0 %reduce-scatter.2.cloned.1.call-done = f32[2,64,128]{2,1,0:T(8,128)} async-done(((f32[2,128,128]{2,1,0:T(8,128)}), f32[2,64,128]{2,1,0:T(8,128)}) %reduce-scatter.2.cloned.1.call-update) | async-done | bytes 65552 | tf_op jit(solution)/shard_map/reduce_scatter | solution.py:249
  697.3 4.2 add_add_fusion
  701.5 137.1 %all-reduce.2.cloned.1.call-done = f32[2,64,128]{2,1,0:T(8,128)} async-done(((f32[2,64,128]{2,1,0:T(8,128)}), f32[2,64,128]{2,1,0:T(8,128)}) %all-reduce.2.cloned.1.call-update) | async-done | bytes 65552 | tf_op jit(solution)/shard_map/psum | solution.py:250
  838.6 1.5 copy.83
  (368 shorter events, 106.9 us)
Async XLA Ops:
  7.2 690.1 %reduce-scatter.2.cloned.1.call-start = ((), (), s32[]{:S(2)}) async-start(), calls=%async_computation.1 | async-start | bytes 196608 | tf_op jit(solution)/shard_map/reduce_scatter | solution.py:249
  7.2 95.0 %collective-permute-start.2 = (f32[2,2,64,2048]{3,2,1,0:T(8,128)}, f32[2,2,64,2048]{3,2,1,0:T(8,128)S(1)}, u32[]{:S(2)}, u32[]{:S(2)}) collective-permute-start(f32[2,2,64,2048]{3,2,1,0:T(8,128)} %param.28), channel_id=1, source_target_pairs={{0,1},{1,2},{2,3},{3,4},{4,5},{5,6},{6,7},{7,8},{8,9},{9,10},{10,1... | collective-permute-start | bytes 6291464 | tf_op jit(solution)/shard_map/ppermute | solution.py:19
  12.2 91.9 %collective-permute-start.3 = (f32[2,2,64,2048]{3,2,1,0:T(8,128)}, f32[2,2,64,2048]{3,2,1,0:T(8,128)}, u32[]{:S(2)}, u32[]{:S(2)}) collective-permute-start(f32[2,2,64,2048]{3,2,1,0:T(8,128)} %param.28), channel_id=1, source_target_pairs={{1,0},{2,1},{3,2},{4,3},{5,4},{6,5},{7,6},{8,7},{9,8},{10,9},{11,1... | collective-permute-start | bytes 6291464 | tf_op jit(solution)/shard_map/ppermute | solution.py:20
  110.0 26.5 %copy-start.1 = (f32[2,128,128]{2,1,0:T(8,128)S(1)}, f32[2,128,128]{2,1,0:T(8,128)}, u32[]{:S(2)}) copy-start(f32[2,128,128]{2,1,0:T(8,128)} %param.29) | copy-start | bytes 393220
  150.8 2.3 collective-permute-start
  167.3 11.3 %collective-permute-start = (f32[1,2,128,128]{3,2,1,0:T(8,128)S(1)}, f32[1,2,128,128]{3,2,1,0:T(8,128)S(1)}, u32[]{:S(2)}, u32[]{:S(2)}) collective-permute-start(f32[1,2,128,128]{3,2,1,0:T(8,128)S(1)} %get-tuple-element.2643), channel_id=1, source_target_pairs={{0,16},{1,17},{2,18},{3,19},{4,20},{5,21},{6,22},{7,23},{8,24},{9,... | collective-permute-start | bytes 393224 | tf_op jit(solution)/shard_map/while/body/eval_jaxpr/ppermute | solution.py:28
  179.3 24.8 %collective-permute-start = (f32[1,2,128,128]{3,2,1,0:T(8,128)S(1)}, f32[1,2,128,128]{3,2,1,0:T(8,128)S(1)}, u32[]{:S(2)}, u32[]{:S(2)}) collective-permute-start(f32[1,2,128,128]{3,2,1,0:T(8,128)S(1)} %get-tuple-element.2643), channel_id=1, source_target_pairs={{0,16},{1,17},{2,18},{3,19},{4,20},{5,21},{6,22},{7,23},{8,24},{9,... | collective-permute-start | bytes 393224 | tf_op jit(solution)/shard_map/while/body/eval_jaxpr/ppermute | solution.py:28
  204.8 3.2 collective-permute-start
  208.8 3.2 collective-permute-start
  212.8 3.2 collective-permute-start
  216.7 3.2 collective-permute-start
  220.7 3.2 collective-permute-start
  224.6 3.2 collective-permute-start
  230.4 22.4 %collective-permute-start.1 = (f32[1,2,128,128]{3,2,1,0:T(8,128)S(1)}, f32[1,2,128,128]{3,2,1,0:T(8,128)S(1)}, u32[]{:S(2)}, u32[]{:S(2)}) collective-permute-start(f32[1,2,128,128]{3,2,1,0:T(8,128)S(1)} %get-tuple-element.2660), channel_id=1, source_target_pairs={{16,0},{17,1},{18,2},{19,3},{20,4},{21,5},{22,6},{23,7},{24,8},{25... | collective-permute-start | bytes 393224 | tf_op jit(solution)/shard_map/while/body/eval_jaxpr/ppermute | solution.py:28
  273.4 3.2 collective-permute-start.1
  297.3 3.2 collective-permute-start.1
  301.3 3.2 collective-permute-start.1
  305.3 3.2 collective-permute-start.1
  309.2 3.2 collective-permute-start.1
  313.2 3.2 collective-permute-start.1
  317.1 3.2 collective-permute-start.1
  321.1 3.2 collective-permute-start.1
  324.3 3.4 copy-start
  324.3 3.4 copy-start.2
  429.4 268.0 %collective-permute-start.4 = (f32[2,2,64,2048]{3,2,1,0:T(8,128)}, f32[2,2,64,2048]{3,2,1,0:T(8,128)S(1)}, u32[]{:S(2)}, u32[]{:S(2)}) collective-permute-start(f32[2,2,64,2048]{3,2,1,0:T(8,128)} %get-tuple-element.2429), channel_id=1, source_target_pairs={{0,1},{1,2},{2,3},{3,4},{4,5},{5,6},{6,7},{7,8},{8,9},{9,10},{10,1... | collective-permute-start | bytes 6291464 | tf_op jit(solution)/shard_map/ppermute | solution.py:19
  522.9 174.4 %collective-permute-start.5 = (f32[2,2,64,2048]{3,2,1,0:T(8,128)}, f32[2,2,64,2048]{3,2,1,0:T(8,128)}, u32[]{:S(2)}, u32[]{:S(2)}) collective-permute-start(f32[2,2,64,2048]{3,2,1,0:T(8,128)} %get-tuple-element.2430), channel_id=1, source_target_pairs={{1,0},{2,1},{3,2},{4,3},{5,4},{6,5},{7,6},{8,7},{9,8},{10,9},{11,1... | collective-permute-start | bytes 6291464 | tf_op jit(solution)/shard_map/ppermute | solution.py:20
  524.3 314.4 %all-reduce.2.cloned.1.call-start = ((), (), s32[]{:S(2)}) async-start(), calls=%async_computation.2 | async-start | bytes 131072 | tf_op jit(solution)/shard_map/psum | solution.py:250
Sparse Core Ops, SparseCore 0:
  524.4 172.8 reduce-scatter.1
  702.8 135.8 all-reduce.1
where the time goes:
time: 851 us; the launch traced here: 847 us
  waiting for transfers between devices  443 us (52%)
  starting transfers between devices  162 us (19%)
  local copies, waits for them, and re-layouts  84.7 us (10%)
  loops' own time  65.3 us (8%)
  matrix products  47.9 us (6%)
  other arithmetic  29.6 us (3%)
  between operations  14.2 us (2%)
    reduce_scatter x1, waiting for transfers between devices, shards(): lax.psum_scatter(probe_acc, 'depth', scatter_dimension=1, tiled=True)  173 us
    psum x1, waiting for transfers between devices, shards(): probe_grad = lax.psum(probe_rows, 'tile')  137 us
    ppermute x2, starting transfers between devices, with_halo(): before = lax.ppermute(last, axis, up)  98.5 us
    ppermute x2, waiting for transfers between devices, with_halo(): before = lax.ppermute(last, axis, up)  86.1 us
    ppermute x18, starting transfers between devices, shifted(): return lax.ppermute(value, axis, pairs)  60.8 us
    ppermute x18, waiting for transfers between devices, shifted(): return lax.ppermute(value, axis, pairs)  45.2 us
    another operation x1, loops' own time, shards(): grads = lax.fori_loop(0, order.shape[0], place_one, grads_start)  45.1 us
    dynamic_update_slice x8, local copies, waits for them, and re-layouts, place_one(): lax.dynamic_update_slice(total, current + windows[item] * weights[item],...  26 us
  transfers between devices with their start and end apart: 24, of which 22 were waited for; matrix products, arithmetic and copies ran while one was open for 1% of the time, Pallas kernels for 0%

commit v1 on v0

v1 whole, which is shorter than its diff:
```python
import math

import jax
import jax.numpy as jnp
import ml_dtypes
import numpy as np
from jax import lax
from jax.experimental import pallas as pl
from jax.experimental.pallas import tpu as pltpu
from jax.sharding import PartitionSpec as P

FRESNEL = 0.5
LANES = 128


def split_table(table):
    head = table.astype(np.float32).astype(ml_dtypes.bfloat16)
    tail = (table - head.astype(np.float64)).astype(np.float32).astype(ml_dtypes.bfloat16)
    return np.stack([head, tail])


def tables(size):
    index = np.arange(size)
    dft = np.exp(-2j * math.pi / size * (index[:, None] * index[None, :] % size)) / math.sqrt(size)
    freq = (index + size // 2) % size - size // 2
    phase = np.exp(-1j * FRESNEL * math.pi / size * freq.astype(np.float64) ** 2)
    prop = dft.conj() @ (phase[:, None] * dft)
    prop = 0.5 * (prop + prop.T)
    out = []
    for m in (prop, dft):
        right = np.block([[m.real, m.imag], [-m.imag, m.real]])
        out += [split_table(right), split_table(right.T)]
    return out


def halves(x):
    head = x.astype(jnp.bfloat16)
    tail = (x - head.astype(jnp.float32)).astype(jnp.bfloat16)
    return head, tail


def dot(a, b):
    return jnp.dot(a, b, preferred_element_type=jnp.float32)


def two_sided(re, im, right, left, slots, size):
    head, tail = halves(jnp.concatenate([re, im], axis=1))
    y = dot(head, right[0]) + dot(tail, right[0]) + dot(head, right[1])
    z = jnp.concatenate(
        [
            jnp.concatenate(
                [y[j * size : (j + 1) * size, :size], y[j * size : (j + 1) * size, size:]], axis=0
            )
            for j in range(slots)
        ],
        axis=1,
    )
    head, tail = halves(z)
    y = dot(left[0], head) + dot(left[0], tail) + dot(left[1], head)
    out_re = [y[:size, j * size : (j + 1) * size] for j in range(slots)]
    out_im = [y[size:, j * size : (j + 1) * size] for j in range(slots)]
    return jnp.concatenate(out_re, axis=0), jnp.concatenate(out_im, axis=0)


def gather_kernel(pos, trans, *outs):
    depth = pos[0, 0]
    blocks = trans.shape[2] // LANES
    shape = (trans.shape[0], trans.shape[1], LANES)
    lane = lax.broadcasted_iota(jnp.int32, shape, 2)
    for which in range(3):
        for rel in range(2):
            out = outs[2 * which + rel]

            def one(j, carry, which=which, rel=rel, out=out):
                slot = 2 * j + (depth if rel == 0 else 1 - depth)
                col = pos[2 + 2 * which, slot]
                block = col // LANES
                after = jnp.minimum(block + 1, blocks - 1)
                x = trans[:, :, pl.ds(pl.multiple_of(block * LANES, LANES), LANES)]
                y = trans[:, :, pl.ds(pl.multiple_of(after * LANES, LANES), LANES)]
                out[j] = jnp.where(lane >= col - block * LANES, x, y)
                return carry

            lax.fori_loop(0, out.shape[0], one, 0)


def wave_kernel(
    pos, probe, diff, keep_rim, keep_own, got_rim, got_own, a_right, a_left, f_right, f_left,
    rim_keep, own_keep, rim_give, own_give, probe_out, patch, psi,
):
    depth = pos[0, 0]
    filled = pos[0, 1]
    rounds, _, half, size = keep_rim.shape
    group = keep_rim.shape[1] // 2
    slices = 2 * group

    def slot_of(j):
        return 2 * j + depth

    def rows(j):
        return slice(j * size, (j + 1) * size)

    def shift_of(j):
        return pos[1, slot_of(j)], pos[2, slot_of(j)] % LANES

    for j in range(rounds):
        down, across = shift_of(j)
        for part in range(2):
            rolled = pltpu.roll(pltpu.roll(probe[part], down, 0), across, 1)
            psi[0, part, rows(j), :] = rolled
            for s in range(slices):
                a = part * group + s % group
                mine = depth == s // group
                patch[s, part, j * size : j * size + half, :] = jnp.where(
                    mine, keep_rim[j, a], got_rim[j, a]
                )
                patch[s, part, j * size + half : (j + 1) * size, :] = jnp.where(
                    mine, keep_own[j, a], got_own[j, a]
                )

    def times(a, b):
        return a[0] * b[0] - a[1] * b[1], a[0] * b[1] + a[1] * b[0]

    def load(ref, s):
        return ref[s, 0], ref[s, 1]

    def apply(wave, right, left):
        return two_sided(wave[0], wave[1], right, left, rounds, size)

    for s in range(slices - 1):
        wave = apply(times(load(patch, s), load(psi, s)), a_right, a_left)
        psi[s + 1, 0] = wave[0]
        psi[s + 1, 1] = wave[1]
    far = apply(times(load(patch, slices - 1), load(psi, slices - 1)), f_right, f_left)
    measured = jnp.concatenate([diff[slot_of(j)] for j in range(rounds)], axis=0)
    misfit = far[0] * far[0] + far[1] * far[1] - measured
    back = (misfit * far[0], -(misfit * far[1]))
    for s in reversed(range(slices)):
        if s == slices - 1:
            along = apply(back, f_right, f_left)
        else:
            along = apply(back, a_right, a_left)
        term = times(load(psi, s), along)
        term = (term[0], -term[1])
        back = times(load(patch, s), along)
        mine = depth == s // group

        def store(rim, own, term=term, s=s):
            for j in range(rounds):
                on = slot_of(j) < filled
                for part in range(2):
                    a = part * group + s % group
                    value = jnp.where(on, term[part][rows(j)], 0.0)
                    rim[j, a] = value[:half]
                    own[j, a] = value[half:]

        @pl.when(mine)
        def _(store=store):
            store(rim_keep, own_keep)

        @pl.when(jnp.logical_not(mine))
        def _(store=store):
            store(rim_give, own_give)

    for part in range(2):
        total = jnp.zeros((size, size), jnp.float32)
        for j in range(rounds):
            down, across = shift_of(j)
            value = jnp.where(slot_of(j) < filled, back[part][rows(j)], 0.0)
            value = pltpu.roll(value, lax.rem(size - down, size), 0)
            total = total + pltpu.roll(value, lax.rem(size - across, size), 1)
        probe_out[part] = total if part == 0 else -total


def scatter_kernel(pos, own_k, own_g, near_k, near_g, far_k, far_g, out):
    depth = pos[0, 0]
    odd = pos[0, 2]
    blocks = out.shape[2] // LANES
    shape = (out.shape[0], out.shape[1], LANES)
    lane = lax.broadcasted_iota(jnp.int32, shape, 2)
    row = lax.broadcasted_iota(jnp.int32, shape, 1)
    out[...] = jnp.zeros_like(out)
    for index, ref in enumerate((own_k, own_g, near_k, near_g, far_k, far_g)):
        which, rel = index // 2, index % 2

        def one(j, carry, which=which, rel=rel, ref=ref):
            slot = 2 * j + (depth if rel == 0 else 1 - depth)
            value = ref[j]
            col = pos[2 + 2 * which, slot]
            if which:
                under = odd if which == 1 else 1 - odd
                start = pos[1 + 2 * which, slot]
                low = jnp.where(under == 1, 0, start)
                high = jnp.where(under == 1, start, shape[1])
                value = jnp.where((row >= low) & (row < high), value, 0.0)
            block = col // LANES
            after = jnp.minimum(block + 1, blocks - 1)
            inside = lane >= col - block * LANES
            at = pl.ds(pl.multiple_of(block * LANES, LANES), LANES)
            out[:, :, at] = out[:, :, at] + jnp.where(inside, value, 0.0)
            at = pl.ds(pl.multiple_of(after * LANES, LANES), LANES)
            out[:, :, at] = out[:, :, at] + jnp.where(inside, 0.0, value)
            return carry

        lax.fori_loop(0, ref.shape[0], one, 0)


SMEM = pl.BlockSpec(memory_space=pltpu.SMEM)
VMEM = pl.BlockSpec(memory_space=pltpu.VMEM)
PARAMS = pltpu.CompilerParams(vmem_limit_bytes=48 * 1024 * 1024)


def shards(transmission, probe, scan_rows, scan_cols, tile_counts, diffraction):
    size = probe.shape[-1]
    half = size // 2
    group, strip, cols = transmission.shape[1:]
    rounds = scan_rows.shape[0] // 2
    tiles = lax.axis_size("tile")
    depth = lax.axis_index("depth")
    tile = lax.axis_index("tile")
    odd = tile % 2
    f32 = jnp.float32

    beside = [(c, c ^ 1) for c in range(tiles)]
    across = [(c, c + 1 if c % 2 else c - 1) for c in range(1, tiles - 1)]
    hop = [(c, c + 2 if c % 2 else c - 2) for c in range(tiles)]
    hop = [(a, b) for a, b in hop if 0 <= b < tiles]
    hop_back = [(b, a) for a, b in hop]
    swap = [(0, 1), (1, 0)]

    start = scan_rows - (tile * strip - half)
    place = jnp.stack([start, scan_cols]).astype(jnp.int32)
    place_near = lax.ppermute(place, "tile", beside)
    place_far = lax.ppermute(place, "tile", across)
    head = jnp.zeros((1, scan_rows.shape[0]), jnp.int32)
    head = head.at[0, 0].set(depth).at[0, 1].set(tile_counts[tile]).at[0, 2].set(odd)
    pos = jnp.concatenate([head, place, place_near, place_far], axis=0)

    flat = transmission.reshape(2 * group, strip, cols)
    piece = jax.ShapeDtypeStruct((rounds, 2 * group, strip, LANES), f32)
    own_k, own_g, near_k, near_g, far_k, far_g = pl.pallas_call(
        gather_kernel,
        out_shape=[piece] * 6,
        in_specs=[SMEM, VMEM],
        out_specs=[VMEM] * 6,
        compiler_params=PARAMS,
        name="gather",
    )(pos, flat)

    near_start = place_near[0].reshape(rounds, 2)

    def rim_of(near, far, parity):
        begin = lax.dynamic_index_in_dim(near_start, parity, 1, keepdims=False)
        row = lax.broadcasted_iota(jnp.int32, near.shape, 2)
        above = row >= begin[:, None, None, None]
        return jnp.where(above == (odd == 0), near, far)

    hop_g = lax.ppermute(far_g, "tile", hop)
    hop_k = lax.ppermute(far_k, "tile", hop)
    own_got = lax.ppermute(own_g, "depth", swap)
    rim_g = lax.ppermute(rim_of(near_g, hop_g, 1 - depth), "tile", beside)
    rim_k = lax.ppermute(rim_of(near_k, hop_k, depth), "tile", beside)
    rim_got = lax.ppermute(rim_g, "depth", swap)

    tabs = [jnp.asarray(t) for t in tables(size)]
    waves = (2 * group, 2, rounds * size, size)
    rim_keep, own_keep, rim_give, own_give, probe_part = pl.pallas_call(
        wave_kernel,
        out_shape=[piece] * 4 + [jax.ShapeDtypeStruct(probe.shape, f32)],
        in_specs=[SMEM] + [VMEM] * 10,
        out_specs=[VMEM] * 5,
        scratch_shapes=[pltpu.VMEM(waves, f32), pltpu.VMEM(waves, f32)],
        compiler_params=PARAMS,
        name="waves",
    )(pos, probe, diffraction, rim_k, own_k, rim_got, own_got, *tabs)

    rim_back = lax.ppermute(rim_give, "depth", swap)
    own_back = lax.ppermute(own_give, "depth", swap)
    near_k = lax.ppermute(rim_keep, "tile", beside)
    near_g = lax.ppermute(rim_back, "tile", beside)
    far_k = lax.ppermute(near_k, "tile", hop_back)
    far_g = lax.ppermute(near_g, "tile", hop_back)
    probe_rows = lax.psum_scatter(probe_part, "depth", scatter_dimension=1, tiled=True)
    probe_grad = lax.psum(probe_rows, "tile")

    grads = pl.pallas_call(
        scatter_kernel,
        out_shape=jax.ShapeDtypeStruct(flat.shape, f32),
        in_specs=[SMEM] + [VMEM] * 6,
        out_specs=VMEM,
        compiler_params=PARAMS,
        name="scatter",
    )(pos, own_keep, own_back, near_k, near_g, far_k, far_g)
    return (grads.reshape(transmission.shape), probe_grad)


def solution(mesh):
    placed = (P(None, "depth", "tile", None), P(), P("tile"), P("tile"), P(), P("tile", None, None))
    return jax.shard_map(
        shards,
        mesh=mesh,
        in_specs=placed,
        out_specs=(P(None, "depth", "tile", None), P(None, "depth", None)),
        check_vma=False,
    )
```

time: 851 us -> 238 us (0.28)
  waiting for transfers between devices: 443 us -> 169 us
  starting transfers between devices: 162 us -> 18.7 us
  local copies, waits for them, and re-layouts: 84.7 us -> 10.9 us
  loops' own time: 65.3 us -> 0 us
  matrix products: 47.9 us -> 0 us
  other arithmetic: 29.6 us -> 8.3 us
  Pallas kernels: 0 us -> 16.2 us
    reduce_scatter x1, waiting for transfers between devices: 173 us -> 7.72 us  [shards(): lax.psum_scatter(probe_part, 'depth', scatter_dimension=1, tiled=True)]
    ppermute x22 -> x14, starting transfers between devices: 162 us -> 18.6 us  [the longest x1 5.74 us: shards(): place_near = lax.ppermute(place, 'tile', beside)]
    ppermute x22 -> x14, waiting for transfers between devices: 133 us -> 59.3 us  [the longest x1 14.2 us: shards(): hop_g = lax.ppermute(far_g, 'tile', hop)]
    another operation x24 -> x0, loops' own time: 65.3 us -> none  [the longest x1 45.1 us: shards(): grads = lax.fori_loop(0, order.shape[0], place_one, grads_start)]
    dot_general x160 -> x0, matrix products: 47.9 us -> none  [the longest x80 25.1 us: prod(): return jnp.einsum('...ij,jk->...ik', x, m, precision=HIGH)]
    psum x1, waiting for transfers between devices: 137 us -> 102 us  [shards(): probe_grad = lax.psum(probe_rows, 'tile')]
    gather x28 -> x0, local copies, waits for them, and re-layouts: 26.4 us -> none
    dynamic_update_slice x8 -> x0, local copies, waits for them, and re-layouts: 26 us -> none  [place_one(): lax.dynamic_update_slice(total, current + windows[item] * weights[item],...]
  transfers between devices with their start and end apart: 24 -> 16, of which waited for: 22 -> 10; matrix products, arithmetic and copies ran while one was open for 1% -> 5% of each run, Pallas kernels for 0% -> 2%
where the time goes in v1:
time: 238 us
  waiting for transfers between devices  169 us (71%)
  starting transfers between devices  18.7 us (8%)
  Pallas kernels  16.2 us (7%)
  between operations  14.9 us (6%)
  local copies, waits for them, and re-layouts  10.9 us (5%)
  other arithmetic  8.3 us (3%)
    psum x1, waiting for transfers between devices, shards(): probe_grad = lax.psum(probe_rows, 'tile')  102 us
    ppermute x1, waiting for transfers between devices, shards(): hop_g = lax.ppermute(far_g, 'tile', hop)  14.2 us
    ppermute x1, waiting for transfers between devices, shards(): near_k = lax.ppermute(rim_keep, 'tile', beside)  12.5 us
    ppermute x1, waiting for transfers between devices, shards(): rim_k = lax.ppermute(rim_of(near_k, hop_k, depth), 'tile', beside)  10.1 us
    pallas_call x1, Pallas kernels, shards(): pl.pallas_call(wave_kernel, out_shape=[piece] * 4 + [jax.ShapeDtypeStruct...  9.79 us
    ppermute x1, waiting for transfers between devices, shards(): hop_k = lax.ppermute(far_k, 'tile', hop)  8.01 us
    reduce_scatter x1, waiting for transfers between devices, shards(): lax.psum_scatter(probe_part, 'depth', scatter_dimension=1, tiled=True)  7.72 us
    ppermute x1, waiting for transfers between devices, shards(): near_g = lax.ppermute(rim_back, 'tile', beside)  6.5 us
  transfers between devices with their start and end apart: 16, of which 10 were waited for; matrix products, arithmetic and copies ran while one was open for 5% of the time, Pallas kernels for 2%

profile of v1, /device:TPU:0, one launch (start us, length us, event | category | flops | bytes accessed | tf_op | source)
XLA Modules:
  0.0 237.7 jit_solution(2935422612132981352)
XLA Ops:
  7.2 0.0 reduce-scatter.2.cloned.1.call-start
  7.2 0.7 subtract_bitcast_fusion
  7.9 0.7 pad_add_fusion
  8.5 0.6 collective-permute-start.1
  9.2 5.7 %collective-permute-start = (s32[2,8]{1,0:T(2,128)S(1)}, s32[2,8]{1,0:T(2,128)S(1)}, u32[]{:S(2)}, u32[]{:S(2)}) collective-permute-start(s32[2,8]{1,0:T(2,128)S(1)} %pad_add_fusion), channel_id=1, source_target_pairs={{0,1},{1,0},{2,3},{3,2},{4,5},{5,4},{6,7},{7,6},{8,9},{9,8},{10,11... | collective-permute-start | bytes 200 | tf_op jit(solution)/shard_map/ppermute | solution.py:233
  14.9 0.7 compare_reduce_fusion
  15.6 0.6 and_reduce_fusion
  16.2 0.6 slice.59
  16.9 0.6 slice.58
  18.2 1.2 dynamic_slice.10
  19.4 2.5 %fusion.4 = s32[1,1]{1,0:T(1,128)} fusion(pred[1,1]{1,0:T(4,128)(4,1)} %bitcast.1, s32[1,1]{1,0:T(1,128)} %bitcast.2, s32[]{:T(128)} %bitcast.3, s32[1,1]{1,0:T(1,128)} %bitcast), kind=kLoop, calls=%fused_computation.18 | loop fusion | flops 1 | bytes 17 | tf_op jit(solution)/shard_map/select.4
  21.9 1.4 scatter.14
  23.3 1.9 fusion.5
  25.2 1.4 scatter.18
  26.5 0.0 collective-permute-done.1
  26.5 0.0 collective-permute-done
  26.6 0.7 concatenate.10.pos
  27.2 1.6 copy-done
  28.8 2.6 %gather.1 = (f32[4,4,64,128]{3,2,1,0:T(8,128)S(1)}, f32[4,4,64,128]{3,2,1,0:T(8,128)S(1)}, f32[4,4,64,128]{3,2,1,0:T(8,128)S(1)}, f32[4,4,64,128]{3,2,1,0:T(8,12...) custom-call(s32[7,8]{1,0:T(8,128)S(1)} %concatenate.10.pos, f32[4,64,2048]{2,1,0:T(8,128)S(1)} %bitcast.12), custom_call_target="tpu_custom_call" | custom-call | tf_op jit(solution)/shard_map/gather/pallas_call | solution.py:241
  31.4 0.8 copy-done.7
  32.2 0.8 copy-done.8
  33.0 0.0 copy-start.5
  33.0 0.0 copy-start.6
  33.0 1.4 collective-permute-start.4
  34.5 0.1 reshape_squeeze.3
  34.5 1.3 collective-permute-start.2
  35.8 0.2 dynamic-slice_reduce_fusion
  36.1 14.2 %collective-permute-done.4 = f32[4,4,64,128]{3,2,1,0:T(8,128)} collective-permute-done((f32[4,4,64,128]{3,2,1,0:T(8,128)}, f32[4,4,64,128]{3,2,1,0:T(8,128)}, u32[]{:S(2)}, u32[]{:S(2)}) %collective-permute-start.4) | collective-permute-done | bytes 524320 | tf_op jit(solution)/shard_map/ppermute | solution.py:258
  50.2 1.2 fusion.3
  51.4 0.1 collective-permute-start.5
  51.5 0.1 collective-permute-start.7
  51.6 8.0 %collective-permute-done.2 = f32[4,4,64,128]{3,2,1,0:T(8,128)S(1)} collective-permute-done((f32[4,4,64,128]{3,2,1,0:T(8,128)}, f32[4,4,64,128]{3,2,1,0:T(8,128)S(1)}, u32[]{:S(2)}, u32[]{:S(2)}) %collective-permute-start.2) | collective-permute-done | bytes 524320 | tf_op jit(solution)/shard_map/ppermute | solution.py:259
  59.6 0.1 fusion.1
  59.7 0.1 collective-permute-start.3
  59.8 3.2 %collective-permute-done.5 = f32[4,4,64,128]{3,2,1,0:T(8,128)S(1)} collective-permute-done((f32[4,4,64,128]{3,2,1,0:T(8,128)S(1)}, f32[4,4,64,128]{3,2,1,0:T(8,128)S(1)}, u32[]{:S(2)}, u32[]{:S(2)}) %collective-permute-start.5) | collective-permute-done | bytes 524320 | tf_op jit(solution)/shard_map/ppermute | solution.py:261
  63.0 0.0 collective-permute-start.6
  63.0 0.0 collective-permute-done.7.got_own
  63.0 10.1 %collective-permute-done.3.keep_rim = f32[4,4,64,128]{3,2,1,0:T(8,128)S(1)} collective-permute-done((f32[4,4,64,128]{3,2,1,0:T(8,128)S(1)}, f32[4,4,64,128]{3,2,1,0:T(8,128)S(1)}, u32[]{:S(2)}, u32[]{:S(2)}) %collective-permute-start.3) | collective-permute-done | bytes 524320 | tf_op jit(solution)/shard_map/ppermute | solution.py:262
  73.1 0.0 collective-permute-done.6.got_rim
  73.1 0.0 copy-done.2
  73.1 0.0 copy-done.3
  73.2 0.0 copy-done.4
  73.2 0.0 copy-done.5
  73.2 0.0 copy-done.6
  73.2 9.8 %waves.1 = (f32[4,4,64,128]{3,2,1,0:T(8,128)S(1)}, f32[4,4,64,128]{3,2,1,0:T(8,128)S(1)}, f32[4,4,64,128]{3,2,1,0:T(8,128)S(1)}, f32[4,4,64,128]{3,2,1,0:T(8,128)}, f32[2,128,128]{2,1,0:T(8,128)}) custom-call(s32[7,8]{1,0:T(8,128)S(1)} %concatenate.10.pos, f32[2,128,128]{2,1,0:T(8,128)S(1)} %copy-done.6, f32[8,128,128]{2,1,0:T(8,128)S(1)} %copy-done.1, ...), custom_call_target="tpu_custom_call" | custom-call | tf_op jit(solution)/shard_map/waves/pallas_call | solution.py:267
  83.0 0.0 collective-permute-start.10
  83.0 0.3 collective-permute-start.9
  83.3 1.6 collective-permute-done.10
  84.9 0.3 collective-permute-start.11
  85.2 0.0 collective-permute-start.8
  85.2 12.5 %collective-permute-done.9.near_k = f32[4,4,64,128]{3,2,1,0:T(8,128)S(1)} collective-permute-done((f32[4,4,64,128]{3,2,1,0:T(8,128)S(1)}, f32[4,4,64,128]{3,2,1,0:T(8,128)S(1)}, u32[]{:S(2)}, u32[]{:S(2)}) %collective-permute-start.9) | collective-permute-done | bytes 524320 | tf_op jit(solution)/shard_map/ppermute | solution.py:279
  97.7 4.3 %collective-permute-start.12 = (f32[4,4,64,128]{3,2,1,0:T(8,128)S(1)}, f32[4,4,64,128]{3,2,1,0:T(8,128)S(1)}, u32[]{:S(2)}, u32[]{:S(2)}) collective-permute-start(f32[4,4,64,128]{3,2,1,0:T(8,128)S(1)} %collective-permute-done.9.near_k), channel_id=1, source_target_pairs={{3,1},{0,2},{5,3},{2,4},{7,5},{4,6},{9,7},{6,8},{11,9},{8,10},{13,... | collective-permute-start | bytes 1572872 | tf_op jit(solution)/shard_map/ppermute | solution.py:281
  102.1 6.5 %collective-permute-done.11.near_g = f32[4,4,64,128]{3,2,1,0:T(8,128)S(1)} collective-permute-done((f32[4,4,64,128]{3,2,1,0:T(8,128)S(1)}, f32[4,4,64,128]{3,2,1,0:T(8,128)S(1)}, u32[]{:S(2)}, u32[]{:S(2)}) %collective-permute-start.11) | collective-permute-done | bytes 524320 | tf_op jit(solution)/shard_map/ppermute | solution.py:280
  108.6 4.3 %collective-permute-start.13 = (f32[4,4,64,128]{3,2,1,0:T(8,128)S(1)}, f32[4,4,64,128]{3,2,1,0:T(8,128)S(1)}, u32[]{:S(2)}, u32[]{:S(2)}) collective-permute-start(f32[4,4,64,128]{3,2,1,0:T(8,128)S(1)} %collective-permute-done.11.near_g), channel_id=1, source_target_pairs={{3,1},{0,2},{5,3},{2,4},{7,5},{4,6},{9,7},{6,8},{11,9},{8,10},{13,... | collective-permute-start | bytes 1572872 | tf_op jit(solution)/shard_map/ppermute | solution.py:282
  112.9 0.0 reduce-scatter.2.cloned.1.call-update
  112.9 0.0 all-reduce.3.cloned.1.call-start
  113.0 7.7 %reduce-scatter.2.cloned.1.call-done = f32[2,64,128]{2,1,0:T(8,128)} async-done(((f32[2,128,128]{2,1,0:T(8,128)}), f32[2,64,128]{2,1,0:T(8,128)}) %reduce-scatter.2.cloned.1.call-update) | async-done | bytes 65552 | tf_op jit(solution)/shard_map/reduce_scatter | solution.py:283
  120.7 0.0 all-reduce.3.cloned.1.call-update
  120.7 0.0 collective-permute-done.8.own_g
  120.7 0.0 collective-permute-done.12.far_k
  120.7 3.2 %collective-permute-done.13.far_g = f32[4,4,64,128]{3,2,1,0:T(8,128)S(1)} collective-permute-done((f32[4,4,64,128]{3,2,1,0:T(8,128)S(1)}, f32[4,4,64,128]{3,2,1,0:T(8,128)S(1)}, u32[]{:S(2)}, u32[]{:S(2)}) %collective-permute-start.13) | collective-permute-done | bytes 524320 | tf_op jit(solution)/shard_map/ppermute | solution.py:282
  123.9 3.8 %scatter.20 = f32[4,64,2048]{2,1,0:T(8,128)} custom-call(s32[7,8]{1,0:T(8,128)S(1)} %concatenate.10.pos, f32[4,4,64,128]{3,2,1,0:T(8,128)S(1)} %get-tuple-element.55.own_k, f32[4,4,64,128]{3,2,1,0:T(8,128)S(1)} %collective-permute-done.8.own_g, f32[4,4,64,128]{3,2,1,0:T(8,128)S(1)} %collective-permute-done.9.near_k, ...), custom_call_target="tpu_custom_call" | custom-call | tf_op jit(solution)/shard_map/scatter/pallas_call | solution.py:286
  127.8 101.6 %all-reduce.3.cloned.1.call-done = f32[2,64,128]{2,1,0:T(8,128)} async-done(((f32[2,64,128]{2,1,0:T(8,128)}), f32[2,64,128]{2,1,0:T(8,128)}) %all-reduce.3.cloned.1.call-update) | async-done | bytes 65552 | tf_op jit(solution)/shard_map/psum | solution.py:284
  229.4 1.5 copy.15
  (12 shorter events, 0.0 us)
Async XLA Ops:
  7.2 113.5 %reduce-scatter.2.cloned.1.call-start = ((), (), s32[]{:S(2)}) async-start(), calls=%async_computation.1 | async-start | bytes 196608 | tf_op jit(solution)/shard_map/reduce_scatter | solution.py:283
  8.5 18.0 %collective-permute-start.1 = (s32[2,8]{1,0:T(2,128)S(1)}, s32[2,8]{1,0:T(2,128)S(1)}, u32[]{:S(2)}, u32[]{:S(2)}) collective-permute-start(s32[2,8]{1,0:T(2,128)S(1)} %pad_add_fusion), channel_id=1, source_target_pairs={{1,2},{2,1},{3,4},{4,3},{5,6},{6,5},{7,8},{8,7},{9,10},{10,9},{11,... | collective-permute-start | bytes 200 | tf_op jit(solution)/shard_map/ppermute | solution.py:234
  9.2 17.4 %collective-permute-start = (s32[2,8]{1,0:T(2,128)S(1)}, s32[2,8]{1,0:T(2,128)S(1)}, u32[]{:S(2)}, u32[]{:S(2)}) collective-permute-start(s32[2,8]{1,0:T(2,128)S(1)} %pad_add_fusion), channel_id=1, source_target_pairs={{0,1},{1,0},{2,3},{3,2},{4,5},{5,4},{6,7},{7,6},{8,9},{9,8},{10,11... | collective-permute-start | bytes 200 | tf_op jit(solution)/shard_map/ppermute | solution.py:233
  27.2 1.6 copy-start
  31.4 0.8 copy-start.7
  32.2 0.8 copy-start.8
  33.0 40.2 %copy-start.1 = (f32[8,128,128]{2,1,0:T(8,128)S(1)}, f32[8,128,128]{2,1,0:T(8,128)}, u32[]{:S(2)}) copy-start(f32[8,128,128]{2,1,0:T(8,128)} %diff.1) | copy-start | bytes 1572868
  33.0 40.2 %copy-start.2 = (bf16[2,256,256]{2,1,0:T(8,128)(2,1)S(1)}, bf16[2,256,256]{2,1,0:T(8,128)(2,1)}, u32[]{:S(2)}) copy-start(bf16[2,256,256]{2,1,0:T(8,128)(2,1)} %constant.124.clone.f_left) | copy-start | bytes 786436
  33.0 40.2 %copy-start.3 = (bf16[2,256,256]{2,1,0:T(8,128)(2,1)S(1)}, bf16[2,256,256]{2,1,0:T(8,128)(2,1)}, u32[]{:S(2)}) copy-start(bf16[2,256,256]{2,1,0:T(8,128)(2,1)} %constant.123.clone.f_right) | copy-start | bytes 786436
  33.0 40.2 %copy-start.4 = (bf16[2,256,256]{2,1,0:T(8,128)(2,1)S(1)}, bf16[2,256,256]{2,1,0:T(8,128)(2,1)}, u32[]{:S(2)}) copy-start(bf16[2,256,256]{2,1,0:T(8,128)(2,1)} %constant.122.clone.a_left) | copy-start | bytes 786436
  33.0 40.2 %copy-start.5 = (bf16[2,256,256]{2,1,0:T(8,128)(2,1)S(1)}, bf16[2,256,256]{2,1,0:T(8,128)(2,1)}, u32[]{:S(2)}) copy-start(bf16[2,256,256]{2,1,0:T(8,128)(2,1)} %constant.121.clone.a_right) | copy-start | bytes 786436
  33.0 40.2 %copy-start.6 = (f32[2,128,128]{2,1,0:T(8,128)S(1)}, f32[2,128,128]{2,1,0:T(8,128)}, u32[]{:S(2)}) copy-start(f32[2,128,128]{2,1,0:T(8,128)} %probe.1) | copy-start | bytes 393220
  33.0 17.2 %collective-permute-start.4 = (f32[4,4,64,128]{3,2,1,0:T(8,128)}, f32[4,4,64,128]{3,2,1,0:T(8,128)}, u32[]{:S(2)}, u32[]{:S(2)}) collective-permute-start(f32[4,4,64,128]{3,2,1,0:T(8,128)} %get-tuple-element.53), channel_id=1, source_target_pairs={{1,3},{2,0},{3,5},{4,2},{5,7},{6,4},{7,9},{8,6},{9,11},{10,8},{11,... | collective-permute-start | bytes 1572872 | tf_op jit(solution)/shard_map/ppermute | solution.py:258
  34.5 25.0 %collective-permute-start.2 = (f32[4,4,64,128]{3,2,1,0:T(8,128)}, f32[4,4,64,128]{3,2,1,0:T(8,128)S(1)}, u32[]{:S(2)}, u32[]{:S(2)}) collective-permute-start(f32[4,4,64,128]{3,2,1,0:T(8,128)} %copy-done.8), channel_id=1, source_target_pairs={{1,3},{2,0},{3,5},{4,2},{5,7},{6,4},{7,9},{8,6},{9,11},{10,8},{11,... | collective-permute-start | bytes 1572872 | tf_op jit(solution)/shard_map/ppermute | solution.py:259
  51.4 11.6 %collective-permute-start.5 = (f32[4,4,64,128]{3,2,1,0:T(8,128)S(1)}, f32[4,4,64,128]{3,2,1,0:T(8,128)S(1)}, u32[]{:S(2)}, u32[]{:S(2)}) collective-permute-start(f32[4,4,64,128]{3,2,1,0:T(8,128)S(1)} %fusion.3), channel_id=1, source_target_pairs={{0,1},{1,0},{2,3},{3,2},{4,5},{5,4},{6,7},{7,6},{8,9},{9,8},{10,11... | collective-permute-start | bytes 1572872 | tf_op jit(solution)/shard_map/ppermute | solution.py:261
  51.5 11.5 %collective-permute-start.7 = (f32[4,4,64,128]{3,2,1,0:T(8,128)}, f32[4,4,64,128]{3,2,1,0:T(8,128)S(1)}, u32[]{:S(2)}, u32[]{:S(2)}) collective-permute-start(f32[4,4,64,128]{3,2,1,0:T(8,128)} %copy-done.7), channel_id=1, source_target_pairs={{0,16},{16,0},{1,17},{17,1},{2,18},{18,2},{3,19},{19,3},{4,20},{20... | collective-permute-start | bytes 1572872 | tf_op jit(solution)/shard_map/ppermute | solution.py:260
  59.7 13.4 %collective-permute-start.3 = (f32[4,4,64,128]{3,2,1,0:T(8,128)S(1)}, f32[4,4,64,128]{3,2,1,0:T(8,128)S(1)}, u32[]{:S(2)}, u32[]{:S(2)}) collective-permute-start(f32[4,4,64,128]{3,2,1,0:T(8,128)S(1)} %fusion.1), channel_id=1, source_target_pairs={{0,1},{1,0},{2,3},{3,2},{4,5},{5,4},{6,7},{7,6},{8,9},{9,8},{10,11... | collective-permute-start | bytes 1572872 | tf_op jit(solution)/shard_map/ppermute | solution.py:262
  63.0 10.1 %collective-permute-start.6 = (f32[4,4,64,128]{3,2,1,0:T(8,128)S(1)}, f32[4,4,64,128]{3,2,1,0:T(8,128)S(1)}, u32[]{:S(2)}, u32[]{:S(2)}) collective-permute-start(f32[4,4,64,128]{3,2,1,0:T(8,128)S(1)} %collective-permute-done.5), channel_id=1, source_target_pairs={{0,16},{16,0},{1,17},{17,1},{2,18},{18,2},{3,19},{19,3},{4,20},{20... | collective-permute-start | bytes 1572872 | tf_op jit(solution)/shard_map/ppermute | solution.py:263
  83.0 1.9 collective-permute-start.10
  83.0 14.7 %collective-permute-start.9 = (f32[4,4,64,128]{3,2,1,0:T(8,128)S(1)}, f32[4,4,64,128]{3,2,1,0:T(8,128)S(1)}, u32[]{:S(2)}, u32[]{:S(2)}) collective-permute-start(f32[4,4,64,128]{3,2,1,0:T(8,128)S(1)} %get-tuple-element.57), channel_id=1, source_target_pairs={{0,1},{1,0},{2,3},{3,2},{4,5},{5,4},{6,7},{7,6},{8,9},{9,8},{10,11... | collective-permute-start | bytes 1572872 | tf_op jit(solution)/shard_map/ppermute | solution.py:279
  84.9 23.7 %collective-permute-start.11 = (f32[4,4,64,128]{3,2,1,0:T(8,128)S(1)}, f32[4,4,64,128]{3,2,1,0:T(8,128)S(1)}, u32[]{:S(2)}, u32[]{:S(2)}) collective-permute-start(f32[4,4,64,128]{3,2,1,0:T(8,128)S(1)} %collective-permute-done.10), channel_id=1, source_target_pairs={{0,1},{1,0},{2,3},{3,2},{4,5},{5,4},{6,7},{7,6},{8,9},{9,8},{10,11... | collective-permute-start | bytes 1572872 | tf_op jit(solution)/shard_map/ppermute | solution.py:280
  85.2 35.6 %collective-permute-start.8 = (f32[4,4,64,128]{3,2,1,0:T(8,128)}, f32[4,4,64,128]{3,2,1,0:T(8,128)S(1)}, u32[]{:S(2)}, u32[]{:S(2)}) collective-permute-start(f32[4,4,64,128]{3,2,1,0:T(8,128)} %get-tuple-element.56), channel_id=1, source_target_pairs={{0,16},{16,0},{1,17},{17,1},{2,18},{18,2},{3,19},{19,3},{4,20},{20... | collective-permute-start | bytes 1572872 | tf_op jit(solution)/shard_map/ppermute | solution.py:278
  97.7 23.0 %collective-permute-start.12 = (f32[4,4,64,128]{3,2,1,0:T(8,128)S(1)}, f32[4,4,64,128]{3,2,1,0:T(8,128)S(1)}, u32[]{:S(2)}, u32[]{:S(2)}) collective-permute-start(f32[4,4,64,128]{3,2,1,0:T(8,128)S(1)} %collective-permute-done.9.near_k), channel_id=1, source_target_pairs={{3,1},{0,2},{5,3},{2,4},{7,5},{4,6},{9,7},{6,8},{11,9},{8,10},{13,... | collective-permute-start | bytes 1572872 | tf_op jit(solution)/shard_map/ppermute | solution.py:281
  108.6 15.4 %collective-permute-start.13 = (f32[4,4,64,128]{3,2,1,0:T(8,128)S(1)}, f32[4,4,64,128]{3,2,1,0:T(8,128)S(1)}, u32[]{:S(2)}, u32[]{:S(2)}) collective-permute-start(f32[4,4,64,128]{3,2,1,0:T(8,128)S(1)} %collective-permute-done.11.near_g), channel_id=1, source_target_pairs={{3,1},{0,2},{5,3},{2,4},{7,5},{4,6},{9,7},{6,8},{11,9},{8,10},{13,... | collective-permute-start | bytes 1572872 | tf_op jit(solution)/shard_map/ppermute | solution.py:282
  112.9 116.4 %all-reduce.3.cloned.1.call-start = ((), (), s32[]{:S(2)}) async-start(), calls=%async_computation.2 | async-start | bytes 131072 | tf_op jit(solution)/shard_map/psum | solution.py:284
Sparse Core Ops, SparseCore 0:
  113.0 7.6 reduce-scatter.1
  126.2 103.1 all-reduce.2

commit v2 on v1

--- a/solution.py
+++ b/solution.py
@@ -62,8 +62,14 @@
     return jnp.concatenate(out_re, axis=0), jnp.concatenate(out_im, axis=0)
 
 
-def gather_kernel(pos, trans, *outs):
-    depth = pos[0, 0]
+def axis_places():
+    depth = lax.axis_index("depth")
+    tile = lax.axis_index("tile")
+    return depth, tile, lax.rem(tile, 2)
+
+
+def gather_kernel(own_cols, near_place, far_place, trans, *outs):
+    depth, _, _ = axis_places()
     blocks = trans.shape[2] // LANES
     shape = (trans.shape[0], trans.shape[1], LANES)
     lane = lax.broadcasted_iota(jnp.int32, shape, 2)
@@ -73,7 +79,7 @@
 
             def one(j, carry, which=which, rel=rel, out=out):
                 slot = 2 * j + (depth if rel == 0 else 1 - depth)
-                col = pos[2 + 2 * which, slot]
+                col = own_cols[slot] if which == 0 else (near_place, far_place)[which - 1][1, slot]
                 block = col // LANES
                 after = jnp.minimum(block + 1, blocks - 1)
                 x = trans[:, :, pl.ds(pl.multiple_of(block * LANES, LANES), LANES)]
@@ -85,11 +91,11 @@
 
 
 def wave_kernel(
-    pos, probe, diff, keep_rim, keep_own, got_rim, got_own, a_right, a_left, f_right, f_left,
+    own_rows, own_cols, counts, probe, diff, keep_rim, keep_own, got_rim, got_own, a_right, a_left, f_right, f_left,
     rim_keep, own_keep, rim_give, own_give, probe_out, patch, psi,
 ):
-    depth = pos[0, 0]
-    filled = pos[0, 1]
+    depth, tile, _ = axis_places()
+    filled = counts[tile]
     rounds, _, half, size = keep_rim.shape
     group = keep_rim.shape[1] // 2
     slices = 2 * group
@@ -101,7 +107,8 @@
         return slice(j * size, (j + 1) * size)
 
     def shift_of(j):
-        return pos[1, slot_of(j)], pos[2, slot_of(j)] % LANES
+        slot = slot_of(j)
+        return own_rows[slot] - (tile * half - half), lax.rem(own_cols[slot], LANES)
 
     for j in range(rounds):
         down, across = shift_of(j)
@@ -172,9 +179,8 @@
         probe_out[part] = total if part == 0 else -total
 
 
-def scatter_kernel(pos, own_k, own_g, near_k, near_g, far_k, far_g, out):
-    depth = pos[0, 0]
-    odd = pos[0, 2]
+def scatter_kernel(own_cols, near_place, far_place, own_k, own_g, near_k, near_g, far_k, far_g, out):
+    depth, tile, odd = axis_places()
     blocks = out.shape[2] // LANES
     shape = (out.shape[0], out.shape[1], LANES)
     lane = lax.broadcasted_iota(jnp.int32, shape, 2)
@@ -186,10 +192,12 @@
         def one(j, carry, which=which, rel=rel, ref=ref):
             slot = 2 * j + (depth if rel == 0 else 1 - depth)
             value = ref[j]
-            col = pos[2 + 2 * which, slot]
+            col = own_cols[slot] if which == 0 else (near_place, far_place)[which - 1][1, slot]
             if which:
                 under = odd if which == 1 else 1 - odd
-                start = pos[1 + 2 * which, slot]
+                place = (near_place, far_place)[which - 1]
+                owner = tile + (1 - 2 * odd if which == 1 else 2 * odd - 1)
+                start = place[0, slot] - (owner - 1) * shape[1]
                 low = jnp.where(under == 1, 0, start)
                 high = jnp.where(under == 1, start, shape[1])
                 value = jnp.where((row >= low) & (row < high), value, 0.0)
@@ -228,26 +236,23 @@
     hop_back = [(b, a) for a, b in hop]
     swap = [(0, 1), (1, 0)]
 
-    start = scan_rows - (tile * strip - half)
-    place = jnp.stack([start, scan_cols]).astype(jnp.int32)
+    place = jnp.stack([scan_rows, scan_cols])
     place_near = lax.ppermute(place, "tile", beside)
     place_far = lax.ppermute(place, "tile", across)
-    head = jnp.zeros((1, scan_rows.shape[0]), jnp.int32)
-    head = head.at[0, 0].set(depth).at[0, 1].set(tile_counts[tile]).at[0, 2].set(odd)
-    pos = jnp.concatenate([head, place, place_near, place_far], axis=0)
 
     flat = transmission.reshape(2 * group, strip, cols)
     piece = jax.ShapeDtypeStruct((rounds, 2 * group, strip, LANES), f32)
     own_k, own_g, near_k, near_g, far_k, far_g = pl.pallas_call(
         gather_kernel,
         out_shape=[piece] * 6,
-        in_specs=[SMEM, VMEM],
+        in_specs=[SMEM] * 3 + [VMEM],
         out_specs=[VMEM] * 6,
         compiler_params=PARAMS,
         name="gather",
-    )(pos, flat)
-
-    near_start = place_near[0].reshape(rounds, 2)
+    )(scan_cols, place_near, place_far, flat)
+
+    near_tile = tile + 1 - 2 * odd
+    near_start = (place_near[0] - (near_tile - 1) * strip).reshape(rounds, 2)
 
     def rim_of(near, far, parity):
         begin = lax.dynamic_index_in_dim(near_start, parity, 1, keepdims=False)
@@ -267,12 +272,12 @@
     rim_keep, own_keep, rim_give, own_give, probe_part = pl.pallas_call(
         wave_kernel,
         out_shape=[piece] * 4 + [jax.ShapeDtypeStruct(probe.shape, f32)],
-        in_specs=[SMEM] + [VMEM] * 10,
+        in_specs=[SMEM] * 3 + [VMEM] * 10,
         out_specs=[VMEM] * 5,
         scratch_shapes=[pltpu.VMEM(waves, f32), pltpu.VMEM(waves, f32)],
         compiler_params=PARAMS,
         name="waves",
-    )(pos, probe, diffraction, rim_k, own_k, rim_got, own_got, *tabs)
+    )(scan_rows, scan_cols, tile_counts, probe, diffraction, rim_k, own_k, rim_got, own_got, *tabs)
 
     rim_back = lax.ppermute(rim_give, "depth", swap)
     own_back = lax.ppermute(own_give, "depth", swap)
@@ -280,17 +285,24 @@
     near_g = lax.ppermute(rim_back, "tile", beside)
     far_k = lax.ppermute(near_k, "tile", hop_back)
     far_g = lax.ppermute(near_g, "tile", hop_back)
-    probe_rows = lax.psum_scatter(probe_part, "depth", scatter_dimension=1, tiled=True)
-    probe_grad = lax.psum(probe_rows, "tile")
+    probe_halves = probe_part.reshape(2, 2, half, size)
+    kept = lax.dynamic_index_in_dim(probe_halves, depth, 1, keepdims=False)
+    given = lax.dynamic_index_in_dim(probe_halves, 1 - depth, 1, keepdims=False)
+    probe_grad = kept + lax.ppermute(given, "depth", swap)
+    step = 1
+    while step < tiles:
+        pairs = [(c, c ^ step) for c in range(tiles)]
+        probe_grad = probe_grad + lax.ppermute(probe_grad, "tile", pairs)
+        step *= 2
 
     grads = pl.pallas_call(
         scatter_kernel,
         out_shape=jax.ShapeDtypeStruct(flat.shape, f32),
-        in_specs=[SMEM] + [VMEM] * 6,
+        in_specs=[SMEM] * 3 + [VMEM] * 6,
         out_specs=VMEM,
         compiler_params=PARAMS,
         name="scatter",
-    )(pos, own_keep, own_back, near_k, near_g, far_k, far_g)
+    )(scan_cols, place_near, place_far, own_keep, own_back, near_k, near_g, far_k, far_g)
     return (grads.reshape(transmission.shape), probe_grad)
 
 

time: 238 us -> 123 us (0.52)
  waiting for transfers between devices: 169 us -> 66.1 us
  starting transfers between devices: 18.7 us -> 33 us
  between operations: 14.9 us -> 0.88 us
  local copies, waits for them, and re-layouts: 10.9 us -> 4.2 us
  other arithmetic: 8.3 us -> 2.7 us
    psum x1 -> x0, waiting for transfers between devices: 102 us -> none  [shards(): probe_grad = lax.psum(probe_rows, 'tile')]
    ppermute x0 -> x5, waiting for transfers between devices: none -> 15.1 us  [the longest x4 15.1 us: shards(): probe_grad = probe_grad + lax.ppermute(probe_grad, 'tile', pairs)]
    ppermute x0 -> x5, starting transfers between devices: none -> 8.39 us  [the longest x4 8.39 us: shards(): probe_grad = probe_grad + lax.ppermute(probe_grad, 'tile', pairs)]
    reduce_scatter x1 -> x0, waiting for transfers between devices: 7.72 us -> none  [shards(): lax.psum_scatter(probe_part, 'depth', scatter_dimension=1, tiled=True)]
    another operation x7 -> x1, other arithmetic: 6.97 us -> 0.68 us  [shards(): place = jnp.stack([scan_rows, scan_cols])]
    ppermute x1, waiting for transfers between devices: 3.18 us -> 0.01 us  [shards(): far_g = lax.ppermute(near_g, 'tile', hop_back)]
    scatter x3 -> x0, local copies, waits for them, and re-layouts: 2.76 us -> none  [shards(): head.at[0, 0].set(depth).at[0, 1].set(tile_counts[tile]).at[0, 2].set(odd)]
  transfers between devices with their start and end apart: 16 -> 19, of which waited for: 10 -> 12; matrix products, arithmetic and copies ran while one was open for 5% -> 2% of each run, Pallas kernels for 2% -> 0%
where the time goes in v2:
time: 123 us; the launch traced here: 122 us
  waiting for transfers between devices  66.1 us (54%)
  starting transfers between devices  33 us (27%)
  Pallas kernels  15.4 us (13%)
  local copies, waits for them, and re-layouts  4.2 us (3%)
  other arithmetic  2.7 us (2%)
    ppermute x4, waiting for transfers between devices, shards(): probe_grad = probe_grad + lax.ppermute(probe_grad, 'tile', pairs)  15.1 us
    ppermute x1, waiting for transfers between devices, shards(): hop_g = lax.ppermute(far_g, 'tile', hop)  14.1 us
    ppermute x1, waiting for transfers between devices, shards(): near_k = lax.ppermute(rim_keep, 'tile', beside)  11.1 us
    ppermute x1, waiting for transfers between devices, shards(): rim_k = lax.ppermute(rim_of(near_k, hop_k, depth), 'tile', beside)  10.2 us
    pallas_call x1, Pallas kernels, shards(): pl.pallas_call(wave_kernel, out_shape=[piece] * 4 + [jax.ShapeDtypeStruct...  9.04 us
    ppermute x4, starting transfers between devices, shards(): probe_grad = probe_grad + lax.ppermute(probe_grad, 'tile', pairs)  8.39 us
    ppermute x1, waiting for transfers between devices, shards(): hop_k = lax.ppermute(far_k, 'tile', hop)  6.25 us
    ppermute x1, waiting for transfers between devices, shards(): near_g = lax.ppermute(rim_back, 'tile', beside)  6.02 us
  transfers between devices with their start and end apart: 19, of which 12 were waited for; matrix products, arithmetic and copies ran while one was open for 2% of the time, Pallas kernels for 0%

profile of v2, /device:TPU:0, one launch (start us, length us, event | category | flops | bytes accessed | tf_op | source)
XLA Modules:
  0.0 122.2 jit_solution(5890299919651079438)
XLA Ops:
  0.6 0.7 pad_add_fusion
  1.3 0.6 collective-permute-start.1
  2.0 5.7 %collective-permute-start = (s32[2,8]{1,0:T(2,128)S(1)}, s32[2,8]{1,0:T(2,128)S(1)}, u32[]{:S(2)}, u32[]{:S(2)}) collective-permute-start(s32[2,8]{1,0:T(2,128)S(1)} %pad_add_fusion), channel_id=1, source_target_pairs={{0,1},{1,0},{2,3},{3,2},{4,5},{5,4},{6,7},{7,6},{8,9},{9,8},{10,11... | collective-permute-start | bytes 200 | tf_op jit(solution)/shard_map/ppermute | solution.py:240
  7.7 0.0 collective-permute-done.1.far_place
  7.7 1.5 %collective-permute-done.near_place = s32[2,8]{1,0:T(2,128)S(1)} collective-permute-done((s32[2,8]{1,0:T(2,128)S(1)}, s32[2,8]{1,0:T(2,128)S(1)}, u32[]{:S(2)}, u32[]{:S(2)}) %collective-permute-start) | collective-permute-done | bytes 96 | tf_op jit(solution)/shard_map/ppermute | solution.py:240
  9.3 1.6 %copy-done = f32[2,2,64,2048]{3,2,1,0:T(8,128)S(1)} copy-done((f32[2,2,64,2048]{3,2,1,0:T(8,128)S(1)}, f32[2,2,64,2048]{3,2,1,0:T(8,128)}, u32[]{:S(2)}) %copy-start) | copy-done | bytes 2097176
  10.9 0.7 copy-done.7
  11.5 2.5 %gather.1 = (f32[4,4,64,128]{3,2,1,0:T(8,128)S(1)}, f32[4,4,64,128]{3,2,1,0:T(8,128)S(1)}, f32[4,4,64,128]{3,2,1,0:T(8,128)S(1)}, f32[4,4,64,128]{3,2,1,0:T(8,12...) custom-call(s32[8]{0:T(128)S(1)} %copy-done.7, s32[2,8]{1,0:T(2,128)S(1)} %collective-permute-done.near_place, ...), custom_call_target="tpu_custom_call" | custom-call | tf_op jit(solution)/shard_map/gather/pallas_call | solution.py:245
  14.0 0.8 copy-done.11
  14.8 0.8 copy-done.12
  15.7 0.0 copy-start.5
  15.7 0.0 copy-start.6
  15.7 0.0 copy-start.8
  15.7 0.0 copy-start.9
  15.7 0.0 copy-start.10
  15.7 1.4 %collective-permute-start.4 = (f32[4,4,64,128]{3,2,1,0:T(8,128)}, f32[4,4,64,128]{3,2,1,0:T(8,128)}, u32[]{:S(2)}, u32[]{:S(2)}) collective-permute-start(f32[4,4,64,128]{3,2,1,0:T(8,128)} %get-tuple-element.17), channel_id=1, source_target_pairs={{1,3},{2,0},{3,5},{4,2},{5,7},{6,4},{7,9},{8,6},{9,11},{10,8},{11,... | collective-permute-start | bytes 1572872 | tf_op jit(solution)/shard_map/ppermute | solution.py:263
  17.2 0.1 sub.24
  17.3 1.3 %collective-permute-start.2 = (f32[4,4,64,128]{3,2,1,0:T(8,128)}, f32[4,4,64,128]{3,2,1,0:T(8,128)S(1)}, u32[]{:S(2)}, u32[]{:S(2)}) collective-permute-start(f32[4,4,64,128]{3,2,1,0:T(8,128)} %copy-done.12), channel_id=1, source_target_pairs={{1,3},{2,0},{3,5},{4,2},{5,7},{6,4},{7,9},{8,6},{9,11},{10,8},{11,... | collective-permute-start | bytes 1572872 | tf_op jit(solution)/shard_map/ppermute | solution.py:264
  18.6 0.2 dynamic-slice_reduce_fusion
  18.8 14.1 %collective-permute-done.4 = f32[4,4,64,128]{3,2,1,0:T(8,128)} collective-permute-done((f32[4,4,64,128]{3,2,1,0:T(8,128)}, f32[4,4,64,128]{3,2,1,0:T(8,128)}, u32[]{:S(2)}, u32[]{:S(2)}) %collective-permute-start.4) | collective-permute-done | bytes 524320 | tf_op jit(solution)/shard_map/ppermute | solution.py:263
  32.9 1.2 fusion.3
  34.1 1.3 %collective-permute-start.5 = (f32[4,4,64,128]{3,2,1,0:T(8,128)S(1)}, f32[4,4,64,128]{3,2,1,0:T(8,128)S(1)}, u32[]{:S(2)}, u32[]{:S(2)}) collective-permute-start(f32[4,4,64,128]{3,2,1,0:T(8,128)S(1)} %fusion.3), channel_id=1, source_target_pairs={{0,1},{1,0},{2,3},{3,2},{4,5},{5,4},{6,7},{7,6},{8,9},{9,8},{10,11... | collective-permute-start | bytes 1572872 | tf_op jit(solution)/shard_map/ppermute | solution.py:266
  35.4 0.0 collective-permute-start.7
  35.5 6.2 %collective-permute-done.2 = f32[4,4,64,128]{3,2,1,0:T(8,128)S(1)} collective-permute-done((f32[4,4,64,128]{3,2,1,0:T(8,128)}, f32[4,4,64,128]{3,2,1,0:T(8,128)S(1)}, u32[]{:S(2)}, u32[]{:S(2)}) %collective-permute-start.2) | collective-permute-done | bytes 524320 | tf_op jit(solution)/shard_map/ppermute | solution.py:264
  41.7 0.1 fusion.1
  41.8 1.5 %collective-permute-start.3 = (f32[4,4,64,128]{3,2,1,0:T(8,128)S(1)}, f32[4,4,64,128]{3,2,1,0:T(8,128)S(1)}, u32[]{:S(2)}, u32[]{:S(2)}) collective-permute-start(f32[4,4,64,128]{3,2,1,0:T(8,128)S(1)} %fusion.1), channel_id=1, source_target_pairs={{0,1},{1,0},{2,3},{3,2},{4,5},{5,4},{6,7},{7,6},{8,9},{9,8},{10,11... | collective-permute-start | bytes 1572872 | tf_op jit(solution)/shard_map/ppermute | solution.py:267
  43.3 1.2 collective-permute-done.5
  44.5 0.0 collective-permute-start.6
  44.5 0.0 collective-permute-done.7.got_own
  44.5 10.2 %collective-permute-done.3.keep_rim = f32[4,4,64,128]{3,2,1,0:T(8,128)S(1)} collective-permute-done((f32[4,4,64,128]{3,2,1,0:T(8,128)S(1)}, f32[4,4,64,128]{3,2,1,0:T(8,128)S(1)}, u32[]{:S(2)}, u32[]{:S(2)}) %collective-permute-start.3) | collective-permute-done | bytes 524320 | tf_op jit(solution)/shard_map/ppermute | solution.py:267
  54.6 0.0 collective-permute-done.6.got_rim
  54.6 0.0 copy-done.1
  54.7 0.0 copy-done.2
  54.7 0.0 copy-done.3
  54.7 0.0 copy-done.4
  54.7 0.0 copy-done.5
  54.7 0.0 copy-done.6
  54.7 0.0 copy-done.8
  54.7 0.0 copy-done.9
  54.7 9.0 %waves.1 = (f32[4,4,64,128]{3,2,1,0:T(8,128)S(1)}, f32[4,4,64,128]{3,2,1,0:T(8,128)S(1)}, f32[4,4,64,128]{3,2,1,0:T(8,128)S(1)}, f32[4,4,64,128]{3,2,1,0:T(8,128)S(1)}, f32[2,128,128]{2,1,0:T(8,128)S(1)}) custom-call(s32[8]{0:T(128)S(1)} %copy-done.9, s32[8]{0:T(128)S(1)} %copy-done.8, s32[16]{0:T(128)S(1)} %copy-done.10, f32[2,128,128]{2,1,0:T(8,128)S(1)} %copy-done.6, ...), custom_call_target="tpu_custom_call" | custom-call | tf_op jit(solution)/shard_map/waves/pallas_call | solution.py:272
  63.8 0.1 collective-permute-start.10
  63.9 1.3 %collective-permute-start.9 = (f32[4,4,64,128]{3,2,1,0:T(8,128)S(1)}, f32[4,4,64,128]{3,2,1,0:T(8,128)S(1)}, u32[]{:S(2)}, u32[]{:S(2)}) collective-permute-start(f32[4,4,64,128]{3,2,1,0:T(8,128)S(1)} %get-tuple-element.21), channel_id=1, source_target_pairs={{0,1},{1,0},{2,3},{3,2},{4,5},{5,4},{6,7},{7,6},{8,9},{9,8},{10,11... | collective-permute-start | bytes 1572872 | tf_op jit(solution)/shard_map/ppermute | solution.py:284
  65.2 0.5 collective-permute-done.10
  65.8 1.3 %collective-permute-start.11 = (f32[4,4,64,128]{3,2,1,0:T(8,128)S(1)}, f32[4,4,64,128]{3,2,1,0:T(8,128)S(1)}, u32[]{:S(2)}, u32[]{:S(2)}) collective-permute-start(f32[4,4,64,128]{3,2,1,0:T(8,128)S(1)} %collective-permute-done.10), channel_id=1, source_target_pairs={{0,1},{1,0},{2,3},{3,2},{4,5},{5,4},{6,7},{7,6},{8,9},{9,8},{10,11... | collective-permute-start | bytes 1572872 | tf_op jit(solution)/shard_map/ppermute | solution.py:285
  67.0 0.0 collective-permute-start.14
  67.0 0.5 collective-permute-start.8
  67.6 11.1 %collective-permute-done.9.near_k = f32[4,4,64,128]{3,2,1,0:T(8,128)S(1)} collective-permute-done((f32[4,4,64,128]{3,2,1,0:T(8,128)S(1)}, f32[4,4,64,128]{3,2,1,0:T(8,128)S(1)}, u32[]{:S(2)}, u32[]{:S(2)}) %collective-permute-start.9) | collective-permute-done | bytes 524320 | tf_op jit(solution)/shard_map/ppermute | solution.py:284
  78.6 4.8 %collective-permute-start.12 = (f32[4,4,64,128]{3,2,1,0:T(8,128)S(1)}, f32[4,4,64,128]{3,2,1,0:T(8,128)S(1)}, u32[]{:S(2)}, u32[]{:S(2)}) collective-permute-start(f32[4,4,64,128]{3,2,1,0:T(8,128)S(1)} %collective-permute-done.9.near_k), channel_id=1, source_target_pairs={{3,1},{0,2},{5,3},{2,4},{7,5},{4,6},{9,7},{6,8},{11,9},{8,10},{13,... | collective-permute-start | bytes 1572872 | tf_op jit(solution)/shard_map/ppermute | solution.py:286
  83.4 6.0 %collective-permute-done.11.near_g = f32[4,4,64,128]{3,2,1,0:T(8,128)S(1)} collective-permute-done((f32[4,4,64,128]{3,2,1,0:T(8,128)S(1)}, f32[4,4,64,128]{3,2,1,0:T(8,128)S(1)}, u32[]{:S(2)}, u32[]{:S(2)}) %collective-permute-start.11) | collective-permute-done | bytes 524320 | tf_op jit(solution)/shard_map/ppermute | solution.py:285
  89.4 4.8 %collective-permute-start.13 = (f32[4,4,64,128]{3,2,1,0:T(8,128)S(1)}, f32[4,4,64,128]{3,2,1,0:T(8,128)S(1)}, u32[]{:S(2)}, u32[]{:S(2)}) collective-permute-start(f32[4,4,64,128]{3,2,1,0:T(8,128)S(1)} %collective-permute-done.11.near_g), channel_id=1, source_target_pairs={{3,1},{0,2},{5,3},{2,4},{7,5},{4,6},{9,7},{6,8},{11,9},{8,10},{13,... | collective-permute-start | bytes 1572872 | tf_op jit(solution)/shard_map/ppermute | solution.py:287
  94.2 0.0 collective-permute-done.14
  94.2 0.1 collective-permute-start.15
  94.3 4.3 %collective-permute-done.15 = f32[2,64,128]{2,1,0:T(8,128)S(1)} collective-permute-done((f32[2,64,128]{2,1,0:T(8,128)S(1)}, f32[2,64,128]{2,1,0:T(8,128)S(1)}, u32[]{:S(2)}, u32[]{:S(2)}) %collective-permute-start.15) | collective-permute-done | bytes 65568 | tf_op jit(solution)/shard_map/ppermute | solution.py:295
  98.6 1.7 %collective-permute-start.16 = (f32[2,64,128]{2,1,0:T(8,128)S(1)}, f32[2,64,128]{2,1,0:T(8,128)S(1)}, u32[]{:S(2)}, u32[]{:S(2)}) collective-permute-start(f32[2,64,128]{2,1,0:T(8,128)S(1)} %add.39), channel_id=1, source_target_pairs={{0,2},{1,3},{2,0},{3,1},{4,6},{5,7},{6,4},{7,5},{8,10},{9,11},{10,... | collective-permute-start | bytes 196616 | tf_op jit(solution)/shard_map/ppermute | solution.py:295
  100.2 6.3 %collective-permute-done.16 = f32[2,64,128]{2,1,0:T(8,128)S(1)} collective-permute-done((f32[2,64,128]{2,1,0:T(8,128)S(1)}, f32[2,64,128]{2,1,0:T(8,128)S(1)}, u32[]{:S(2)}, u32[]{:S(2)}) %collective-permute-start.16) | collective-permute-done | bytes 65568 | tf_op jit(solution)/shard_map/ppermute | solution.py:295
  106.6 3.6 %collective-permute-start.17 = (f32[2,64,128]{2,1,0:T(8,128)S(1)}, f32[2,64,128]{2,1,0:T(8,128)S(1)}, u32[]{:S(2)}, u32[]{:S(2)}) collective-permute-start(f32[2,64,128]{2,1,0:T(8,128)S(1)} %add.40), channel_id=1, source_target_pairs={{0,4},{1,5},{2,6},{3,7},{4,0},{5,1},{6,2},{7,3},{8,12},{9,13},{10,... | collective-permute-start | bytes 196616 | tf_op jit(solution)/shard_map/ppermute | solution.py:295
  110.2 2.3 %collective-permute-done.17 = f32[2,64,128]{2,1,0:T(8,128)S(1)} collective-permute-done((f32[2,64,128]{2,1,0:T(8,128)S(1)}, f32[2,64,128]{2,1,0:T(8,128)S(1)}, u32[]{:S(2)}, u32[]{:S(2)}) %collective-permute-start.17) | collective-permute-done | bytes 65568 | tf_op jit(solution)/shard_map/ppermute | solution.py:295
  112.5 3.1 %collective-permute-start.18 = (f32[2,64,128]{2,1,0:T(8,128)S(1)}, f32[2,64,128]{2,1,0:T(8,128)S(1)}, u32[]{:S(2)}, u32[]{:S(2)}) collective-permute-start(f32[2,64,128]{2,1,0:T(8,128)S(1)} %add.41), channel_id=1, source_target_pairs={{0,8},{1,9},{2,10},{3,11},{4,12},{5,13},{6,14},{7,15},{8,0},{9,1},... | collective-permute-start | bytes 196616 | tf_op jit(solution)/shard_map/ppermute | solution.py:295
  115.5 2.2 %collective-permute-done.18 = f32[2,64,128]{2,1,0:T(8,128)S(1)} collective-permute-done((f32[2,64,128]{2,1,0:T(8,128)S(1)}, f32[2,64,128]{2,1,0:T(8,128)S(1)}, u32[]{:S(2)}, u32[]{:S(2)}) %collective-permute-start.18) | collective-permute-done | bytes 65568 | tf_op jit(solution)/shard_map/ppermute | solution.py:295
  117.8 0.6 add.42
  118.4 0.0 collective-permute-done.8.own_g
  118.4 0.0 collective-permute-done.12.far_k
  118.4 0.0 collective-permute-done.13.far_g
  118.4 3.8 %scatter.1 = f32[4,64,2048]{2,1,0:T(8,128)} custom-call(s32[8]{0:T(128)S(1)} %copy-done.8, s32[2,8]{1,0:T(2,128)S(1)} %collective-permute-done.near_place, s32[2,8]{1,0:T(2,128)S(1)} %collective-permute-done.1.far_place, f32[4,4,64,128]{3,2,1,0:T(8,128)S(1)} %get-tuple-element.19.own_k, f32[4,4,64,128]{3,2,1,0:T(8,128)S(1)} %collective-permute-done.8.own_g, ...), custom_call_target="tpu_custom_call" | custom-call | tf_op jit(solution)/shard_map/scatter/pallas_call | solution.py:298
  (15 shorter events, 0.1 us)
Async XLA Ops:
  1.3 6.4 %collective-permute-start.1 = (s32[2,8]{1,0:T(2,128)S(1)}, s32[2,8]{1,0:T(2,128)S(1)}, u32[]{:S(2)}, u32[]{:S(2)}) collective-permute-start(s32[2,8]{1,0:T(2,128)S(1)} %pad_add_fusion), channel_id=1, source_target_pairs={{1,2},{2,1},{3,4},{4,3},{5,6},{6,5},{7,8},{8,7},{9,10},{10,9},{11,... | collective-permute-start | bytes 200 | tf_op jit(solution)/shard_map/ppermute | solution.py:241
  2.0 7.3 %collective-permute-start = (s32[2,8]{1,0:T(2,128)S(1)}, s32[2,8]{1,0:T(2,128)S(1)}, u32[]{:S(2)}, u32[]{:S(2)}) collective-permute-start(s32[2,8]{1,0:T(2,128)S(1)} %pad_add_fusion), channel_id=1, source_target_pairs={{0,1},{1,0},{2,3},{3,2},{4,5},{5,4},{6,7},{7,6},{8,9},{9,8},{10,11... | collective-permute-start | bytes 200 | tf_op jit(solution)/shard_map/ppermute | solution.py:240
  9.3 1.6 %copy-start = (f32[2,2,64,2048]{3,2,1,0:T(8,128)S(1)}, f32[2,2,64,2048]{3,2,1,0:T(8,128)}, u32[]{:S(2)}) copy-start(f32[2,2,64,2048]{3,2,1,0:T(8,128)} %param.10) | copy-start | bytes 6291460
  10.9 0.7 copy-start.7
  14.0 0.8 copy-start.11
  14.8 0.8 copy-start.12
  15.6 39.0 %copy-start.1 = (f32[8,128,128]{2,1,0:T(8,128)S(1)}, f32[8,128,128]{2,1,0:T(8,128)}, u32[]{:S(2)}) copy-start(f32[8,128,128]{2,1,0:T(8,128)} %diff.1) | copy-start | bytes 1572868
  15.6 39.0 %copy-start.2 = (bf16[2,256,256]{2,1,0:T(8,128)(2,1)S(1)}, bf16[2,256,256]{2,1,0:T(8,128)(2,1)}, u32[]{:S(2)}) copy-start(bf16[2,256,256]{2,1,0:T(8,128)(2,1)} %constant.53.clone.f_left) | copy-start | bytes 786436
  15.6 39.0 %copy-start.3 = (bf16[2,256,256]{2,1,0:T(8,128)(2,1)S(1)}, bf16[2,256,256]{2,1,0:T(8,128)(2,1)}, u32[]{:S(2)}) copy-start(bf16[2,256,256]{2,1,0:T(8,128)(2,1)} %constant.52.clone.f_right) | copy-start | bytes 786436
  15.6 39.0 %copy-start.4 = (bf16[2,256,256]{2,1,0:T(8,128)(2,1)S(1)}, bf16[2,256,256]{2,1,0:T(8,128)(2,1)}, u32[]{:S(2)}) copy-start(bf16[2,256,256]{2,1,0:T(8,128)(2,1)} %constant.51.clone.a_left) | copy-start | bytes 786436
  15.7 39.0 %copy-start.5 = (bf16[2,256,256]{2,1,0:T(8,128)(2,1)S(1)}, bf16[2,256,256]{2,1,0:T(8,128)(2,1)}, u32[]{:S(2)}) copy-start(bf16[2,256,256]{2,1,0:T(8,128)(2,1)} %constant.50.clone.a_right) | copy-start | bytes 786436
  15.7 39.0 %copy-start.6 = (f32[2,128,128]{2,1,0:T(8,128)S(1)}, f32[2,128,128]{2,1,0:T(8,128)}, u32[]{:S(2)}) copy-start(f32[2,128,128]{2,1,0:T(8,128)} %probe.1) | copy-start | bytes 393220
  15.7 39.0 %copy-start.8 = (s32[8]{0:T(128)S(1)}, s32[8]{0:T(128)}, u32[]{:S(2)}) copy-start(s32[8]{0:T(128)} %own_cols.5) | copy-start | bytes 100
  15.7 39.0 %copy-start.9 = (s32[8]{0:T(128)S(1)}, s32[8]{0:T(128)}, u32[]{:S(2)}) copy-start(s32[8]{0:T(128)} %own_rows.1) | copy-start | bytes 100
  15.7 39.0 %copy-start.10 = (s32[16]{0:T(128)S(1)}, s32[16]{0:T(128)}, u32[]{:S(2)}) copy-start(s32[16]{0:T(128)} %counts.1) | copy-start | bytes 196
  15.7 17.2 %collective-permute-start.4 = (f32[4,4,64,128]{3,2,1,0:T(8,128)}, f32[4,4,64,128]{3,2,1,0:T(8,128)}, u32[]{:S(2)}, u32[]{:S(2)}) collective-permute-start(f32[4,4,64,128]{3,2,1,0:T(8,128)} %get-tuple-element.17), channel_id=1, source_target_pairs={{1,3},{2,0},{3,5},{4,2},{5,7},{6,4},{7,9},{8,6},{9,11},{10,8},{11,... | collective-permute-start | bytes 1572872 | tf_op jit(solution)/shard_map/ppermute | solution.py:263
  17.3 24.4 %collective-permute-start.2 = (f32[4,4,64,128]{3,2,1,0:T(8,128)}, f32[4,4,64,128]{3,2,1,0:T(8,128)S(1)}, u32[]{:S(2)}, u32[]{:S(2)}) collective-permute-start(f32[4,4,64,128]{3,2,1,0:T(8,128)} %copy-done.12), channel_id=1, source_target_pairs={{1,3},{2,0},{3,5},{4,2},{5,7},{6,4},{7,9},{8,6},{9,11},{10,8},{11,... | collective-permute-start | bytes 1572872 | tf_op jit(solution)/shard_map/ppermute | solution.py:264
  34.1 10.4 %collective-permute-start.5 = (f32[4,4,64,128]{3,2,1,0:T(8,128)S(1)}, f32[4,4,64,128]{3,2,1,0:T(8,128)S(1)}, u32[]{:S(2)}, u32[]{:S(2)}) collective-permute-start(f32[4,4,64,128]{3,2,1,0:T(8,128)S(1)} %fusion.3), channel_id=1, source_target_pairs={{0,1},{1,0},{2,3},{3,2},{4,5},{5,4},{6,7},{7,6},{8,9},{9,8},{10,11... | collective-permute-start | bytes 1572872 | tf_op jit(solution)/shard_map/ppermute | solution.py:266
  35.4 9.0 %collective-permute-start.7 = (f32[4,4,64,128]{3,2,1,0:T(8,128)}, f32[4,4,64,128]{3,2,1,0:T(8,128)S(1)}, u32[]{:S(2)}, u32[]{:S(2)}) collective-permute-start(f32[4,4,64,128]{3,2,1,0:T(8,128)} %copy-done.11), channel_id=1, source_target_pairs={{0,16},{16,0},{1,17},{17,1},{2,18},{18,2},{3,19},{19,3},{4,20},{20... | collective-permute-start | bytes 1572872 | tf_op jit(solution)/shard_map/ppermute | solution.py:265
  41.8 12.8 %collective-permute-start.3 = (f32[4,4,64,128]{3,2,1,0:T(8,128)S(1)}, f32[4,4,64,128]{3,2,1,0:T(8,128)S(1)}, u32[]{:S(2)}, u32[]{:S(2)}) collective-permute-start(f32[4,4,64,128]{3,2,1,0:T(8,128)S(1)} %fusion.1), channel_id=1, source_target_pairs={{0,1},{1,0},{2,3},{3,2},{4,5},{5,4},{6,7},{7,6},{8,9},{9,8},{10,11... | collective-permute-start | bytes 1572872 | tf_op jit(solution)/shard_map/ppermute | solution.py:267
  44.5 10.2 %collective-permute-start.6 = (f32[4,4,64,128]{3,2,1,0:T(8,128)S(1)}, f32[4,4,64,128]{3,2,1,0:T(8,128)S(1)}, u32[]{:S(2)}, u32[]{:S(2)}) collective-permute-start(f32[4,4,64,128]{3,2,1,0:T(8,128)S(1)} %collective-permute-done.5), channel_id=1, source_target_pairs={{0,16},{16,0},{1,17},{17,1},{2,18},{18,2},{3,19},{19,3},{4,20},{20... | collective-permute-start | bytes 1572872 | tf_op jit(solution)/shard_map/ppermute | solution.py:268
  63.8 2.0 %collective-permute-start.10 = (f32[4,4,64,128]{3,2,1,0:T(8,128)S(1)}, f32[4,4,64,128]{3,2,1,0:T(8,128)S(1)}, u32[]{:S(2)}, u32[]{:S(2)}) collective-permute-start(f32[4,4,64,128]{3,2,1,0:T(8,128)S(1)} %get-tuple-element.22), channel_id=1, source_target_pairs={{0,16},{16,0},{1,17},{17,1},{2,18},{18,2},{3,19},{19,3},{4,20},{20... | collective-permute-start | bytes 1572872 | tf_op jit(solution)/shard_map/ppermute | solution.py:282
  63.9 14.8 %collective-permute-start.9 = (f32[4,4,64,128]{3,2,1,0:T(8,128)S(1)}, f32[4,4,64,128]{3,2,1,0:T(8,128)S(1)}, u32[]{:S(2)}, u32[]{:S(2)}) collective-permute-start(f32[4,4,64,128]{3,2,1,0:T(8,128)S(1)} %get-tuple-element.21), channel_id=1, source_target_pairs={{0,1},{1,0},{2,3},{3,2},{4,5},{5,4},{6,7},{7,6},{8,9},{9,8},{10,11... | collective-permute-start | bytes 1572872 | tf_op jit(solution)/shard_map/ppermute | solution.py:284
  65.8 23.7 %collective-permute-start.11 = (f32[4,4,64,128]{3,2,1,0:T(8,128)S(1)}, f32[4,4,64,128]{3,2,1,0:T(8,128)S(1)}, u32[]{:S(2)}, u32[]{:S(2)}) collective-permute-start(f32[4,4,64,128]{3,2,1,0:T(8,128)S(1)} %collective-permute-done.10), channel_id=1, source_target_pairs={{0,1},{1,0},{2,3},{3,2},{4,5},{5,4},{6,7},{7,6},{8,9},{9,8},{10,11... | collective-permute-start | bytes 1572872 | tf_op jit(solution)/shard_map/ppermute | solution.py:285
  67.0 27.2 %collective-permute-start.14 = (f32[2,64,128]{2,1,0:T(8,128)S(1)}, f32[2,64,128]{2,1,0:T(8,128)S(1)}, u32[]{:S(2)}, u32[]{:S(2)}) collective-permute-start(f32[2,64,128]{2,1,0:T(8,128)S(1)} %dynamic-slice_bitcast_fusion), channel_id=1, source_target_pairs={{0,16},{16,0},{1,17},{17,1},{2,18},{18,2},{3,19},{19,3},{4,20},{20... | collective-permute-start | bytes 196616 | tf_op jit(solution)/shard_map/ppermute | solution.py:291
  67.0 51.4 %collective-permute-start.8 = (f32[4,4,64,128]{3,2,1,0:T(8,128)S(1)}, f32[4,4,64,128]{3,2,1,0:T(8,128)S(1)}, u32[]{:S(2)}, u32[]{:S(2)}) collective-permute-start(f32[4,4,64,128]{3,2,1,0:T(8,128)S(1)} %get-tuple-element.20), channel_id=1, source_target_pairs={{0,16},{16,0},{1,17},{17,1},{2,18},{18,2},{3,19},{19,3},{4,20},{20... | collective-permute-start | bytes 1572872 | tf_op jit(solution)/shard_map/ppermute | solution.py:283
  78.6 39.8 %collective-permute-start.12 = (f32[4,4,64,128]{3,2,1,0:T(8,128)S(1)}, f32[4,4,64,128]{3,2,1,0:T(8,128)S(1)}, u32[]{:S(2)}, u32[]{:S(2)}) collective-permute-start(f32[4,4,64,128]{3,2,1,0:T(8,128)S(1)} %collective-permute-done.9.near_k), channel_id=1, source_target_pairs={{3,1},{0,2},{5,3},{2,4},{7,5},{4,6},{9,7},{6,8},{11,9},{8,10},{13,... | collective-permute-start | bytes 1572872 | tf_op jit(solution)/shard_map/ppermute | solution.py:286
  89.4 29.0 %collective-permute-start.13 = (f32[4,4,64,128]{3,2,1,0:T(8,128)S(1)}, f32[4,4,64,128]{3,2,1,0:T(8,128)S(1)}, u32[]{:S(2)}, u32[]{:S(2)}) collective-permute-start(f32[4,4,64,128]{3,2,1,0:T(8,128)S(1)} %collective-permute-done.11.near_g), channel_id=1, source_target_pairs={{3,1},{0,2},{5,3},{2,4},{7,5},{4,6},{9,7},{6,8},{11,9},{8,10},{13,... | collective-permute-start | bytes 1572872 | tf_op jit(solution)/shard_map/ppermute | solution.py:287
  94.2 4.3 %collective-permute-start.15 = (f32[2,64,128]{2,1,0:T(8,128)S(1)}, f32[2,64,128]{2,1,0:T(8,128)S(1)}, u32[]{:S(2)}, u32[]{:S(2)}) collective-permute-start(f32[2,64,128]{2,1,0:T(8,128)S(1)} %bitcast_add_fusion), channel_id=1, source_target_pairs={{0,1},{1,0},{2,3},{3,2},{4,5},{5,4},{6,7},{7,6},{8,9},{9,8},{10,11... | collective-permute-start | bytes 196616 | tf_op jit(solution)/shard_map/ppermute | solution.py:295
  98.6 8.0 %collective-permute-start.16 = (f32[2,64,128]{2,1,0:T(8,128)S(1)}, f32[2,64,128]{2,1,0:T(8,128)S(1)}, u32[]{:S(2)}, u32[]{:S(2)}) collective-permute-start(f32[2,64,128]{2,1,0:T(8,128)S(1)} %add.39), channel_id=1, source_target_pairs={{0,2},{1,3},{2,0},{3,1},{4,6},{5,7},{6,4},{7,5},{8,10},{9,11},{10,... | collective-permute-start | bytes 196616 | tf_op jit(solution)/shard_map/ppermute | solution.py:295
  106.6 5.9 %collective-permute-start.17 = (f32[2,64,128]{2,1,0:T(8,128)S(1)}, f32[2,64,128]{2,1,0:T(8,128)S(1)}, u32[]{:S(2)}, u32[]{:S(2)}) collective-permute-start(f32[2,64,128]{2,1,0:T(8,128)S(1)} %add.40), channel_id=1, source_target_pairs={{0,4},{1,5},{2,6},{3,7},{4,0},{5,1},{6,2},{7,3},{8,12},{9,13},{10,... | collective-permute-start | bytes 196616 | tf_op jit(solution)/shard_map/ppermute | solution.py:295
  112.5 5.3 %collective-permute-start.18 = (f32[2,64,128]{2,1,0:T(8,128)S(1)}, f32[2,64,128]{2,1,0:T(8,128)S(1)}, u32[]{:S(2)}, u32[]{:S(2)}) collective-permute-start(f32[2,64,128]{2,1,0:T(8,128)S(1)} %add.41), channel_id=1, source_target_pairs={{0,8},{1,9},{2,10},{3,11},{4,12},{5,13},{6,14},{7,15},{8,0},{9,1},... | collective-permute-start | bytes 196616 | tf_op jit(solution)/shard_map/ppermute | solution.py:295

commit v3 on v2

v3 whole, which is shorter than its diff:
```python
import math

import jax
import jax.numpy as jnp
import ml_dtypes
import numpy as np
from jax import lax
from jax.experimental import pallas as pl
from jax.experimental.pallas import tpu as pltpu
from jax.sharding import PartitionSpec as P

FRESNEL = 0.5
LANES = 128


def split_table(table):
    head = table.astype(np.float32).astype(ml_dtypes.bfloat16)
    tail = (table - head.astype(np.float64)).astype(np.float32).astype(ml_dtypes.bfloat16)
    return np.stack([head, tail])


def tables(size):
    index = np.arange(size)
    dft = np.exp(-2j * math.pi / size * (index[:, None] * index[None, :] % size)) / math.sqrt(size)
    freq = (index + size // 2) % size - size // 2
    phase = np.exp(-1j * FRESNEL * math.pi / size * freq.astype(np.float64) ** 2)
    prop = dft.conj() @ (phase[:, None] * dft)
    prop = 0.5 * (prop + prop.T)
    out = []
    for m in (prop, dft):
        right = np.block([[m.real, m.imag], [-m.imag, m.real]])
        out += [split_table(right), split_table(right.T)]
    return out


def halves(x):
    head = x.astype(jnp.bfloat16)
    tail = (x - head.astype(jnp.float32)).astype(jnp.bfloat16)
    return head, tail


def dot(a, b):
    return jnp.dot(a, b, preferred_element_type=jnp.float32)


def two_sided(re, im, right, left, slots, size):
    head, tail = halves(jnp.concatenate([re, im], axis=1))
    y = dot(head, right[0]) + dot(tail, right[0]) + dot(head, right[1])
    z = jnp.concatenate(
        [
            jnp.concatenate(
                [y[j * size : (j + 1) * size, :size], y[j * size : (j + 1) * size, size:]], axis=0
            )
            for j in range(slots)
        ],
        axis=1,
    )
    head, tail = halves(z)
    y = dot(left[0], head) + dot(left[0], tail) + dot(left[1], head)
    out_re = [y[:size, j * size : (j + 1) * size] for j in range(slots)]
    out_im = [y[size:, j * size : (j + 1) * size] for j in range(slots)]
    return jnp.concatenate(out_re, axis=0), jnp.concatenate(out_im, axis=0)


def axis_places():
    depth = lax.axis_index("depth")
    tile = lax.axis_index("tile")
    return depth, tile, lax.rem(tile, 2)


def gather_kernel(own_cols, near_place, far_place, trans, *outs):
    depth, _, _ = axis_places()
    blocks = trans.shape[2] // LANES
    shape = (trans.shape[0], trans.shape[1], LANES)
    lane = lax.broadcasted_iota(jnp.int32, shape, 2)
    for which in range(3):
        for rel in range(2):
            out = outs[2 * which + rel]

            def one(j, carry, which=which, rel=rel, out=out):
                slot = 2 * j + (depth if rel == 0 else 1 - depth)
                col = own_cols[slot] if which == 0 else (near_place, far_place)[which - 1][1, slot]
                block = col // LANES
                after = jnp.minimum(block + 1, blocks - 1)
                x = trans[:, :, pl.ds(pl.multiple_of(block * LANES, LANES), LANES)]
                y = trans[:, :, pl.ds(pl.multiple_of(after * LANES, LANES), LANES)]
                out[j] = jnp.where(lane >= col - block * LANES, x, y)
                return carry

            lax.fori_loop(0, out.shape[0], one, 0)


MESH = pl.DeviceIdType.MESH


def main_kernel(
    own_rows, own_cols, counts, near_place, probe, diff,
    own_k, own_g, near_k, near_g, far_k, far_g, a_right, a_left, f_right, f_left,
    own_k_out, own_g_out, near_k_out, near_g_out, far_k_out, far_g_out, probe_out,
    hopped, merged, rim_in, give_in, rim_back, own_in, rim_grad, own_grad, patch, psi,
    probe_part, probe_got, send_sem, recv_sem,
):
    depth, tile, odd = axis_places()
    tiles = lax.axis_size("tile")
    filled = counts[tile]
    rounds, arrays, half, size = own_k.shape
    group = arrays // 2
    slices = 2 * group
    pair = patch.shape[2] // size

    def flipped(bit):
        return tile + bit - 2 * bit * lax.rem(lax.div(tile, bit), 2)

    other = (1 - depth, tile)
    beside = (depth, flipped(1))
    onward = (depth, lax.rem(tile + 4 * odd - 2 + tiles, tiles))
    backward = (depth, lax.rem(tile - 4 * odd + 2 + tiles, tiles))
    bits = []
    while 2 ** len(bits) < tiles:
        bits.append(2 ** len(bits))
    bits = bits[::-1]

    barrier = pltpu.get_barrier_semaphore()
    greeted = [other, beside, onward, backward] + [(depth, flipped(b)) for b in bits if b > 2]
    for device in greeted:
        pl.semaphore_signal(barrier, inc=1, device_id=device, device_id_type=MESH)
    pl.semaphore_wait(barrier, len(greeted))

    def copy(src, dst, device, sem):
        return pltpu.make_async_remote_copy(
            src_ref=src, dst_ref=dst, send_sem=send_sem.at[sem], recv_sem=recv_sem.at[sem],
            device_id=device, device_id_type=MESH,
        )

    def hop_in(rel, j):
        return copy((far_k, far_g)[rel].at[j], hopped.at[rel, j], onward, rel * rounds + j)

    def cross_in(rel, j):
        dst = give_in.at[j] if rel else rim_in.at[0, j]
        return copy(merged.at[rel, j], dst, beside, (2 + rel) * rounds + j)

    def own_swap(j):
        return copy(own_g.at[j], own_in.at[1, j], other, 4 * rounds + j)

    def rim_swap(j):
        return copy(give_in.at[j], rim_in.at[1, j], other, 5 * rounds + j)

    def own_return(j):
        return copy(own_grad.at[1, j], own_g_out.at[j], other, 6 * rounds + j)

    def rim_return(j):
        return copy(rim_grad.at[1, j], rim_back.at[j], other, 7 * rounds + j)

    def cross_out(rel, j):
        src = rim_back.at[j] if rel else rim_grad.at[0, j]
        return copy(src, (near_k_out, near_g_out)[rel].at[j], beside, (8 + rel) * rounds + j)

    def hop_out(rel, j):
        refs = ((near_k_out, far_k_out), (near_g_out, far_g_out))[rel]
        return copy(refs[0].at[j], refs[1].at[j], backward, (10 + rel) * rounds + j)

    def probe_swap():
        return copy(probe_part.at[1 - depth], probe_got.at[0], other, 12 * rounds)

    def probe_step(i):
        device = (depth, flipped(bits[i]))
        return copy(probe_part.at[2 + i], probe_got.at[1 + i], device, 12 * rounds + 1 + i)

    for j in range(rounds):
        hop_in(1, j).start()
        hop_in(0, j).start()
    for j in range(rounds):
        own_swap(j).start()
    own_in[0] = own_k[...]
    row = lax.broadcasted_iota(jnp.int32, (arrays, half, size), 1)
    near_tile = tile + 1 - 2 * odd

    def merge(j, carry):
        for rel in (1, 0):
            hop_in(rel, j).wait_recv()
            slot = 2 * j + (1 - depth if rel else depth)
            begin = near_place[0, slot] - (near_tile - 1) * half
            near, far = (near_k, near_g)[rel][j], hopped[rel, j]
            near_rows = (row >= begin).astype(jnp.int32) != odd
            merged[rel, j] = jnp.where(near_rows, near, far)
            cross_in(rel, j).start()
        return carry

    lax.fori_loop(0, rounds, merge, 0)

    def pass_on(j, carry):
        cross_in(1, j).wait_recv()
        rim_swap(j).start()
        return carry

    def times(a, b):
        return a[0] * b[0] - a[1] * b[1], a[0] * b[1] + a[1] * b[0]

    def load(ref, s):
        return ref[s, 0], ref[s, 1]

    def apply(wave, right, left):
        return two_sided(wave[0], wave[1], right, left, pair, size)

    def rows(i):
        return slice(i * size, (i + 1) * size)

    def waves(p, carry):
        lax.fori_loop(p * pair, p * pair + pair, pass_on, 0)
        spots = []
        for i in range(pair):
            j = p * pair + i
            slot = 2 * j + depth
            down = own_rows[slot] - (tile - 1) * half
            across = lax.rem(own_cols[slot], LANES)
            spots.append((j, slot, down, across, slot < filled))
            for part in range(2):
                psi[0, part, rows(i), :] = pltpu.roll(pltpu.roll(probe[part], down, 0), across, 1)
        for i in range(pair):
            j = spots[i][0]
            cross_in(0, j).wait_recv()
            own_swap(j).wait_recv()
            rim_swap(j).wait_recv()
            for s in range(slices):
                side = lax.rem(depth + s // group, 2)
                for part in range(2):
                    a = part * group + s % group
                    patch[s, part, i * size : i * size + half, :] = rim_in[side, j, a]
                    patch[s, part, i * size + half : (i + 1) * size, :] = own_in[side, j, a]

        def forward(s, carry):
            wave = apply(times(load(patch, s), load(psi, s)), a_right, a_left)
            psi[s + 1, 0] = wave[0]
            psi[s + 1, 1] = wave[1]
            return carry

        lax.fori_loop(0, slices - 1, forward, 0)
        far = apply(times(load(patch, slices - 1), load(psi, slices - 1)), f_right, f_left)
        measured = jnp.concatenate([diff[spot[1]] for spot in spots], axis=0)
        misfit = far[0] * far[0] + far[1] * far[1] - measured

        def finish(s, along):
            term = times(load(psi, s), along)
            term = (term[0], -term[1])
            side = lax.rem(depth + lax.div(s, group), 2)
            for i, (j, _, _, _, on) in enumerate(spots):
                for part in range(2):
                    a = part * group + lax.rem(s, group)
                    value = jnp.where(on, term[part][rows(i)], 0.0)
                    rim_grad[side, j, a] = value[:half]
                    own_grad[side, j, a] = value[half:]
            return times(load(patch, s), along)

        back = apply((misfit * far[0], -(misfit * far[1])), f_right, f_left)
        back = finish(jnp.int32(slices - 1), back)

        def reverse(n, back):
            return finish(slices - 2 - n, apply(back, a_right, a_left))

        back = lax.fori_loop(0, slices - 1, reverse, back)
        for i in range(pair):
            j = spots[i][0]
            rim_return(j).start()
            cross_out(0, j).start()
            own_return(j).start()
        for part in range(2):
            total = jnp.zeros((size, size), jnp.float32)
            for i, (_, _, down, across, on) in enumerate(spots):
                value = jnp.where(on, back[part][rows(i)], 0.0)
                value = pltpu.roll(value, lax.rem(size - down, size), 0)
                total = total + pltpu.roll(value, lax.rem(size - across, size), 1)
            total = total if part == 0 else -total
            for side in range(2):
                before = probe_part[side, part]
                probe_part[side, part] = before + total[side * half : (side + 1) * half]
        return carry

    probe_part[0] = jnp.zeros_like(probe_part[0])
    probe_part[1] = jnp.zeros_like(probe_part[1])
    lax.fori_loop(0, rounds // pair, waves, 0)

    probe_swap().start()

    def give(j, carry):
        rim_return(j).wait_recv()
        cross_out(1, j).start()
        return carry

    lax.fori_loop(0, rounds, give, 0)
    probe_swap().wait_recv()
    probe_part[2] = probe_part[depth] + probe_got[0]
    probe_step(0).start()

    done = 0
    for rel, first in ((0, 0), (0, rounds // 2), (1, 0), (1, rounds // 2)):

        def onto(j, carry, rel=rel):
            cross_out(rel, j).wait_recv()
            hop_out(rel, j).start()
            return carry

        lax.fori_loop(first, first + rounds // 2, onto, 0)
        if done < len(bits) - 1:
            probe_step(done).wait_recv()
            probe_part[3 + done] = probe_part[2 + done] + probe_got[1 + done]
            done += 1
            probe_step(done).start()
    while done < len(bits):
        probe_step(done).wait_recv()
        probe_part[3 + done] = probe_part[2 + done] + probe_got[1 + done]
        done += 1
        if done < len(bits):
            probe_step(done).start()
    probe_out[...] = probe_part[2 + len(bits)]
    own_k_out[...] = own_grad[0]

    def drain(j, carry):
        own_return(j).wait_recv()
        for rel in range(2):
            hop_out(rel, j).wait_recv()
            hop_in(rel, j).wait_send()
            cross_out(rel, j).wait_send()
            hop_out(rel, j).wait_send()
            cross_in(rel, j).wait_send()
        own_swap(j).wait_send()
        rim_swap(j).wait_send()
        own_return(j).wait_send()
        rim_return(j).wait_send()
        return carry

    lax.fori_loop(0, rounds, drain, 0)
    probe_swap().wait_send()
    for i in range(len(bits)):
        probe_step(i).wait_send()


def scatter_kernel(own_cols, near_place, far_place, own_k, own_g, near_k, near_g, far_k, far_g, out):
    depth, tile, odd = axis_places()
    blocks = out.shape[2] // LANES
    shape = (out.shape[0], out.shape[1], LANES)
    lane = lax.broadcasted_iota(jnp.int32, shape, 2)
    row = lax.broadcasted_iota(jnp.int32, shape, 1)
    out[...] = jnp.zeros_like(out)
    for index, ref in enumerate((own_k, own_g, near_k, near_g, far_k, far_g)):
        which, rel = index // 2, index % 2

        def one(j, carry, which=which, rel=rel, ref=ref):
            slot = 2 * j + (depth if rel == 0 else 1 - depth)
            value = ref[j]
            col = own_cols[slot] if which == 0 else (near_place, far_place)[which - 1][1, slot]
            if which:
                under = odd if which == 1 else 1 - odd
                place = (near_place, far_place)[which - 1]
                owner = tile + (1 - 2 * odd if which == 1 else 2 * odd - 1)
                start = place[0, slot] - (owner - 1) * shape[1]
                low = jnp.where(under == 1, 0, start)
                high = jnp.where(under == 1, start, shape[1])
                exists = (owner >= 0) & (owner < lax.axis_size("tile"))
                high = jnp.where(exists, high, low)
                value = jnp.where((row >= low) & (row < high), value, 0.0)
            block = col // LANES
            after = jnp.minimum(block + 1, blocks - 1)
            inside = lane >= col - block * LANES
            at = pl.ds(pl.multiple_of(block * LANES, LANES), LANES)
            out[:, :, at] = out[:, :, at] + jnp.where(inside, value, 0.0)
            at = pl.ds(pl.multiple_of(after * LANES, LANES), LANES)
            out[:, :, at] = out[:, :, at] + jnp.where(inside, 0.0, value)
            return carry

        lax.fori_loop(0, ref.shape[0], one, 0)


SMEM = pl.BlockSpec(memory_space=pltpu.SMEM)
VMEM = pl.BlockSpec(memory_space=pltpu.VMEM)
PARAMS = pltpu.CompilerParams(vmem_limit_bytes=48 * 1024 * 1024)


def shards(transmission, probe, scan_rows, scan_cols, tile_counts, diffraction):
    size = probe.shape[-1]
    half = size // 2
    group, strip, cols = transmission.shape[1:]
    rounds = scan_rows.shape[0] // 2
    tiles = lax.axis_size("tile")
    f32 = jnp.float32

    beside = [(c, c ^ 1) for c in range(tiles)]
    across = [(c, c + 1 if c % 2 else c - 1) for c in range(1, tiles - 1)]

    place = jnp.stack([scan_rows, scan_cols])
    place_near = lax.ppermute(place, "tile", beside)
    place_far = lax.ppermute(place, "tile", across)

    flat = transmission.reshape(2 * group, strip, cols)
    piece = jax.ShapeDtypeStruct((rounds, 2 * group, strip, LANES), f32)
    own_k, own_g, near_k, near_g, far_k, far_g = pl.pallas_call(
        gather_kernel,
        out_shape=[piece] * 6,
        in_specs=[SMEM] * 3 + [VMEM],
        out_specs=[VMEM] * 6,
        compiler_params=PARAMS,
        name="gather",
    )(scan_cols, place_near, place_far, flat)

    tabs = [jnp.asarray(t) for t in tables(size)]
    pair = 2
    stages = (tiles - 1).bit_length()
    sems = pltpu.SemaphoreType.DMA((12 * rounds + 1 + stages,))
    both = pltpu.VMEM((2,) + piece.shape, f32)
    single = pltpu.VMEM(piece.shape, f32)
    waves = pltpu.VMEM((2 * group, 2, pair * size, size), f32)
    rows_shape = (probe.shape[0], half, size)
    *parts, probe_grad = pl.pallas_call(
        main_kernel,
        out_shape=[piece] * 6 + [jax.ShapeDtypeStruct(rows_shape, f32)],
        in_specs=[SMEM] * 4 + [VMEM] * 12,
        out_specs=[VMEM] * 7,
        scratch_shapes=[both, both, both, single, single, both, both, both]
        + [waves, waves]
        + [pltpu.VMEM((3 + stages,) + rows_shape, f32), pltpu.VMEM((1 + stages,) + rows_shape, f32)]
        + [sems, sems],
        compiler_params=pltpu.CompilerParams(
            vmem_limit_bytes=48 * 1024 * 1024, collective_id=0, has_side_effects=True
        ),
        name="waves",
    )(
        scan_rows, scan_cols, tile_counts, place_near, probe, diffraction,
        own_k, own_g, near_k, near_g, far_k, far_g, *tabs,
    )

    grads = pl.pallas_call(
        scatter_kernel,
        out_shape=jax.ShapeDtypeStruct(flat.shape, f32),
        in_specs=[SMEM] * 3 + [VMEM] * 6,
        out_specs=VMEM,
        compiler_params=PARAMS,
        name="scatter",
    )(scan_cols, place_near, place_far, *parts)
    return (grads.reshape(transmission.shape), probe_grad)


def solution(mesh):
    placed = (P(None, "depth", "tile", None), P(), P("tile"), P("tile"), P(), P("tile", None, None))
    return jax.shard_map(
        shards,
        mesh=mesh,
        in_specs=placed,
        out_specs=(P(None, "depth", "tile", None), P(None, "depth", None)),
        check_vma=False,
    )
```

time: 123 us -> 109 us (0.89)
  the two profiles are of different devices: /device:TPU:0 before, /device:TPU:8 now
where the time goes in v3:
time: 109 us
  Pallas kernels  93.4 us (86%)
  local copies, waits for them, and re-layouts  6.11 us (6%)
  starting transfers between devices  4.94 us (5%)
  waiting for transfers between devices  2.92 us (3%)
    pallas_call x1, Pallas kernels, shards(): pl.pallas_call(main_kernel, out_shape=[piece] * 6 + [jax.ShapeDtypeStruct...  87.9 us
    unnamed x29, local copies, waits for them, and re-layouts  6.11 us
    ppermute x1, starting transfers between devices, shards(): place_far = lax.ppermute(place, 'tile', across)  4.23 us
    pallas_call x1, Pallas kernels, shards(): pl.pallas_call(scatter_kernel, out_shape=jax.ShapeDtypeStruct(flat.shape,...  3.82 us
    ppermute x1, waiting for transfers between devices, shards(): place_far = lax.ppermute(place, 'tile', across)  2.3 us
  transfers between devices with their start and end apart: 2, of which 2 were waited for; matrix products, arithmetic and copies ran while one was open for 0% of the time, Pallas kernels for 0%

profile of v3, /device:TPU:8, one launch (start us, length us, event | category | flops | bytes accessed | tf_op | source)
XLA Modules:
  0.0 108.8 jit_solution(16859071549850025897)
XLA Ops:
  0.6 0.0 copy-start.12
  0.6 0.0 copy-start.13
  0.6 0.7 pad_add_fusion
  1.4 4.2 %collective-permute-start.1 = (s32[2,8]{1,0:T(2,128)S(1)}, s32[2,8]{1,0:T(2,128)S(1)}, u32[]{:S(2)}, u32[]{:S(2)}) collective-permute-start(s32[2,8]{1,0:T(2,128)S(1)} %pad_add_fusion), channel_id=1, source_target_pairs={{1,2},{2,1},{3,4},{4,3},{5,6},{6,5},{7,8},{8,7},{9,10},{10,9},{11,... | collective-permute-start | bytes 200 | tf_op jit(solution)/shard_map/ppermute | solution.py:391
  5.6 0.7 collective-permute-start
  6.3 2.3 %collective-permute-done.1.far_place = s32[2,8]{1,0:T(2,128)S(1)} collective-permute-done((s32[2,8]{1,0:T(2,128)S(1)}, s32[2,8]{1,0:T(2,128)S(1)}, u32[]{:S(2)}, u32[]{:S(2)}) %collective-permute-start.1) | collective-permute-done | bytes 96 | tf_op jit(solution)/shard_map/ppermute | solution.py:391
  8.6 0.6 collective-permute-done.near_place
  9.2 0.0 copy-start
  9.2 1.6 %copy-done = f32[2,2,64,2048]{3,2,1,0:T(8,128)S(1)} copy-done((f32[2,2,64,2048]{3,2,1,0:T(8,128)S(1)}, f32[2,2,64,2048]{3,2,1,0:T(8,128)}, u32[]{:S(2)}) %copy-start) | copy-done | bytes 2097176
  10.8 0.0 copy-start.11
  10.8 0.7 copy-done.11
  11.5 0.0 copy-start.1
  11.5 0.0 copy-start.6
  11.5 0.0 copy-start.7
  11.5 0.0 copy-start.8
  11.5 0.0 copy-start.9
  11.5 0.0 copy-start.10
  11.5 1.7 %gather.1 = (f32[4,4,64,128]{3,2,1,0:T(8,128)S(1)}, f32[4,4,64,128]{3,2,1,0:T(8,128)S(1)}, f32[4,4,64,128]{3,2,1,0:T(8,128)S(1)}, f32[4,4,64,128]{3,2,1,0:T(8,12...) custom-call(s32[8]{0:T(128)S(1)} %copy-done.11, s32[2,8]{1,0:T(2,128)S(1)} %collective-permute-done.near_place, ...), custom_call_target="tpu_custom_call" | custom-call | tf_op jit(solution)/shard_map/gather/pallas_call | solution.py:395
  13.3 0.0 copy-start.2
  13.3 0.8 copy-done.2
  14.1 0.0 copy-start.3
  14.1 0.8 copy-done.3
  14.9 0.0 copy-start.4
  14.9 0.8 copy-done.4
  15.7 0.0 copy-start.5
  15.7 0.8 copy-done.5
  16.5 0.0 copy-done.12
  16.5 0.0 copy-done.13
  16.5 0.0 copy-done.1
  16.5 0.0 copy-done.6
  16.5 0.0 copy-done.7
  16.5 0.0 copy-done.8
  16.5 0.0 copy-done.9
  16.5 0.0 copy-done.10
  16.5 87.9 %waves.1 = (f32[4,4,64,128]{3,2,1,0:T(8,128)S(1)}, f32[4,4,64,128]{3,2,1,0:T(8,128)S(1)}, f32[4,4,64,128]{3,2,1,0:T(8,128)S(1)}, f32[4,4,64,128]{3,2,1,0:T(8,128...) custom-call(s32[8]{0:T(128)S(1)} %copy-done.12, s32[8]{0:T(128)S(1)} %copy-done.11, ...), custom_call_target="tpu_custom_call" | custom-call | tf_op jit(solution)/shard_map/waves/pallas_call | solution.py:412
  104.4 3.8 %scatter.1 = f32[4,64,2048]{2,1,0:T(8,128)} custom-call(s32[8]{0:T(128)S(1)} %copy-done.11, s32[2,8]{1,0:T(2,128)S(1)} %collective-permute-done.near_place, s32[2,8]{1,0:T(2,128)S(1)} %collective-permute-done.1.far_place, f32[4,4,64,128]{3,2,1,0:T(8,128)S(1)} %get-tuple-element.21.own_k, f32[4,4,64,128]{3,2,1,0:T(8,128)S(1)} %get-tuple-element.22.own_g, ...), custom_call_target="tpu_custom_call" | custom-call | tf_op jit(solution)/shard_map/scatter/pallas_call | solution.py:430
  108.2 0.6 copy.13
Async XLA Ops:
  0.6 15.9 %copy-start.12 = (s32[8]{0:T(128)S(1)}, s32[8]{0:T(128)}, u32[]{:S(2)}) copy-start(s32[8]{0:T(128)} %own_rows.1) | copy-start | bytes 100
  0.6 15.8 %copy-start.13 = (s32[16]{0:T(128)S(1)}, s32[16]{0:T(128)}, u32[]{:S(2)}) copy-start(s32[16]{0:T(128)} %counts.1) | copy-start | bytes 196
  1.4 7.2 %collective-permute-start.1 = (s32[2,8]{1,0:T(2,128)S(1)}, s32[2,8]{1,0:T(2,128)S(1)}, u32[]{:S(2)}, u32[]{:S(2)}) collective-permute-start(s32[2,8]{1,0:T(2,128)S(1)} %pad_add_fusion), channel_id=1, source_target_pairs={{1,2},{2,1},{3,4},{4,3},{5,6},{6,5},{7,8},{8,7},{9,10},{10,9},{11,... | collective-permute-start | bytes 200 | tf_op jit(solution)/shard_map/ppermute | solution.py:391
  5.6 3.6 %collective-permute-start = (s32[2,8]{1,0:T(2,128)S(1)}, s32[2,8]{1,0:T(2,128)S(1)}, u32[]{:S(2)}, u32[]{:S(2)}) collective-permute-start(s32[2,8]{1,0:T(2,128)S(1)} %pad_add_fusion), channel_id=1, source_target_pairs={{0,1},{1,0},{2,3},{3,2},{4,5},{5,4},{6,7},{7,6},{8,9},{9,8},{10,11... | collective-permute-start | bytes 200 | tf_op jit(solution)/shard_map/ppermute | solution.py:390
  9.2 1.6 %copy-start = (f32[2,2,64,2048]{3,2,1,0:T(8,128)S(1)}, f32[2,2,64,2048]{3,2,1,0:T(8,128)}, u32[]{:S(2)}) copy-start(f32[2,2,64,2048]{3,2,1,0:T(8,128)} %param.10) | copy-start | bytes 6291460
  10.8 0.7 copy-start.11
  11.5 5.0 %copy-start.1 = (f32[8,128,128]{2,1,0:T(8,128)S(1)}, f32[8,128,128]{2,1,0:T(8,128)}, u32[]{:S(2)}) copy-start(f32[8,128,128]{2,1,0:T(8,128)} %diff.1) | copy-start | bytes 1572868
  11.5 5.0 %copy-start.6 = (bf16[2,256,256]{2,1,0:T(8,128)(2,1)S(1)}, bf16[2,256,256]{2,1,0:T(8,128)(2,1)}, u32[]{:S(2)}) copy-start(bf16[2,256,256]{2,1,0:T(8,128)(2,1)} %constant.11.clone.f_left) | copy-start | bytes 786436
  11.5 5.0 %copy-start.7 = (bf16[2,256,256]{2,1,0:T(8,128)(2,1)S(1)}, bf16[2,256,256]{2,1,0:T(8,128)(2,1)}, u32[]{:S(2)}) copy-start(bf16[2,256,256]{2,1,0:T(8,128)(2,1)} %constant.10.clone.f_right) | copy-start | bytes 786436
  11.5 5.0 %copy-start.8 = (bf16[2,256,256]{2,1,0:T(8,128)(2,1)S(1)}, bf16[2,256,256]{2,1,0:T(8,128)(2,1)}, u32[]{:S(2)}) copy-start(bf16[2,256,256]{2,1,0:T(8,128)(2,1)} %constant.9.clone.a_left) | copy-start | bytes 786436
  11.5 5.0 %copy-start.9 = (bf16[2,256,256]{2,1,0:T(8,128)(2,1)S(1)}, bf16[2,256,256]{2,1,0:T(8,128)(2,1)}, u32[]{:S(2)}) copy-start(bf16[2,256,256]{2,1,0:T(8,128)(2,1)} %constant.8.clone.a_right) | copy-start | bytes 786436
  11.5 5.0 %copy-start.10 = (f32[2,128,128]{2,1,0:T(8,128)S(1)}, f32[2,128,128]{2,1,0:T(8,128)}, u32[]{:S(2)}) copy-start(f32[2,128,128]{2,1,0:T(8,128)} %probe.1) | copy-start | bytes 393220
  13.3 0.8 copy-start.2
  14.1 0.8 copy-start.3
  14.9 0.8 copy-start.4
  15.7 0.8 copy-start.5

commit v4 on v3

--- a/solution.py
+++ b/solution.py
@@ -97,8 +97,8 @@
     own_rows, own_cols, counts, near_place, probe, diff,
     own_k, own_g, near_k, near_g, far_k, far_g, a_right, a_left, f_right, f_left,
     own_k_out, own_g_out, near_k_out, near_g_out, far_k_out, far_g_out, probe_out,
-    hopped, merged, rim_in, give_in, rim_back, own_in, rim_grad, own_grad, patch, psi,
-    probe_part, probe_got, send_sem, recv_sem,
+    hopped, merged, rim_in, give_in, rim_back, own_in, near_in, rim_grad, own_grad, patch, psi, hold,
+    probe_part, probe_got, send_sem, recv_sem, load_sem,
 ):
     depth, tile, odd = axis_places()
     tiles = lax.axis_size("tile")
@@ -120,6 +120,14 @@
         bits.append(2 ** len(bits))
     bits = bits[::-1]
 
+    loads = [
+        pltpu.make_async_copy(src, dst, load_sem.at[i])
+        for i, (src, dst) in enumerate(
+            ((near_g, near_in.at[1]), (near_k, near_in.at[0]), (own_k, own_in.at[0]))
+        )
+    ]
+    for local in loads:
+        local.start()
     barrier = pltpu.get_barrier_semaphore()
     greeted = [other, beside, onward, backward] + [(depth, flipped(b)) for b in bits if b > 2]
     for device in greeted:
@@ -166,32 +174,31 @@
         device = (depth, flipped(bits[i]))
         return copy(probe_part.at[2 + i], probe_got.at[1 + i], device, 12 * rounds + 1 + i)
 
-    for j in range(rounds):
-        hop_in(1, j).start()
-        hop_in(0, j).start()
+    order = [(rel, j) for j in range(rounds) for rel in (1, 0)]
+    for item in order[:2]:
+        hop_in(*item).start()
     for j in range(rounds):
         own_swap(j).start()
-    own_in[0] = own_k[...]
+    for local in loads:
+        local.wait()
     row = lax.broadcasted_iota(jnp.int32, (arrays, half, size), 1)
     near_tile = tile + 1 - 2 * odd
 
-    def merge(j, carry):
-        for rel in (1, 0):
-            hop_in(rel, j).wait_recv()
-            slot = 2 * j + (1 - depth if rel else depth)
-            begin = near_place[0, slot] - (near_tile - 1) * half
-            near, far = (near_k, near_g)[rel][j], hopped[rel, j]
-            near_rows = (row >= begin).astype(jnp.int32) != odd
-            merged[rel, j] = jnp.where(near_rows, near, far)
-            cross_in(rel, j).start()
-        return carry
-
-    lax.fori_loop(0, rounds, merge, 0)
-
-    def pass_on(j, carry):
+    def merge(i):
+        rel, j = order[i]
+        hop_in(rel, j).wait_send()
+        if i + 2 < len(order):
+            hop_in(*order[i + 2]).start()
+        hop_in(rel, j).wait_recv()
+        slot = 2 * j + (1 - depth if rel else depth)
+        begin = near_place[0, slot] - (near_tile - 1) * half
+        near_rows = (row >= begin).astype(jnp.int32) != odd
+        merged[rel, j] = jnp.where(near_rows, near_in[rel, j], hopped[rel, j])
+        cross_in(rel, j).start()
+
+    def pass_on(j):
         cross_in(1, j).wait_recv()
         rim_swap(j).start()
-        return carry
 
     def times(a, b):
         return a[0] * b[0] - a[1] * b[1], a[0] * b[1] + a[1] * b[0]
@@ -205,8 +212,7 @@
     def rows(i):
         return slice(i * size, (i + 1) * size)
 
-    def waves(p, carry):
-        lax.fori_loop(p * pair, p * pair + pair, pass_on, 0)
+    def waves(p):
         spots = []
         for i in range(pair):
             j = p * pair + i
@@ -227,79 +233,103 @@
                     a = part * group + s % group
                     patch[s, part, i * size : i * size + half, :] = rim_in[side, j, a]
                     patch[s, part, i * size + half : (i + 1) * size, :] = own_in[side, j, a]
-
-        def forward(s, carry):
+        for s in range(slices - 1):
             wave = apply(times(load(patch, s), load(psi, s)), a_right, a_left)
             psi[s + 1, 0] = wave[0]
             psi[s + 1, 1] = wave[1]
-            return carry
-
-        lax.fori_loop(0, slices - 1, forward, 0)
-        far = apply(times(load(patch, slices - 1), load(psi, slices - 1)), f_right, f_left)
+            if s == 0:
+                yield
+        s = slices - 1
+        far = apply(times(load(patch, s), load(psi, s)), f_right, f_left)
         measured = jnp.concatenate([diff[spot[1]] for spot in spots], axis=0)
         misfit = far[0] * far[0] + far[1] * far[1] - measured
-
-        def finish(s, along):
+        hold[0] = misfit * far[0]
+        hold[1] = -(misfit * far[1])
+        yield
+        for s in reversed(range(slices)):
+            tabs = (f_right, f_left) if s == slices - 1 else (a_right, a_left)
+            along = apply((hold[0], hold[1]), *tabs)
             term = times(load(psi, s), along)
             term = (term[0], -term[1])
-            side = lax.rem(depth + lax.div(s, group), 2)
+            side = lax.rem(depth + s // group, 2)
             for i, (j, _, _, _, on) in enumerate(spots):
                 for part in range(2):
-                    a = part * group + lax.rem(s, group)
+                    a = part * group + s % group
                     value = jnp.where(on, term[part][rows(i)], 0.0)
                     rim_grad[side, j, a] = value[:half]
                     own_grad[side, j, a] = value[half:]
-            return times(load(patch, s), along)
-
-        back = apply((misfit * far[0], -(misfit * far[1])), f_right, f_left)
-        back = finish(jnp.int32(slices - 1), back)
-
-        def reverse(n, back):
-            return finish(slices - 2 - n, apply(back, a_right, a_left))
-
-        back = lax.fori_loop(0, slices - 1, reverse, back)
+            back = times(load(patch, s), along)
+            hold[0] = back[0]
+            hold[1] = back[1]
+            if s == 2:
+                yield
         for i in range(pair):
             j = spots[i][0]
             rim_return(j).start()
-            cross_out(0, j).start()
             own_return(j).start()
+        yield
         for part in range(2):
             total = jnp.zeros((size, size), jnp.float32)
             for i, (_, _, down, across, on) in enumerate(spots):
-                value = jnp.where(on, back[part][rows(i)], 0.0)
+                value = jnp.where(on, hold[part, rows(i), :], 0.0)
                 value = pltpu.roll(value, lax.rem(size - down, size), 0)
                 total = total + pltpu.roll(value, lax.rem(size - across, size), 1)
             total = total if part == 0 else -total
             for side in range(2):
-                before = probe_part[side, part]
-                probe_part[side, part] = before + total[side * half : (side + 1) * half]
-        return carry
-
-    probe_part[0] = jnp.zeros_like(probe_part[0])
-    probe_part[1] = jnp.zeros_like(probe_part[1])
-    lax.fori_loop(0, rounds // pair, waves, 0)
+                value = total[side * half : (side + 1) * half]
+                if p:
+                    value = value + probe_part[side, part]
+                probe_part[side, part] = value
+
+    first = waves(0)
+    for i in range(len(order)):
+        merge(i)
+        if i == 4:
+            pass_on(0)
+            pass_on(1)
+        if i >= 5:
+            next(first)
+    pass_on(2)
+    pass_on(3)
+    next(first)
+
+    back_order = [(0, 0), (0, 1), (1, 0), (1, 1), (0, 2), (0, 3), (1, 2), (1, 3)]
+
+    def send_back(i):
+        if i < len(back_order):
+            rel, j = back_order[i]
+            if rel:
+                rim_return(j).wait_recv()
+            cross_out(rel, j).start()
+
+    def onto(i):
+        cross_out(*back_order[i]).wait_send()
+        send_back(i + 2)
+        cross_out(*back_order[i]).wait_recv()
+        hop_out(*back_order[i]).start()
+
+    send_back(0)
+    send_back(1)
+    next(first, None)
+    second = waves(1)
+    next(second)
+    next(second)
+    next(second)
+    onto(0)
+    onto(1)
+    next(second)
+    onto(2)
+    next(second, None)
 
     probe_swap().start()
 
-    def give(j, carry):
-        rim_return(j).wait_recv()
-        cross_out(1, j).start()
-        return carry
-
-    lax.fori_loop(0, rounds, give, 0)
     probe_swap().wait_recv()
     probe_part[2] = probe_part[depth] + probe_got[0]
     probe_step(0).start()
 
     done = 0
-    for rel, first in ((0, 0), (0, rounds // 2), (1, 0), (1, rounds // 2)):
-
-        def onto(j, carry, rel=rel):
-            cross_out(rel, j).wait_recv()
-            hop_out(rel, j).start()
-            return carry
-
-        lax.fori_loop(first, first + rounds // 2, onto, 0)
+    for i in range(3, len(back_order)):
+        onto(i)
         if done < len(bits) - 1:
             probe_step(done).wait_recv()
             probe_part[3 + done] = probe_part[2 + done] + probe_got[1 + done]
@@ -318,8 +348,6 @@
         own_return(j).wait_recv()
         for rel in range(2):
             hop_out(rel, j).wait_recv()
-            hop_in(rel, j).wait_send()
-            cross_out(rel, j).wait_send()
             hop_out(rel, j).wait_send()
             cross_in(rel, j).wait_send()
         own_swap(j).wait_send()
@@ -372,6 +400,7 @@
 
 SMEM = pl.BlockSpec(memory_space=pltpu.SMEM)
 VMEM = pl.BlockSpec(memory_space=pltpu.VMEM)
+ANY = pl.BlockSpec(memory_space=pl.ANY)
 PARAMS = pltpu.CompilerParams(vmem_limit_bytes=48 * 1024 * 1024)
 
 
@@ -412,12 +441,12 @@
     *parts, probe_grad = pl.pallas_call(
         main_kernel,
         out_shape=[piece] * 6 + [jax.ShapeDtypeStruct(rows_shape, f32)],
-        in_specs=[SMEM] * 4 + [VMEM] * 12,
+        in_specs=[SMEM] * 4 + [VMEM] * 2 + [ANY] * 6 + [VMEM] * 4,
         out_specs=[VMEM] * 7,
-        scratch_shapes=[both, both, both, single, single, both, both, both]
-        + [waves, waves]
+        scratch_shapes=[both, both, both, single, single, both, both, both, both]
+        + [waves, waves, pltpu.VMEM((2, pair * size, size), f32)]
         + [pltpu.VMEM((3 + stages,) + rows_shape, f32), pltpu.VMEM((1 + stages,) + rows_shape, f32)]
-        + [sems, sems],
+        + [sems, sems, pltpu.SemaphoreType.DMA((3,))],
         compiler_params=pltpu.CompilerParams(
             vmem_limit_bytes=48 * 1024 * 1024, collective_id=0, has_side_effects=True
         ),

time: 109 us -> 97.7 us (0.90)
  the two profiles are of different devices: /device:TPU:8 before, /device:TPU:0 now
where the time goes in v4:
time: 97.7 us; the launch traced here: 97.6 us
  Pallas kernels  82.1 us (84%)
  starting transfers between devices  6.39 us (7%)
  local copies, waits for them, and re-layouts  6.11 us (6%)
  waiting for transfers between devices  1.55 us (2%)
    pallas_call x1, Pallas kernels, shards(): pl.pallas_call(main_kernel, out_shape=[piece] * 6 + [jax.ShapeDtypeStruct...  76.5 us
    unnamed x29, local copies, waits for them, and re-layouts  6.11 us
    ppermute x1, starting transfers between devices, shards(): place_near = lax.ppermute(place, 'tile', beside)  5.74 us
    pallas_call x1, Pallas kernels, shards(): pl.pallas_call(scatter_kernel, out_shape=jax.ShapeDtypeStruct(flat.shape,...  3.81 us
  transfers between devices with their start and end apart: 2, of which 1 were waited for; matrix products, arithmetic and copies ran while one was open for 0% of the time, Pallas kernels for 0%

profile of v4, /device:TPU:0, one launch (start us, length us, event | category | flops | bytes accessed | tf_op | source)
XLA Modules:
  0.0 97.6 jit_solution(12455982361085643009)
XLA Ops:
  0.6 0.0 copy-start.12
  0.6 0.0 copy-start.13
  0.6 0.7 pad_add_fusion
  1.4 0.6 collective-permute-start.1
  2.0 5.7 %collective-permute-start = (s32[2,8]{1,0:T(2,128)S(1)}, s32[2,8]{1,0:T(2,128)S(1)}, u32[]{:S(2)}, u32[]{:S(2)}) collective-permute-start(s32[2,8]{1,0:T(2,128)S(1)} %pad_add_fusion), channel_id=1, source_target_pairs={{0,1},{1,0},{2,3},{3,2},{4,5},{5,4},{6,7},{7,6},{8,9},{9,8},{10,11... | collective-permute-start | bytes 200 | tf_op jit(solution)/shard_map/ppermute | solution.py:419
  7.8 0.0 collective-permute-done.1.far_place
  7.8 1.5 %collective-permute-done.near_place = s32[2,8]{1,0:T(2,128)S(1)} collective-permute-done((s32[2,8]{1,0:T(2,128)S(1)}, s32[2,8]{1,0:T(2,128)S(1)}, u32[]{:S(2)}, u32[]{:S(2)}) %collective-permute-start) | collective-permute-done | bytes 96 | tf_op jit(solution)/shard_map/ppermute | solution.py:419
  9.3 0.0 copy-start
  9.3 1.6 %copy-done = f32[2,2,64,2048]{3,2,1,0:T(8,128)S(1)} copy-done((f32[2,2,64,2048]{3,2,1,0:T(8,128)S(1)}, f32[2,2,64,2048]{3,2,1,0:T(8,128)}, u32[]{:S(2)}) %copy-start) | copy-done | bytes 2097176
  10.9 0.0 copy-start.11
  10.9 0.7 copy-done.11
  11.6 0.0 copy-start.1
  11.6 0.0 copy-start.6
  11.6 0.0 copy-start.7
  11.6 0.0 copy-start.8
  11.6 0.0 copy-start.9
  11.6 0.0 copy-start.10
  11.6 1.7 %gather.1 = (f32[4,4,64,128]{3,2,1,0:T(8,128)S(1)}, f32[4,4,64,128]{3,2,1,0:T(8,128)S(1)}, f32[4,4,64,128]{3,2,1,0:T(8,128)S(1)}, f32[4,4,64,128]{3,2,1,0:T(8,12...) custom-call(s32[8]{0:T(128)S(1)} %copy-done.11, s32[2,8]{1,0:T(2,128)S(1)} %collective-permute-done.near_place, ...), custom_call_target="tpu_custom_call" | custom-call | tf_op jit(solution)/shard_map/gather/pallas_call | solution.py:424
  13.3 0.0 copy-start.2
  13.4 0.8 copy-done.2
  14.1 0.0 copy-start.3
  14.1 0.8 copy-done.3
  14.9 0.0 copy-start.4
  14.9 0.8 copy-done.4
  15.7 0.0 copy-start.5
  15.7 0.8 copy-done.5
  16.6 0.0 copy-done.12
  16.6 0.0 copy-done.13
  16.6 0.0 copy-done.1
  16.6 0.0 copy-done.6
  16.6 0.0 copy-done.7
  16.6 0.0 copy-done.8
  16.6 0.0 copy-done.9
  16.6 0.0 copy-done.10
  16.6 76.5 %waves.1 = (f32[4,4,64,128]{3,2,1,0:T(8,128)S(1)}, f32[4,4,64,128]{3,2,1,0:T(8,128)S(1)}, f32[4,4,64,128]{3,2,1,0:T(8,128)S(1)}, f32[4,4,64,128]{3,2,1,0:T(8,128...) custom-call(s32[8]{0:T(128)S(1)} %copy-done.12, s32[8]{0:T(128)S(1)} %copy-done.11, ...), custom_call_target="tpu_custom_call" | custom-call | tf_op jit(solution)/shard_map/waves/pallas_call | solution.py:441
  93.1 3.8 %scatter.1 = f32[4,64,2048]{2,1,0:T(8,128)} custom-call(s32[8]{0:T(128)S(1)} %copy-done.11, s32[2,8]{1,0:T(2,128)S(1)} %collective-permute-done.near_place, s32[2,8]{1,0:T(2,128)S(1)} %collective-permute-done.1.far_place, f32[4,4,64,128]{3,2,1,0:T(8,128)S(1)} %get-tuple-element.21.own_k, f32[4,4,64,128]{3,2,1,0:T(8,128)S(1)} %get-tuple-element.22.own_g, ...), custom_call_target="tpu_custom_call" | custom-call | tf_op jit(solution)/shard_map/scatter/pallas_call | solution.py:459
  96.9 0.6 copy.13
Async XLA Ops:
  0.6 15.9 %copy-start.12 = (s32[8]{0:T(128)S(1)}, s32[8]{0:T(128)}, u32[]{:S(2)}) copy-start(s32[8]{0:T(128)} %own_rows.1) | copy-start | bytes 100
  0.6 15.9 %copy-start.13 = (s32[16]{0:T(128)S(1)}, s32[16]{0:T(128)}, u32[]{:S(2)}) copy-start(s32[16]{0:T(128)} %counts.1) | copy-start | bytes 196
  1.4 6.4 %collective-permute-start.1 = (s32[2,8]{1,0:T(2,128)S(1)}, s32[2,8]{1,0:T(2,128)S(1)}, u32[]{:S(2)}, u32[]{:S(2)}) collective-permute-start(s32[2,8]{1,0:T(2,128)S(1)} %pad_add_fusion), channel_id=1, source_target_pairs={{1,2},{2,1},{3,4},{4,3},{5,6},{6,5},{7,8},{8,7},{9,10},{10,9},{11,... | collective-permute-start | bytes 200 | tf_op jit(solution)/shard_map/ppermute | solution.py:420
  2.0 7.3 %collective-permute-start = (s32[2,8]{1,0:T(2,128)S(1)}, s32[2,8]{1,0:T(2,128)S(1)}, u32[]{:S(2)}, u32[]{:S(2)}) collective-permute-start(s32[2,8]{1,0:T(2,128)S(1)} %pad_add_fusion), channel_id=1, source_target_pairs={{0,1},{1,0},{2,3},{3,2},{4,5},{5,4},{6,7},{7,6},{8,9},{9,8},{10,11... | collective-permute-start | bytes 200 | tf_op jit(solution)/shard_map/ppermute | solution.py:419
  9.3 1.6 %copy-start = (f32[2,2,64,2048]{3,2,1,0:T(8,128)S(1)}, f32[2,2,64,2048]{3,2,1,0:T(8,128)}, u32[]{:S(2)}) copy-start(f32[2,2,64,2048]{3,2,1,0:T(8,128)} %param.10) | copy-start | bytes 6291460
  10.9 0.7 copy-start.11
  11.6 5.0 %copy-start.1 = (f32[8,128,128]{2,1,0:T(8,128)S(1)}, f32[8,128,128]{2,1,0:T(8,128)}, u32[]{:S(2)}) copy-start(f32[8,128,128]{2,1,0:T(8,128)} %diff.1) | copy-start | bytes 1572868
  11.6 5.0 %copy-start.6 = (bf16[2,256,256]{2,1,0:T(8,128)(2,1)S(1)}, bf16[2,256,256]{2,1,0:T(8,128)(2,1)}, u32[]{:S(2)}) copy-start(bf16[2,256,256]{2,1,0:T(8,128)(2,1)} %constant.11.clone.f_left) | copy-start | bytes 786436
  11.6 5.0 %copy-start.7 = (bf16[2,256,256]{2,1,0:T(8,128)(2,1)S(1)}, bf16[2,256,256]{2,1,0:T(8,128)(2,1)}, u32[]{:S(2)}) copy-start(bf16[2,256,256]{2,1,0:T(8,128)(2,1)} %constant.10.clone.f_right) | copy-start | bytes 786436
  11.6 5.0 %copy-start.8 = (bf16[2,256,256]{2,1,0:T(8,128)(2,1)S(1)}, bf16[2,256,256]{2,1,0:T(8,128)(2,1)}, u32[]{:S(2)}) copy-start(bf16[2,256,256]{2,1,0:T(8,128)(2,1)} %constant.9.clone.a_left) | copy-start | bytes 786436
  11.6 5.0 %copy-start.9 = (bf16[2,256,256]{2,1,0:T(8,128)(2,1)S(1)}, bf16[2,256,256]{2,1,0:T(8,128)(2,1)}, u32[]{:S(2)}) copy-start(bf16[2,256,256]{2,1,0:T(8,128)(2,1)} %constant.8.clone.a_right) | copy-start | bytes 786436
  11.6 5.0 %copy-start.10 = (f32[2,128,128]{2,1,0:T(8,128)S(1)}, f32[2,128,128]{2,1,0:T(8,128)}, u32[]{:S(2)}) copy-start(f32[2,128,128]{2,1,0:T(8,128)} %probe.1) | copy-start | bytes 393220
  13.3 0.8 copy-start.2
  14.1 0.8 copy-start.3
  14.9 0.8 copy-start.4
  15.7 0.8 copy-start.5

commit v5 on v4

--- a/solution.py
+++ b/solution.py
@@ -16,7 +16,7 @@
 def split_table(table):
     head = table.astype(np.float32).astype(ml_dtypes.bfloat16)
     tail = (table - head.astype(np.float64)).astype(np.float32).astype(ml_dtypes.bfloat16)
-    return np.stack([head, tail])
+    return np.concatenate([head, tail])
 
 
 def tables(size):
@@ -44,8 +44,10 @@
 
 
 def two_sided(re, im, right, left, slots, size):
+    count = slots * size
     head, tail = halves(jnp.concatenate([re, im], axis=1))
-    y = dot(head, right[0]) + dot(tail, right[0]) + dot(head, right[1])
+    y = dot(jnp.concatenate([head, tail], axis=0), right[: 2 * size])
+    y = y[:count] + y[count:] + dot(head, right[2 * size :])
     z = jnp.concatenate(
         [
             jnp.concatenate(
@@ -56,7 +58,8 @@
         axis=1,
     )
     head, tail = halves(z)
-    y = dot(left[0], head) + dot(left[0], tail) + dot(left[1], head)
+    y = dot(left[...], head)
+    y = y[: 2 * size] + y[2 * size :] + dot(left[: 2 * size], tail)
     out_re = [y[:size, j * size : (j + 1) * size] for j in range(slots)]
     out_im = [y[size:, j * size : (j + 1) * size] for j in range(slots)]
     return jnp.concatenate(out_re, axis=0), jnp.concatenate(out_im, axis=0)
@@ -94,11 +97,23 @@
 
 
 def main_kernel(
-    own_rows, own_cols, counts, near_place, probe, diff,
-    own_k, own_g, near_k, near_g, far_k, far_g, a_right, a_left, f_right, f_left,
+    own_rows, own_cols, counts, near_place, probe_hbm, diff_hbm,
+    own_k, own_g, near_k, near_g, far_k, far_g, *rest,
+):
+    tables_hbm, rest = rest[:4], rest[4:]
+    exchange(
+        own_rows, own_cols, counts, near_place, probe_hbm, diff_hbm,
+        own_k, own_g, near_k, near_g, far_k, far_g, tables_hbm, *rest,
+    )
+
+
+def exchange(
+    own_rows, own_cols, counts, near_place, probe_hbm, diff_hbm,
+    own_k, own_g, near_k, near_g, far_k, far_g, tables_hbm,
     own_k_out, own_g_out, near_k_out, near_g_out, far_k_out, far_g_out, probe_out,
     hopped, merged, rim_in, give_in, rim_back, own_in, near_in, rim_grad, own_grad, patch, psi, hold,
-    probe_part, probe_got, send_sem, recv_sem, load_sem,
+    probe_part, probe_got, probe, diff, a_right, a_left, f_right, f_left,
+    send_sem, recv_sem, load_sem,
 ):
     depth, tile, odd = axis_places()
     tiles = lax.axis_size("tile")
@@ -123,7 +138,14 @@
     loads = [
         pltpu.make_async_copy(src, dst, load_sem.at[i])
         for i, (src, dst) in enumerate(
-            ((near_g, near_in.at[1]), (near_k, near_in.at[0]), (own_k, own_in.at[0]))
+            (
+                (near_g, near_in.at[1]),
+                (near_k, near_in.at[0]),
+                (own_k, own_in.at[0]),
+                (probe_hbm, probe),
+                (diff_hbm, diff),
+                *zip(tables_hbm, (a_right, a_left, f_right, f_left)),
+            )
         )
     ]
     for local in loads:
@@ -179,7 +201,7 @@
         hop_in(*item).start()
     for j in range(rounds):
         own_swap(j).start()
-    for local in loads:
+    for local in loads[:3]:
         local.wait()
     row = lax.broadcasted_iota(jnp.int32, (arrays, half, size), 1)
     near_tile = tile + 1 - 2 * odd
@@ -237,8 +259,7 @@
             wave = apply(times(load(patch, s), load(psi, s)), a_right, a_left)
             psi[s + 1, 0] = wave[0]
             psi[s + 1, 1] = wave[1]
-            if s == 0:
-                yield
+            yield
         s = slices - 1
         far = apply(times(load(patch, s), load(psi, s)), f_right, f_left)
         measured = jnp.concatenate([diff[spot[1]] for spot in spots], axis=0)
@@ -261,7 +282,7 @@
             back = times(load(patch, s), along)
             hold[0] = back[0]
             hold[1] = back[1]
-            if s == 2:
+            if s:
                 yield
         for i in range(pair):
             j = spots[i][0]
@@ -287,10 +308,14 @@
         if i == 4:
             pass_on(0)
             pass_on(1)
+            for local in loads[3:]:
+                local.wait()
         if i >= 5:
+            next(first)
             next(first)
     pass_on(2)
     pass_on(3)
+    next(first)
     next(first)
 
     back_order = [(0, 0), (0, 1), (1, 0), (1, 1), (0, 2), (0, 3), (1, 2), (1, 3)]
@@ -312,11 +337,12 @@
     send_back(1)
     next(first, None)
     second = waves(1)
+    for i in range(5):
+        next(second)
+    onto(0)
     next(second)
+    onto(1)
     next(second)
-    next(second)
-    onto(0)
-    onto(1)
     next(second)
     onto(2)
     next(second, None)
@@ -441,12 +467,14 @@
     *parts, probe_grad = pl.pallas_call(
         main_kernel,
         out_shape=[piece] * 6 + [jax.ShapeDtypeStruct(rows_shape, f32)],
-        in_specs=[SMEM] * 4 + [VMEM] * 2 + [ANY] * 6 + [VMEM] * 4,
+        in_specs=[SMEM] * 4 + [ANY] * 12,
         out_specs=[VMEM] * 7,
         scratch_shapes=[both, both, both, single, single, both, both, both, both]
         + [waves, waves, pltpu.VMEM((2, pair * size, size), f32)]
         + [pltpu.VMEM((3 + stages,) + rows_shape, f32), pltpu.VMEM((1 + stages,) + rows_shape, f32)]
-        + [sems, sems, pltpu.SemaphoreType.DMA((3,))],
+        + [pltpu.VMEM(probe.shape, f32), pltpu.VMEM(diffraction.shape, f32)]
+        + [pltpu.VMEM(t.shape, t.dtype) for t in tabs]
+        + [sems, sems, pltpu.SemaphoreType.DMA((9,))],
         compiler_params=pltpu.CompilerParams(
             vmem_limit_bytes=48 * 1024 * 1024, collective_id=0, has_side_effects=True
         ),

time: 97.7 us -> 98.6 us (level)
  no operation moved by 1% of the time
where the time goes in v5:
time: 98.6 us; the launch traced here: 98.4 us
  Pallas kernels  82.9 us (84%)
  starting transfers between devices  6.39 us (6%)
  local copies, waits for them, and re-layouts  6.11 us (6%)
  waiting for transfers between devices  1.55 us (2%)
    pallas_call x1, Pallas kernels, shards(): pl.pallas_call(main_kernel, out_shape=[piece] * 6 + [jax.ShapeDtypeStruct...  77.3 us
    unnamed x29, local copies, waits for them, and re-layouts  6.11 us
    ppermute x1, starting transfers between devices, shards(): place_near = lax.ppermute(place, 'tile', beside)  5.74 us
    pallas_call x1, Pallas kernels, shards(): pl.pallas_call(scatter_kernel, out_shape=jax.ShapeDtypeStruct(flat.shape,...  3.81 us
  transfers between devices with their start and end apart: 2, of which 1 were waited for; matrix products, arithmetic and copies ran while one was open for 0% of the time, Pallas kernels for 0%

profile of v5, /device:TPU:0, one launch (start us, length us, event | category | flops | bytes accessed | tf_op | source)
XLA Modules:
  0.0 98.4 jit_solution(3959469822967998215)
XLA Ops:
  0.6 0.0 copy-start.12
  0.6 0.0 copy-start.13
  0.6 0.7 pad_add_fusion
  1.4 0.6 collective-permute-start.1
  2.0 5.7 %collective-permute-start = (s32[2,8]{1,0:T(2,128)S(1)}, s32[2,8]{1,0:T(2,128)S(1)}, u32[]{:S(2)}, u32[]{:S(2)}) collective-permute-start(s32[2,8]{1,0:T(2,128)S(1)} %pad_add_fusion), channel_id=1, source_target_pairs={{0,1},{1,0},{2,3},{3,2},{4,5},{5,4},{6,7},{7,6},{8,9},{9,8},{10,11... | collective-permute-start | bytes 200 | tf_op jit(solution)/shard_map/ppermute | solution.py:445
  7.8 0.0 collective-permute-done.1.far_place
  7.8 1.5 %collective-permute-done.near_place = s32[2,8]{1,0:T(2,128)S(1)} collective-permute-done((s32[2,8]{1,0:T(2,128)S(1)}, s32[2,8]{1,0:T(2,128)S(1)}, u32[]{:S(2)}, u32[]{:S(2)}) %collective-permute-start) | collective-permute-done | bytes 96 | tf_op jit(solution)/shard_map/ppermute | solution.py:445
  9.3 0.0 copy-start
  9.3 1.6 %copy-done = f32[2,2,64,2048]{3,2,1,0:T(8,128)S(1)} copy-done((f32[2,2,64,2048]{3,2,1,0:T(8,128)S(1)}, f32[2,2,64,2048]{3,2,1,0:T(8,128)}, u32[]{:S(2)}) %copy-start) | copy-done | bytes 2097176
  10.9 0.0 copy-start.11
  10.9 0.7 copy-done.11
  11.6 0.0 copy-start.1
  11.6 0.0 copy-start.6
  11.6 0.0 copy-start.7
  11.6 0.0 copy-start.8
  11.6 0.0 copy-start.9
  11.6 0.0 copy-start.10
  11.6 1.7 %gather.1 = (f32[4,4,64,128]{3,2,1,0:T(8,128)S(1)}, f32[4,4,64,128]{3,2,1,0:T(8,128)S(1)}, f32[4,4,64,128]{3,2,1,0:T(8,128)S(1)}, f32[4,4,64,128]{3,2,1,0:T(8,12...) custom-call(s32[8]{0:T(128)S(1)} %copy-done.11, s32[2,8]{1,0:T(2,128)S(1)} %collective-permute-done.near_place, ...), custom_call_target="tpu_custom_call" | custom-call | tf_op jit(solution)/shard_map/gather/pallas_call | solution.py:450
  13.3 0.0 copy-start.2
  13.4 0.8 copy-done.2
  14.1 0.0 copy-start.3
  14.1 0.8 copy-done.3
  14.9 0.0 copy-start.4
  14.9 0.8 copy-done.4
  15.7 0.0 copy-start.5
  15.7 0.8 copy-done.5
  16.6 0.0 copy-done.12
  16.6 0.0 copy-done.13
  16.6 0.0 copy-done.1
  16.6 0.0 copy-done.6
  16.6 0.0 copy-done.7
  16.6 0.0 copy-done.8
  16.6 0.0 copy-done.9
  16.6 0.0 copy-done.10
  16.6 77.3 %waves.1 = (f32[4,4,64,128]{3,2,1,0:T(8,128)S(1)}, f32[4,4,64,128]{3,2,1,0:T(8,128)S(1)}, f32[4,4,64,128]{3,2,1,0:T(8,128)S(1)}, f32[4,4,64,128]{3,2,1,0:T(8,128...) custom-call(s32[8]{0:T(128)S(1)} %copy-done.12, s32[8]{0:T(128)S(1)} %copy-done.11, ...), custom_call_target="tpu_custom_call" | custom-call | tf_op jit(solution)/shard_map/waves/pallas_call | solution.py:467
  93.9 3.8 %scatter.1 = f32[4,64,2048]{2,1,0:T(8,128)} custom-call(s32[8]{0:T(128)S(1)} %copy-done.11, s32[2,8]{1,0:T(2,128)S(1)} %collective-permute-done.near_place, s32[2,8]{1,0:T(2,128)S(1)} %collective-permute-done.1.far_place, f32[4,4,64,128]{3,2,1,0:T(8,128)S(1)} %get-tuple-element.21.own_k, f32[4,4,64,128]{3,2,1,0:T(8,128)S(1)} %get-tuple-element.22.own_g, ...), custom_call_target="tpu_custom_call" | custom-call | tf_op jit(solution)/shard_map/scatter/pallas_call | solution.py:487
  97.8 0.6 copy.13
Async XLA Ops:
  0.6 15.9 %copy-start.12 = (s32[8]{0:T(128)S(1)}, s32[8]{0:T(128)}, u32[]{:S(2)}) copy-start(s32[8]{0:T(128)} %own_rows.1) | copy-start | bytes 100
  0.6 15.9 %copy-start.13 = (s32[16]{0:T(128)S(1)}, s32[16]{0:T(128)}, u32[]{:S(2)}) copy-start(s32[16]{0:T(128)} %counts.1) | copy-start | bytes 196
  1.4 6.4 %collective-permute-start.1 = (s32[2,8]{1,0:T(2,128)S(1)}, s32[2,8]{1,0:T(2,128)S(1)}, u32[]{:S(2)}, u32[]{:S(2)}) collective-permute-start(s32[2,8]{1,0:T(2,128)S(1)} %pad_add_fusion), channel_id=1, source_target_pairs={{1,2},{2,1},{3,4},{4,3},{5,6},{6,5},{7,8},{8,7},{9,10},{10,9},{11,... | collective-permute-start | bytes 200 | tf_op jit(solution)/shard_map/ppermute | solution.py:446
  2.0 7.3 %collective-permute-start = (s32[2,8]{1,0:T(2,128)S(1)}, s32[2,8]{1,0:T(2,128)S(1)}, u32[]{:S(2)}, u32[]{:S(2)}) collective-permute-start(s32[2,8]{1,0:T(2,128)S(1)} %pad_add_fusion), channel_id=1, source_target_pairs={{0,1},{1,0},{2,3},{3,2},{4,5},{5,4},{6,7},{7,6},{8,9},{9,8},{10,11... | collective-permute-start | bytes 200 | tf_op jit(solution)/shard_map/ppermute | solution.py:445
  9.3 1.6 %copy-start = (f32[2,2,64,2048]{3,2,1,0:T(8,128)S(1)}, f32[2,2,64,2048]{3,2,1,0:T(8,128)}, u32[]{:S(2)}) copy-start(f32[2,2,64,2048]{3,2,1,0:T(8,128)} %param.10) | copy-start | bytes 6291460
  10.9 0.7 copy-start.11
  11.6 5.0 %copy-start.1 = (f32[8,128,128]{2,1,0:T(8,128)S(1)}, f32[8,128,128]{2,1,0:T(8,128)}, u32[]{:S(2)}) copy-start(f32[8,128,128]{2,1,0:T(8,128)} %diff_hbm.1) | copy-start | bytes 1572868
  11.6 5.0 %copy-start.6 = (bf16[512,256]{1,0:T(8,128)(2,1)S(1)}, bf16[512,256]{1,0:T(8,128)(2,1)}, u32[]{:S(2)}) copy-start(bf16[512,256]{1,0:T(8,128)(2,1)} %constant.11.clone.rest_3_) | copy-start | bytes 786436
  11.6 5.0 %copy-start.7 = (bf16[512,256]{1,0:T(8,128)(2,1)S(1)}, bf16[512,256]{1,0:T(8,128)(2,1)}, u32[]{:S(2)}) copy-start(bf16[512,256]{1,0:T(8,128)(2,1)} %constant.10.clone.rest_2_) | copy-start | bytes 786436
  11.6 5.0 %copy-start.8 = (bf16[512,256]{1,0:T(8,128)(2,1)S(1)}, bf16[512,256]{1,0:T(8,128)(2,1)}, u32[]{:S(2)}) copy-start(bf16[512,256]{1,0:T(8,128)(2,1)} %constant.9.clone.rest_1_) | copy-start | bytes 786436
  11.6 5.0 %copy-start.9 = (bf16[512,256]{1,0:T(8,128)(2,1)S(1)}, bf16[512,256]{1,0:T(8,128)(2,1)}, u32[]{:S(2)}) copy-start(bf16[512,256]{1,0:T(8,128)(2,1)} %constant.8.clone.rest_0_) | copy-start | bytes 786436
  11.6 5.0 %copy-start.10 = (f32[2,128,128]{2,1,0:T(8,128)S(1)}, f32[2,128,128]{2,1,0:T(8,128)}, u32[]{:S(2)}) copy-start(f32[2,128,128]{2,1,0:T(8,128)} %probe_hbm.1) | copy-start | bytes 393220
  13.3 0.8 copy-start.2
  14.1 0.8 copy-start.3
  14.9 0.8 copy-start.4
  15.7 0.8 copy-start.5

commit v6 on v5

--- a/solution.py
+++ b/solution.py
@@ -94,6 +94,7 @@
 
 
 MESH = pl.DeviceIdType.MESH
+WINDOW = 3
 
 
 def main_kernel(
@@ -197,7 +198,7 @@
         return copy(probe_part.at[2 + i], probe_got.at[1 + i], device, 12 * rounds + 1 + i)
 
     order = [(rel, j) for j in range(rounds) for rel in (1, 0)]
-    for item in order[:2]:
+    for item in order[:WINDOW]:
         hop_in(*item).start()
     for j in range(rounds):
         own_swap(j).start()
@@ -209,8 +210,8 @@
     def merge(i):
         rel, j = order[i]
         hop_in(rel, j).wait_send()
-        if i + 2 < len(order):
-            hop_in(*order[i + 2]).start()
+        if i + WINDOW < len(order):
+            hop_in(*order[i + WINDOW]).start()
         hop_in(rel, j).wait_recv()
         slot = 2 * j + (1 - depth if rel else depth)
         begin = near_place[0, slot] - (near_tile - 1) * half
@@ -329,21 +330,22 @@
 
     def onto(i):
         cross_out(*back_order[i]).wait_send()
-        send_back(i + 2)
+        send_back(i + WINDOW)
         cross_out(*back_order[i]).wait_recv()
         hop_out(*back_order[i]).start()
 
     send_back(0)
     send_back(1)
     next(first, None)
+    send_back(2)
     second = waves(1)
     for i in range(5):
         next(second)
     onto(0)
     next(second)
-    onto(1)
     next(second)
     next(second)
+    onto(1)
     onto(2)
     next(second, None)
 
@@ -427,7 +429,7 @@
 SMEM = pl.BlockSpec(memory_space=pltpu.SMEM)
 VMEM = pl.BlockSpec(memory_space=pltpu.VMEM)
 ANY = pl.BlockSpec(memory_space=pl.ANY)
-PARAMS = pltpu.CompilerParams(vmem_limit_bytes=48 * 1024 * 1024)
+PARAMS = pltpu.CompilerParams(vmem_limit_bytes=16 * 1024 * 1024)
 
 
 def shards(transmission, probe, scan_rows, scan_cols, tile_counts, diffraction):
@@ -476,7 +478,7 @@
         + [pltpu.VMEM(t.shape, t.dtype) for t in tabs]
         + [sems, sems, pltpu.SemaphoreType.DMA((9,))],
         compiler_params=pltpu.CompilerParams(
-            vmem_limit_bytes=48 * 1024 * 1024, collective_id=0, has_side_effects=True
+            vmem_limit_bytes=24 * 1024 * 1024, collective_id=0, has_side_effects=True
         ),
         name="waves",
     )(

time: 98.6 us -> 97 us (0.984)
  local copies, waits for them, and re-layouts: 6.11 us -> 2.92 us
  Pallas kernels: 82.9 us -> 84.1 us
    unnamed x29 -> x23, local copies, waits for them, and re-layouts: 6.11 us -> 2.92 us
    pallas_call x1, Pallas kernels: 77.3 us -> 78.6 us  [shards(): pl.pallas_call(main_kernel, out_shape=[piece] * 6 + [jax.ShapeDtypeStruct...]
where the time goes in v6:
time: 97 us; the launch traced here: 96.5 us
  Pallas kernels  84.1 us (87%)
  starting transfers between devices  6.39 us (7%)
  local copies, waits for them, and re-layouts  2.92 us (3%)
  waiting for transfers between devices  1.55 us (2%)
    pallas_call x1, Pallas kernels, shards(): pl.pallas_call(main_kernel, out_shape=[piece] * 6 + [jax.ShapeDtypeStruct...  78.6 us
    ppermute x1, starting transfers between devices, shards(): place_near = lax.ppermute(place, 'tile', beside)  5.74 us
    pallas_call x1, Pallas kernels, shards(): pl.pallas_call(scatter_kernel, out_shape=jax.ShapeDtypeStruct(flat.shape,...  3.81 us
    unnamed x23, local copies, waits for them, and re-layouts  2.92 us
  transfers between devices with their start and end apart: 2, of which 1 were waited for; matrix products, arithmetic and copies ran while one was open for 0% of the time, Pallas kernels for 0%

profile of v6, /device:TPU:0, one launch (start us, length us, event | category | flops | bytes accessed | tf_op | source)
XLA Modules:
  0.0 96.5 jit_solution(7198104073035391912)
XLA Ops:
  0.6 0.0 copy-start.9
  0.6 0.0 copy-start.8
  0.7 0.0 copy-start.10
  0.7 0.7 pad_add_fusion
  1.4 0.7 collective-permute-start.1
  2.0 5.7 %collective-permute-start = (s32[2,8]{1,0:T(2,128)S(1)}, s32[2,8]{1,0:T(2,128)S(1)}, u32[]{:S(2)}, u32[]{:S(2)}) collective-permute-start(s32[2,8]{1,0:T(2,128)S(1)} %pad_add_fusion), channel_id=1, source_target_pairs={{0,1},{1,0},{2,3},{3,2},{4,5},{5,4},{6,7},{7,6},{8,9},{9,8},{10,11... | collective-permute-start | bytes 200 | tf_op jit(solution)/shard_map/ppermute | solution.py:447
  7.8 0.0 collective-permute-done.1.far_place
  7.8 1.5 %collective-permute-done.near_place = s32[2,8]{1,0:T(2,128)S(1)} collective-permute-done((s32[2,8]{1,0:T(2,128)S(1)}, s32[2,8]{1,0:T(2,128)S(1)}, u32[]{:S(2)}, u32[]{:S(2)}) %collective-permute-start) | collective-permute-done | bytes 96 | tf_op jit(solution)/shard_map/ppermute | solution.py:447
  9.3 0.0 copy-start
  9.3 1.6 %copy-done = f32[2,2,64,2048]{3,2,1,0:T(8,128)S(1)} copy-done((f32[2,2,64,2048]{3,2,1,0:T(8,128)S(1)}, f32[2,2,64,2048]{3,2,1,0:T(8,128)}, u32[]{:S(2)}) %copy-start) | copy-done | bytes 2097176
  10.9 0.0 copy-start.7
  10.9 0.7 copy-done.7
  11.6 0.0 copy-start.1
  11.6 0.0 copy-start.2
  11.6 0.0 copy-start.3
  11.6 0.0 copy-start.4
  11.6 0.0 copy-start.5
  11.6 0.0 copy-start.6
  11.6 1.7 %gather.1 = (f32[4,4,64,128]{3,2,1,0:T(8,128)S(1)}, f32[4,4,64,128]{3,2,1,0:T(8,128)S(1)}, f32[4,4,64,128]{3,2,1,0:T(8,128)S(1)}, f32[4,4,64,128]{3,2,1,0:T(8,12...) custom-call(s32[8]{0:T(128)S(1)} %copy-done.7, s32[2,8]{1,0:T(2,128)S(1)} %collective-permute-done.near_place, ...), custom_call_target="tpu_custom_call" | custom-call | tf_op jit(solution)/shard_map/gather/pallas_call | solution.py:452
  13.4 0.0 copy-done.9
  13.4 0.0 copy-done.8
  13.4 0.0 copy-done.10
  13.4 0.0 copy-done.1
  13.4 0.0 copy-done.2
  13.4 0.0 copy-done.3
  13.4 0.0 copy-done.4
  13.4 0.0 copy-done.5
  13.4 0.0 copy-done.6
  13.4 78.6 %waves.1 = (f32[4,4,64,128]{3,2,1,0:T(8,128)S(1)}, f32[4,4,64,128]{3,2,1,0:T(8,128)S(1)}, f32[4,4,64,128]{3,2,1,0:T(8,128)S(1)}, f32[4,4,64,128]{3,2,1,0:T(8,128...) custom-call(s32[8]{0:T(128)S(1)} %copy-done.9, s32[8]{0:T(128)S(1)} %copy-done.8, ...), custom_call_target="tpu_custom_call" | custom-call | tf_op jit(solution)/shard_map/waves/pallas_call | solution.py:469
  92.0 3.8 %scatter.1 = f32[4,64,2048]{2,1,0:T(8,128)} custom-call(s32[8]{0:T(128)S(1)} %copy-done.8, s32[2,8]{1,0:T(2,128)S(1)} %collective-permute-done.near_place, s32[2,8]{1,0:T(2,128)S(1)} %collective-permute-done.1.far_place, f32[4,4,64,128]{3,2,1,0:T(8,128)S(1)} %get-tuple-element.21.own_k, f32[4,4,64,128]{3,2,1,0:T(8,128)S(1)} %get-tuple-element.22.own_g, ...), custom_call_target="tpu_custom_call" | custom-call | tf_op jit(solution)/shard_map/scatter/pallas_call | solution.py:489
  95.8 0.6 copy.13
Async XLA Ops:
  0.6 12.7 %copy-start.9 = (s32[8]{0:T(128)S(1)}, s32[8]{0:T(128)}, u32[]{:S(2)}) copy-start(s32[8]{0:T(128)} %own_rows.1) | copy-start | bytes 100
  0.6 12.7 %copy-start.8 = (s32[8]{0:T(128)S(1)}, s32[8]{0:T(128)}, u32[]{:S(2)}) copy-start(s32[8]{0:T(128)} %own_cols.5) | copy-start | bytes 100
  0.7 12.7 %copy-start.10 = (s32[16]{0:T(128)S(1)}, s32[16]{0:T(128)}, u32[]{:S(2)}) copy-start(s32[16]{0:T(128)} %counts.1) | copy-start | bytes 196
  1.4 6.4 %collective-permute-start.1 = (s32[2,8]{1,0:T(2,128)S(1)}, s32[2,8]{1,0:T(2,128)S(1)}, u32[]{:S(2)}, u32[]{:S(2)}) collective-permute-start(s32[2,8]{1,0:T(2,128)S(1)} %pad_add_fusion), channel_id=1, source_target_pairs={{1,2},{2,1},{3,4},{4,3},{5,6},{6,5},{7,8},{8,7},{9,10},{10,9},{11,... | collective-permute-start | bytes 200 | tf_op jit(solution)/shard_map/ppermute | solution.py:448
  2.0 7.3 %collective-permute-start = (s32[2,8]{1,0:T(2,128)S(1)}, s32[2,8]{1,0:T(2,128)S(1)}, u32[]{:S(2)}, u32[]{:S(2)}) collective-permute-start(s32[2,8]{1,0:T(2,128)S(1)} %pad_add_fusion), channel_id=1, source_target_pairs={{0,1},{1,0},{2,3},{3,2},{4,5},{5,4},{6,7},{7,6},{8,9},{9,8},{10,11... | collective-permute-start | bytes 200 | tf_op jit(solution)/shard_map/ppermute | solution.py:447
  9.3 1.6 %copy-start = (f32[2,2,64,2048]{3,2,1,0:T(8,128)S(1)}, f32[2,2,64,2048]{3,2,1,0:T(8,128)}, u32[]{:S(2)}) copy-start(f32[2,2,64,2048]{3,2,1,0:T(8,128)} %param.10) | copy-start | bytes 6291460
  10.9 0.7 copy-start.7
  11.6 1.8 %copy-start.1 = (f32[8,128,128]{2,1,0:T(8,128)S(1)}, f32[8,128,128]{2,1,0:T(8,128)}, u32[]{:S(2)}) copy-start(f32[8,128,128]{2,1,0:T(8,128)} %diff_hbm.1) | copy-start | bytes 1572868
  11.6 1.8 %copy-start.2 = (bf16[512,256]{1,0:T(8,128)(2,1)S(1)}, bf16[512,256]{1,0:T(8,128)(2,1)}, u32[]{:S(2)}) copy-start(bf16[512,256]{1,0:T(8,128)(2,1)} %constant.11.clone.rest_3_) | copy-start | bytes 786436
  11.6 1.8 %copy-start.3 = (bf16[512,256]{1,0:T(8,128)(2,1)S(1)}, bf16[512,256]{1,0:T(8,128)(2,1)}, u32[]{:S(2)}) copy-start(bf16[512,256]{1,0:T(8,128)(2,1)} %constant.10.clone.rest_2_) | copy-start | bytes 786436
  11.6 1.8 %copy-start.4 = (bf16[512,256]{1,0:T(8,128)(2,1)S(1)}, bf16[512,256]{1,0:T(8,128)(2,1)}, u32[]{:S(2)}) copy-start(bf16[512,256]{1,0:T(8,128)(2,1)} %constant.9.clone.rest_1_) | copy-start | bytes 786436
  11.6 1.8 %copy-start.5 = (bf16[512,256]{1,0:T(8,128)(2,1)S(1)}, bf16[512,256]{1,0:T(8,128)(2,1)}, u32[]{:S(2)}) copy-start(bf16[512,256]{1,0:T(8,128)(2,1)} %constant.8.clone.rest_0_) | copy-start | bytes 786436
  11.6 1.8 %copy-start.6 = (f32[2,128,128]{2,1,0:T(8,128)S(1)}, f32[2,128,128]{2,1,0:T(8,128)}, u32[]{:S(2)}) copy-start(f32[2,128,128]{2,1,0:T(8,128)} %probe_hbm.1) | copy-start | bytes 393220

commit v7 on v6

--- a/solution.py
+++ b/solution.py
@@ -358,7 +358,7 @@
     done = 0
     for i in range(3, len(back_order)):
         onto(i)
-        if done < len(bits) - 1:
+        if i >= 5 and done < len(bits) - 1:
             probe_step(done).wait_recv()
             probe_part[3 + done] = probe_part[2 + done] + probe_got[1 + done]
             done += 1

time: 97 us -> 93.5 us (0.964)
  Pallas kernels: 84.1 us -> 80.9 us
    pallas_call x1, Pallas kernels: 78.6 us -> 75.4 us  [shards(): pl.pallas_call(main_kernel, out_shape=[piece] * 6 + [jax.ShapeDtypeStruct...]
where the time goes in v7:
time: 93.5 us; the launch traced here: 93.3 us
  Pallas kernels  80.9 us (87%)
  starting transfers between devices  6.39 us (7%)
  local copies, waits for them, and re-layouts  2.92 us (3%)
  waiting for transfers between devices  1.55 us (2%)
    pallas_call x1, Pallas kernels, shards(): pl.pallas_call(main_kernel, out_shape=[piece] * 6 + [jax.ShapeDtypeStruct...  75.4 us
    ppermute x1, starting transfers between devices, shards(): place_near = lax.ppermute(place, 'tile', beside)  5.74 us
    pallas_call x1, Pallas kernels, shards(): pl.pallas_call(scatter_kernel, out_shape=jax.ShapeDtypeStruct(flat.shape,...  3.81 us
    unnamed x23, local copies, waits for them, and re-layouts  2.92 us
  transfers between devices with their start and end apart: 2, of which 1 were waited for; matrix products, arithmetic and copies ran while one was open for 0% of the time, Pallas kernels for 0%

profile of v7, /device:TPU:0, one launch (start us, length us, event | category | flops | bytes accessed | tf_op | source)
XLA Modules:
  0.0 93.3 jit_solution(8472360891657552975)
XLA Ops:
  0.6 0.0 copy-start.9
  0.6 0.0 copy-start.8
  0.7 0.0 copy-start.10
  0.7 0.7 pad_add_fusion
  1.4 0.7 collective-permute-start.1
  2.0 5.7 %collective-permute-start = (s32[2,8]{1,0:T(2,128)S(1)}, s32[2,8]{1,0:T(2,128)S(1)}, u32[]{:S(2)}, u32[]{:S(2)}) collective-permute-start(s32[2,8]{1,0:T(2,128)S(1)} %pad_add_fusion), channel_id=1, source_target_pairs={{0,1},{1,0},{2,3},{3,2},{4,5},{5,4},{6,7},{7,6},{8,9},{9,8},{10,11... | collective-permute-start | bytes 200 | tf_op jit(solution)/shard_map/ppermute | solution.py:447
  7.8 0.0 collective-permute-done.1.far_place
  7.8 1.5 %collective-permute-done.near_place = s32[2,8]{1,0:T(2,128)S(1)} collective-permute-done((s32[2,8]{1,0:T(2,128)S(1)}, s32[2,8]{1,0:T(2,128)S(1)}, u32[]{:S(2)}, u32[]{:S(2)}) %collective-permute-start) | collective-permute-done | bytes 96 | tf_op jit(solution)/shard_map/ppermute | solution.py:447
  9.3 0.0 copy-start
  9.3 1.6 %copy-done = f32[2,2,64,2048]{3,2,1,0:T(8,128)S(1)} copy-done((f32[2,2,64,2048]{3,2,1,0:T(8,128)S(1)}, f32[2,2,64,2048]{3,2,1,0:T(8,128)}, u32[]{:S(2)}) %copy-start) | copy-done | bytes 2097176
  10.9 0.0 copy-start.7
  10.9 0.7 copy-done.7
  11.6 0.0 copy-start.1
  11.6 0.0 copy-start.2
  11.6 0.0 copy-start.3
  11.6 0.0 copy-start.4
  11.6 0.0 copy-start.5
  11.6 0.0 copy-start.6
  11.6 1.7 %gather.1 = (f32[4,4,64,128]{3,2,1,0:T(8,128)S(1)}, f32[4,4,64,128]{3,2,1,0:T(8,128)S(1)}, f32[4,4,64,128]{3,2,1,0:T(8,128)S(1)}, f32[4,4,64,128]{3,2,1,0:T(8,12...) custom-call(s32[8]{0:T(128)S(1)} %copy-done.7, s32[2,8]{1,0:T(2,128)S(1)} %collective-permute-done.near_place, ...), custom_call_target="tpu_custom_call" | custom-call | tf_op jit(solution)/shard_map/gather/pallas_call | solution.py:452
  13.4 0.0 copy-done.9
  13.4 0.0 copy-done.8
  13.4 0.0 copy-done.10
  13.4 0.0 copy-done.1
  13.4 0.0 copy-done.2
  13.4 0.0 copy-done.3
  13.4 0.0 copy-done.4
  13.4 0.0 copy-done.5
  13.4 0.0 copy-done.6
  13.4 75.4 %waves.1 = (f32[4,4,64,128]{3,2,1,0:T(8,128)S(1)}, f32[4,4,64,128]{3,2,1,0:T(8,128)S(1)}, f32[4,4,64,128]{3,2,1,0:T(8,128)S(1)}, f32[4,4,64,128]{3,2,1,0:T(8,128...) custom-call(s32[8]{0:T(128)S(1)} %copy-done.9, s32[8]{0:T(128)S(1)} %copy-done.8, ...), custom_call_target="tpu_custom_call" | custom-call | tf_op jit(solution)/shard_map/waves/pallas_call | solution.py:469
  88.8 3.8 %scatter.1 = f32[4,64,2048]{2,1,0:T(8,128)} custom-call(s32[8]{0:T(128)S(1)} %copy-done.8, s32[2,8]{1,0:T(2,128)S(1)} %collective-permute-done.near_place, s32[2,8]{1,0:T(2,128)S(1)} %collective-permute-done.1.far_place, f32[4,4,64,128]{3,2,1,0:T(8,128)S(1)} %get-tuple-element.21.own_k, f32[4,4,64,128]{3,2,1,0:T(8,128)S(1)} %get-tuple-element.22.own_g, ...), custom_call_target="tpu_custom_call" | custom-call | tf_op jit(solution)/shard_map/scatter/pallas_call | solution.py:489
  92.7 0.6 copy.13
Async XLA Ops:
  0.6 12.7 %copy-start.9 = (s32[8]{0:T(128)S(1)}, s32[8]{0:T(128)}, u32[]{:S(2)}) copy-start(s32[8]{0:T(128)} %own_rows.1) | copy-start | bytes 100
  0.6 12.7 %copy-start.8 = (s32[8]{0:T(128)S(1)}, s32[8]{0:T(128)}, u32[]{:S(2)}) copy-start(s32[8]{0:T(128)} %own_cols.5) | copy-start | bytes 100
  0.7 12.7 %copy-start.10 = (s32[16]{0:T(128)S(1)}, s32[16]{0:T(128)}, u32[]{:S(2)}) copy-start(s32[16]{0:T(128)} %counts.1) | copy-start | bytes 196
  1.4 6.4 %collective-permute-start.1 = (s32[2,8]{1,0:T(2,128)S(1)}, s32[2,8]{1,0:T(2,128)S(1)}, u32[]{:S(2)}, u32[]{:S(2)}) collective-permute-start(s32[2,8]{1,0:T(2,128)S(1)} %pad_add_fusion), channel_id=1, source_target_pairs={{1,2},{2,1},{3,4},{4,3},{5,6},{6,5},{7,8},{8,7},{9,10},{10,9},{11,... | collective-permute-start | bytes 200 | tf_op jit(solution)/shard_map/ppermute | solution.py:448
  2.0 7.3 %collective-permute-start = (s32[2,8]{1,0:T(2,128)S(1)}, s32[2,8]{1,0:T(2,128)S(1)}, u32[]{:S(2)}, u32[]{:S(2)}) collective-permute-start(s32[2,8]{1,0:T(2,128)S(1)} %pad_add_fusion), channel_id=1, source_target_pairs={{0,1},{1,0},{2,3},{3,2},{4,5},{5,4},{6,7},{7,6},{8,9},{9,8},{10,11... | collective-permute-start | bytes 200 | tf_op jit(solution)/shard_map/ppermute | solution.py:447
  9.3 1.6 %copy-start = (f32[2,2,64,2048]{3,2,1,0:T(8,128)S(1)}, f32[2,2,64,2048]{3,2,1,0:T(8,128)}, u32[]{:S(2)}) copy-start(f32[2,2,64,2048]{3,2,1,0:T(8,128)} %param.10) | copy-start | bytes 6291460
  10.9 0.7 copy-start.7
  11.6 1.8 %copy-start.1 = (f32[8,128,128]{2,1,0:T(8,128)S(1)}, f32[8,128,128]{2,1,0:T(8,128)}, u32[]{:S(2)}) copy-start(f32[8,128,128]{2,1,0:T(8,128)} %diff_hbm.1) | copy-start | bytes 1572868
  11.6 1.8 %copy-start.2 = (bf16[512,256]{1,0:T(8,128)(2,1)S(1)}, bf16[512,256]{1,0:T(8,128)(2,1)}, u32[]{:S(2)}) copy-start(bf16[512,256]{1,0:T(8,128)(2,1)} %constant.11.clone.rest_3_) | copy-start | bytes 786436
  11.6 1.8 %copy-start.3 = (bf16[512,256]{1,0:T(8,128)(2,1)S(1)}, bf16[512,256]{1,0:T(8,128)(2,1)}, u32[]{:S(2)}) copy-start(bf16[512,256]{1,0:T(8,128)(2,1)} %constant.10.clone.rest_2_) | copy-start | bytes 786436
  11.6 1.8 %copy-start.4 = (bf16[512,256]{1,0:T(8,128)(2,1)S(1)}, bf16[512,256]{1,0:T(8,128)(2,1)}, u32[]{:S(2)}) copy-start(bf16[512,256]{1,0:T(8,128)(2,1)} %constant.9.clone.rest_1_) | copy-start | bytes 786436
  11.6 1.8 %copy-start.5 = (bf16[512,256]{1,0:T(8,128)(2,1)S(1)}, bf16[512,256]{1,0:T(8,128)(2,1)}, u32[]{:S(2)}) copy-start(bf16[512,256]{1,0:T(8,128)(2,1)} %constant.8.clone.rest_0_) | copy-start | bytes 786436
  11.6 1.8 %copy-start.6 = (f32[2,128,128]{2,1,0:T(8,128)S(1)}, f32[2,128,128]{2,1,0:T(8,128)}, u32[]{:S(2)}) copy-start(f32[2,128,128]{2,1,0:T(8,128)} %probe_hbm.1) | copy-start | bytes 393220
